TPU v7x, 256 devices: a whole 4x4x8 slice. The times are simulated.
256 devices in a mesh: seq: 64 (over z, y, core), ch: 4 (over x).
Axes of the slice: x: 4, y: 4, z: 8, core: 2. Of those that a mesh axis runs over, the one named last changes fastest.
Arguments:
- q_feat: bfloat16 [16384, 4096], P('seq', 'ch'), may hold values from -6 to 6
- k_feat: bfloat16 [16384, 4096], P('seq', 'ch'), may hold values from -6 to 6
- v_feat: bfloat16 [16384, 4096], P('seq', 'ch'), may hold values from -6 to 6
- short_taps: float32 [3, 3, 4096], P(None, None, 'ch'), may hold values from -3.5 to 3.5
- decay_rate: float32 [16, 4096], P(None, 'ch'), may hold values from 0 to 1, as said below
- residue: float32 [16, 4096], P(None, 'ch'), may hold values from -1 to 1
- skip_gain: float32 [4096], P('ch'), may hold values from -6 to 6
- out_weight: bfloat16 [4096, 4096], P('seq', 'ch'), may hold values from -0.09375 to 0.09375
- doc_starts: int32 [64, 4], P('seq'), may hold values from 0 to 256, as said below
- reset_flags: int32 [64, 4], P('seq'), may hold values from 0 to 1, as said below
Outputs:
- mixer_out: bfloat16 [16384, 4096], P('seq', 'ch')
Inputs may be any that keep to these rules, and one draw needn't show every extreme that they name: `doc_starts`: row s lists ascending the offsets within shard s at which documents begin, then unused slots holding 256; a shard holds at most 4 starts, some shard exactly 4, some shard none. `reset_flags`: only used slots hold 1; in each shard at most one slot holds 1, and some shard has one. `decay_rate`: positive rates.
All inputs are finite; a program needn't handle non-finite values.
Results may differ from a plain program's by a relative error of at most 0.018.
Values may be sent and summed in bfloat16 or wider, within the bound.
No kernel may reach another device: no remote copies, remote signals or barrier semaphores. Data moves between devices by JAX's collectives and lax.ppermute only.
A program may use at most 128 MiB of HBM per device.

v0:
```python
import math

import jax
import jax.numpy as jnp
from jax import lax
from jax.sharding import PartitionSpec as P

BLOCK = 128


def from_behind(block, axis, distance):
    devices = range(lax.axis_size(axis))
    route = [(i - distance, i) for i in devices if i - distance in devices]
    return lax.ppermute(block, axis, route)


def entering_2(value, axis, join, neutral):
    count, mine = (lax.axis_size(axis), lax.axis_index(axis))
    pieces = jax.tree.map(lambda part: lax.all_gather(part, axis), value)
    running = jax.tree.map(
        lambda part, zero: jnp.full_like(part, 0) + jnp.asarray(zero, part.dtype), value, neutral
    )

    def hop(position, running):
        longer = join(running, jax.tree.map(lambda part: part[position], pieces))
        return jax.tree.map(lambda new, old: jnp.where(position < mine, new, old), longer, running)

    return lax.fori_loop(0, count - 1, hop, running)


def short_filter(features, rim_rows, tap_weights, keep_mask):
    token_rows = features.shape[0]
    tap_count = tap_weights.shape[0]
    joined = jnp.concatenate([rim_rows, features], axis=0)
    summed = tap_weights[0] * features.astype(jnp.float32)
    valid_mask = jnp.ones((token_rows,), jnp.float32)
    for offset in range(1, tap_count):
        valid_mask = valid_mask * jnp.concatenate(
            [jnp.ones((offset - 1,), jnp.float32), keep_mask[: token_rows - offset + 1]]
        )
        lagged = joined[tap_count - 1 - offset : tap_count - 1 - offset + token_rows].astype(
            jnp.float32
        )
        summed = summed + tap_weights[offset] * valid_mask[:, None] * lagged
    return summed.astype(jnp.bfloat16)


def transform_tables(length):
    period = 2 * length
    time_axis = jnp.arange(length, dtype=jnp.int32)
    cos_freq = jnp.arange(length + 1, dtype=jnp.int32)
    sin_freq = jnp.arange(1, length, dtype=jnp.int32)
    cos_angle = (
        2.0
        * math.pi
        / period
        * (cos_freq[:, None] * time_axis[None, :] % period).astype(jnp.float32)
    )
    sin_angle = (
        2.0
        * math.pi
        / period
        * (sin_freq[:, None] * time_axis[None, :] % period).astype(jnp.float32)
    )
    forward = jnp.concatenate([jnp.cos(cos_angle), jnp.sin(sin_angle)], axis=0)
    edge_weight = (
        jnp.where((cos_freq == 0) | (cos_freq == length), 1.0, 2.0).astype(jnp.float32) / period
    )
    inverse = jnp.concatenate(
        [(jnp.cos(cos_angle) * edge_weight[:, None]).T, (jnp.sin(sin_angle) * (2.0 / period)).T],
        axis=1,
    )
    return (forward, inverse)


def chain_combine(earlier, later):
    return (earlier[0] * later[0], later[0] * earlier[1] + later[1])


def local(
    q_feat,
    k_feat,
    v_feat,
    short_taps,
    decay_rate,
    residue,
    skip_gain,
    out_weight,
    doc_starts,
    reset_flags,
):
    highest = lax.Precision.HIGHEST
    token_rows, channels = q_feat.shape
    tap_count = short_taps.shape[1]
    block_count = token_rows // BLOCK
    position = jnp.arange(token_rows, dtype=jnp.int32)
    matches = position[:, None] == doc_starts[0][None, :]
    starts_here = jnp.any(matches, axis=1).astype(jnp.float32)
    resets = jnp.any(matches & (reset_flags[0][None, :] == 1), axis=1).astype(jnp.float32)
    keep_mask = 1.0 - starts_here
    rim_keep = []
    for offset in range(tap_count - 1):
        rim_index = token_rows - (tap_count - 1) + offset
        rim_keep.append(jnp.prod(keep_mask[rim_index + 1 :]))
    rim_scale = jnp.stack(rim_keep).astype(jnp.bfloat16)
    three_feats = (q_feat, k_feat, v_feat)
    tails = (
        jnp.stack([feature_rows[token_rows - (tap_count - 1) :] for feature_rows in three_feats])
        * rim_scale[None, :, None]
    )
    arrived = from_behind(tails, "seq", 1)
    q_short = short_filter(q_feat, arrived[0], short_taps[0], keep_mask)
    k_short = short_filter(k_feat, arrived[1], short_taps[1], keep_mask)
    v_short = short_filter(v_feat, arrived[2], short_taps[2], keep_mask)
    gated = k_short.astype(jnp.float32) * v_short.astype(jnp.float32)
    forward, inverse = transform_tables(BLOCK)
    steps_axis = jnp.arange(BLOCK + 1, dtype=jnp.float32)
    powers = jnp.exp(-steps_axis[None, :, None] * decay_rate[:, None, :])
    filter_taps = jnp.einsum("njc,nc->jc", powers[:, :BLOCK], residue, precision=highest)
    spectrum = jnp.dot(forward, filter_taps, precision=highest)
    cos_part = spectrum[: BLOCK + 1]
    sin_part = spectrum[BLOCK + 1 :]
    reset_blocks = resets.reshape(block_count, BLOCK)
    block_pos = jnp.arange(BLOCK, dtype=jnp.float32)
    has_reset = jnp.sum(reset_blocks, axis=1)
    cut_index = jnp.sum(reset_blocks * block_pos[None, :], axis=1)
    after_cut = (block_pos[None, :] >= cut_index[:, None]).astype(jnp.float32)
    blocks = gated.reshape(block_count, BLOCK, channels)
    late_part = blocks * after_cut[:, :, None]
    freq_data = jnp.einsum("fs,bsc->bfc", forward, blocks, precision=highest)
    data_cos = freq_data[:, : BLOCK + 1]
    data_sin = freq_data[:, BLOCK + 1 :]
    cross_term = data_sin * sin_part[None]
    edge_rows = jnp.zeros((block_count, 1, channels), jnp.float32)
    real_part = data_cos * cos_part[None] - jnp.concatenate(
        [edge_rows, cross_term, edge_rows], axis=1
    )
    imag_part = data_cos[:, 1:BLOCK] * sin_part[None] + data_sin * cos_part[None, 1:BLOCK]
    outputs = jnp.einsum(
        "tf,bfc->btc", inverse, jnp.concatenate([real_part, imag_part], axis=1), precision=highest
    )
    block_ids = jnp.arange(block_count, dtype=jnp.float32)
    reset_block = jnp.sum(has_reset * block_ids).astype(jnp.int32)
    cut_here = lax.dynamic_index_in_dim(cut_index, reset_block, 0, keepdims=False)
    flag_here = lax.dynamic_index_in_dim(has_reset, reset_block, 0, keepdims=False)
    early_rows = lax.dynamic_index_in_dim(blocks, reset_block, 0, keepdims=False)
    early_mask = (block_pos < cut_here).astype(jnp.float32)
    early_lag = jnp.maximum(cut_here - 1.0 - block_pos, 0.0)
    early_weight = jnp.exp(-early_lag[:, None, None] * decay_rate[None]) * early_mask[:, None, None]
    early_state = jnp.einsum("snc,sc->nc", early_weight, early_rows, precision=highest)
    late_gap = jnp.maximum(block_pos - cut_here + 1.0, 0.0)
    late_weight = jnp.exp(-late_gap[:, None, None] * decay_rate[None]) * residue[None]
    leaked = (
        jnp.einsum("tnc,nc->tc", late_weight, early_state, precision=highest)
        * ((1.0 - early_mask) * flag_here)[:, None]
    )
    current = lax.dynamic_index_in_dim(outputs, reset_block, 0, keepdims=True)
    within = lax.dynamic_update_slice_in_dim(outputs, current - leaked[None], reset_block, 0)
    reversed_powers = powers[:, BLOCK - 1 :: -1]
    block_states = jnp.einsum("nsc,bsc->bnc", reversed_powers, late_part, precision=highest)
    block_pass = powers[None, :, BLOCK] * (1.0 - has_reset)[:, None, None]

    def advance(carried_state, block_item):
        pass_factor, fresh_state = block_item
        product_pass, summed_state = carried_state
        return (
            (product_pass * pass_factor, pass_factor * summed_state + fresh_state),
            (product_pass, summed_state),
        )

    starting = (jnp.ones_like(decay_rate), jnp.zeros_like(decay_rate))
    (shard_pass, shard_state), (lead_pass, lead_state) = lax.scan(
        advance, starting, (block_pass, block_states)
    )
    _, entering = entering_2(
        (shard_pass, shard_state),
        "seq",
        chain_combine,
        (jnp.ones_like(shard_pass), jnp.zeros_like(shard_state)),
    )
    entering_states = lead_pass * entering[None] + lead_state
    alive_mask = 1.0 - has_reset[:, None] * after_cut
    weighted = residue[:, None, :] * powers[:, 1:]
    carried = (
        jnp.einsum("nic,bnc->bic", weighted, entering_states, precision=highest)
        * alive_mask[:, :, None]
    )
    filtered = (within + carried).reshape(token_rows, channels)
    mixed = (q_short.astype(jnp.float32) * (filtered + skip_gain[None, :] * gated)).astype(
        jnp.bfloat16
    )
    projected = lax.dot_general(
        mixed,
        lax.all_gather(out_weight, "seq", axis=0, tiled=True),
        (((1,), (1,)), ((), ())),
        preferred_element_type=jnp.float32,
    )
    result = lax.psum_scatter(projected.astype(jnp.bfloat16), "ch", scatter_dimension=1, tiled=True)
    return result


def solution(mesh):
    placed = (
        P("seq", "ch"),
        P("seq", "ch"),
        P("seq", "ch"),
        P(None, None, "ch"),
        P(None, "ch"),
        P(None, "ch"),
        P("ch"),
        P("seq", "ch"),
        P("seq", None),
        P("seq", None),
    )
    return jax.shard_map(
        local, mesh=mesh, in_specs=placed, out_specs=P("seq", "ch"), check_vma=False
    )
```

profile of v0, /device:TPU:1, one launch (start us, length us, event | category | flops | bytes accessed | tf_op | source)
XLA Modules:
  0.0 351.4 jit_solution(9788704270896219125)
XLA Ops:
  10.9 4.6 %collective-permute-start = (bf16[3,2,1024]{2,1,0:T(2,128)(2,1)S(1)}, bf16[3,2,1024]{2,1,0:T(2,128)(2,1)S(1)}, u32[]{:S(2)}, u32[]{:S(2)}) collective-permute-start(bf16[3,2,1024]{2,1,0:T(2,128)(2,1)S(1)} %maximum_multiply_fusion), channel_id=1, source_target_pairs={{0,4},{4,8},{8,12},{12,16},{16,20},{20,24},{24,28},{28,32},{32,36}... | collective-permute-start | bytes 36872 | tf_op jit(solution)/shard_map/ppermute | solution.py:14
  17.2 2.0 multiply_exponential_fusion
  19.3 7.2 %slice_multiply_fusion = (f32[16,128,1024]{2,0,1:T(8,128)}, f32[16,128,1024]{2,0,1:T(8,128)}) fusion(f32[16,129,1024]{2,0,1:T(8,128)S(1)} %multiply_exponential_fusion, f32[16,1024]{1,0:T(8,128)S(1)} %copy-done.5), kind=kLoop, calls=%fused_computation.9 | loop fusion | flops 2097152 | bytes 33619968 | tf_op jit(solution)/shard_map/mul | solution.py:183
  26.5 1.0 copy-done
  27.6 8.3 %rev.3 = f32[16,128,1024]{2,0,1:T(8,128)} reverse(f32[16,128,1024]{2,0,1:T(8,128)} %get-tuple-element.240), dimensions={1} | reverse | bytes 16777216 | tf_op jit(solution)/shard_map/rev | solution.py:159
  35.9 9.3 %copy.25 = f32[16,128,1024]{1,0,2:T(8,128)} copy(f32[16,128,1024]{2,0,1:T(8,128)} %rev.3) | data formatting | bytes 16777216 | tf_op jit(solution)/shard_map/rev | solution.py:159
  45.3 0.9 convert_multiply_fusion
  46.8 15.2 %convolution_bitcast_fusion.1 = f32[2,16,1024]{1,0,2:T(2,128)S(1)} fusion(f32[16,128,1024]{1,0,2:T(8,128)} %copy.25, f32[2,128,1024]{1,0,2:T(2,128)S(1)} %copy.24, f32[2,128]{1,0:T(2,128)S(1)} %fusion.55), kind=kOutput, calls=%fused_computation.19 | convolution fusion | flops 50593792 | bytes 9569280 | tf_op jit(solution)/shard_map/nsc,bsc->bnc/dot_general | solution.py:160
  62.5 1.4 while.31
  66.9 5.4 %multiply_reduce_fusion.2 = f32[1024,128]{0,1:T(8,128)S(1)} fusion(f32[1024,16]{0,1:T(8,128)S(1)} %bitcast.120, f32[16,129,1024]{2,0,1:T(8,128)} %copy-done), kind=kLoop, calls=%fused_computation.12 | loop fusion | flops 4063232 | bytes 8978432 | tf_op jit(solution)/shard_map/njc,nc->jc/dot_general | solution.py:119
  72.3 1.0 fusion.26
  77.5 1.3 subtract_multiply_fusion
  78.9 9.3 %copy.28 = f32[16,128,1024]{1,0,2:T(8,128)} copy(f32[16,128,1024]{2,0,1:T(8,128)} %get-tuple-element.239) | data formatting | bytes 16777216 | tf_op jit(solution)/shard_map/mul | solution.py:183
  88.1 1.8 convolution_bitcast_fusion
  90.8 2.1 multiply_reduce_fusion.1
  92.9 1.4 fusion.1
  94.3 1.0 copy.58
  95.3 2.7 multiply_reduce_fusion
  98.0 0.9 fusion.13
  98.9 47.4 %all-gather.8.cloned.1.call-done = f32[1024,1024]{1,0:T(8,128)} async-done(((f32[16,1024]{1,0:T(8,128)}), f32[1024,1024]{1,0:T(8,128)}) %all-gather.8.cloned.1.call-update) | async-done | bytes 4194320 | tf_op jit(solution)/shard_map/all_gather | solution.py:19
  146.4 79.1 %all-gather.10.cloned.1.call-done = f32[1024,1024]{1,0:T(8,128)} async-done(((f32[16,1024]{1,0:T(8,128)}), f32[1024,1024]{1,0:T(8,128)}) %all-gather.10.cloned.1.call-update) | async-done | bytes 4194320 | tf_op jit(solution)/shard_map/all_gather | solution.py:19
  225.5 59.1 %while.32 = (s32[]{:T(128)}, f32[16,1024]{1,0:T(8,128)S(1)}, s32[]{:T(128)}, f32[64,16,1024]{2,1,0:T(8,128)}, f32[64,16,1024]{2,1,0:T(8,128)}, /*index=5*/s32[]{:T(128)}, s32[]{:T(128)}) while((s32[]{:T(128)}, f32[16,1024]{1,0:T(8,128)S(1)}, s32[]{:T(128)}, f32[64,16,1024]{2,1,0:T(8,128)}, f32[64,16,1024]{2,1,0:T(8,128)}, ...), condition=%wide.region_8.9_spmd.clone, body=%wide.region_7.8_spmd.clone.sunk | while | flops 65540 | bytes 262253 | solution.py:28
  255.5 0.9 fusion.71
  279.8 1.0 fusion.71
  281.7 0.9 fusion.71
  282.7 1.0 fusion.71
  285.2 9.4 %fusion.62 = f32[1024,2,128]{2,1,0:T(2,128)S(1)} fusion(f32[2,16,1024]{1,0,2:T(2,128)S(1)} %copy.27, f32[16,128,1024]{1,0,2:T(8,128)} %copy.28), kind=kOutput, calls=%fused_computation.139 | convolution fusion | flops 50331648 | bytes 9568256 | tf_op jit(solution)/shard_map/nic,bnc->bic/dot_general | solution.py:185
  295.3 1.4 bitcast_add_fusion.3
  296.7 2.5 fusion.8
  299.2 9.4 %all-gather.6.cloned.1.call-done = bf16[4096,1024]{1,0:T(8,128)(2,1)} async-done(((bf16[64,1024]{1,0:T(8,128)(2,1)}), bf16[4096,1024]{1,0:T(8,128)(2,1)}) %all-gather.6.cloned.1.call-update) | async-done | bytes 8388624 | tf_op jit(solution)/shard_map/all_gather | solution.py:194
  308.6 7.1 %convolution_convert_fusion = bf16[256,4096]{1,0:T(8,128)(2,1)} fusion(bf16[256,1024]{1,0:T(8,128)(2,1)S(1)} %fusion.8, bf16[4096,1024]{1,0:T(8,128)(2,1)} %all-gather.6.cloned.1.call-done), kind=kOutput, calls=%fused_computation.13 | convolution fusion | flops 2148532224 | bytes 11010048 | tf_op jit(solution)/shard_map/dot_general | solution.py:192
  315.7 29.1 %reduce-scatter.2.cloned.1.call-done = bf16[256,1024]{1,0:T(8,128)(2,1)} async-done(((bf16[256,4096]{1,0:T(8,128)(2,1)}), bf16[256,1024]{1,0:T(8,128)(2,1)}) %reduce-scatter.2.cloned.1.call-update) | async-done | bytes 524304 | tf_op jit(solution)/shard_map/reduce_scatter | solution.py:198
  (135 shorter events, 70.6 us)
Async XLA Ops:
  6.5 12.7 %copy-start.5 = (f32[16,1024]{1,0:T(8,128)S(1)}, f32[16,1024]{1,0:T(8,128)}, u32[]{:S(2)}) copy-start(f32[16,1024]{1,0:T(8,128)} %param.19) | copy-start | bytes 196612
  6.5 139.8 %all-gather.8.cloned.1.call-start = ((), (), s32[]{:S(2)}) async-start(), calls=%async_computation.3 | async-start | bytes 4259840 | tf_op jit(solution)/shard_map/all_gather | solution.py:19
  10.9 34.3 %collective-permute-start = (bf16[3,2,1024]{2,1,0:T(2,128)(2,1)S(1)}, bf16[3,2,1024]{2,1,0:T(2,128)(2,1)S(1)}, u32[]{:S(2)}, u32[]{:S(2)}) collective-permute-start(bf16[3,2,1024]{2,1,0:T(2,128)(2,1)S(1)} %maximum_multiply_fusion), channel_id=1, source_target_pairs={{0,4},{4,8},{8,12},{12,16},{16,20},{20,24},{24,28},{28,32},{32,36}... | collective-permute-start | bytes 36872 | tf_op jit(solution)/shard_map/ppermute | solution.py:14
  19.3 8.2 %copy-start = (f32[16,129,1024]{2,0,1:T(8,128)}, f32[16,129,1024]{2,0,1:T(8,128)S(1)}, u32[]{:S(2)}) copy-start(f32[16,129,1024]{2,0,1:T(8,128)S(1)} %multiply_exponential_fusion) | copy-start | bytes 25362436
  35.9 9.4 %copy-start.3 = (bf16[256,1024]{1,0:T(8,128)(2,1)S(1)}, bf16[256,1024]{1,0:T(8,128)(2,1)}, u32[]{:S(2)}) copy-start(bf16[256,1024]{1,0:T(8,128)(2,1)} %param.15) | copy-start | bytes 1572868
  35.9 9.4 %copy-start.4 = (bf16[256,1024]{1,0:T(8,128)(2,1)S(1)}, bf16[256,1024]{1,0:T(8,128)(2,1)}, u32[]{:S(2)}) copy-start(bf16[256,1024]{1,0:T(8,128)(2,1)} %param.16) | copy-start | bytes 1572868
  64.0 0.6 copy-start.1
  64.0 0.7 copy-start.2
  64.6 160.9 %all-gather.10.cloned.1.call-start = ((), (), s32[]{:S(2)}) async-start(), calls=%async_computation.4 | async-start | bytes 4259840 | tf_op jit(solution)/shard_map/all_gather | solution.py:19
  65.4 243.2 %all-gather.6.cloned.1.call-start = ((), (), s32[]{:S(2)}) async-start(), calls=%async_computation.1 | async-start | bytes 8519680 | tf_op jit(solution)/shard_map/all_gather | solution.py:194
  66.1 278.7 %reduce-scatter.2.cloned.1.call-start = ((), (), s32[]{:S(2)}) async-start(), calls=%async_computation.2 | async-start | bytes 2621440 | tf_op jit(solution)/shard_map/reduce_scatter | solution.py:198
  88.1 2.7 copy-start.8
  90.8 193.8 %copy-start.6 = (f32[2,16,1024]{2,1,0:T(8,128)S(1)}, f32[2,16,1024]{2,1,0:T(8,128)}, u32[]{:S(2)}) copy-start(f32[2,16,1024]{2,1,0:T(8,128)} %get-tuple-element.139) | copy-start | bytes 393220
  90.8 193.8 %copy-start.7 = (f32[2,16,1024]{2,1,0:T(8,128)S(1)}, f32[2,16,1024]{2,1,0:T(8,128)}, u32[]{:S(2)}) copy-start(f32[2,16,1024]{2,1,0:T(8,128)} %get-tuple-element.143) | copy-start | bytes 393220
  284.6 12.1 %copy-start.9 = (f32[1024]{0:T(1024)S(1)}, f32[1024]{0:T(1024)}, u32[]{:S(2)}) copy-start(f32[1024]{0:T(1024)} %param.20) | copy-start | bytes 12292
Sparse Core Ops, SparseCore 0:
  64.7 81.5 all-gather.7
  149.1 76.2 all-gather.9
  228.2 80.2 all-gather.5
  315.8 28.9 reduce-scatter.1
where the time goes:
time: 355 us; the launch traced here: 351 us
  waiting for transfers between devices  166 us (47%)
  other arithmetic  91.6 us (26%)
  local copies, waits for them, and re-layouts  36.3 us (10%)
  matrix products  35.8 us (10%)
  between operations  14.8 us (4%)
  starting transfers between devices  4.89 us (1%)
    all_gather x2, waiting for transfers between devices, entering_2(): pieces = jax.tree.map(lambda part: lax.all_gather(part, axis), value)  127 us
    select_n x63, other arithmetic, hop(): jnp.where(position < mine, new, old)  57.8 us
    reduce_scatter x1, waiting for transfers between devices, local(): lax.psum_scatter(projected.astype(jnp.bfloat16), 'ch', scatter_dimension=...  29.1 us
    rev x2, local copies, waits for them, and re-layouts, local(): reversed_powers = powers[:, BLOCK - 1::-1]  17.6 us
    dot_general x1, matrix products, local(): jnp.einsum('nsc,bsc->bnc', reversed_powers, late_part, precision=highest)  15.2 us
    all_gather x1, waiting for transfers between devices, local(): lax.all_gather(out_weight, 'seq', axis=0, tiled=True)  9.42 us
    dot_general x1, matrix products, local(): jnp.einsum('nic,bnc->bic', weighted, entering_states, precision=highest)  9.36 us
    mul x1, local copies, waits for them, and re-layouts, local(): weighted = residue[:, None, :] * powers[:, 1:]  9.28 us
  transfers between devices with their start and end apart: 5, of which 4 were waited for; matrix products, arithmetic and copies ran while one was open for 38% of the time, Pallas kernels for 0%

commit v1 on v0

v1 whole, which is shorter than its diff:
```python
import jax
import jax.numpy as jnp
from jax import lax
from jax.experimental import pallas as pl
from jax.experimental.pallas import tpu as pltpu
from jax.sharding import PartitionSpec as P

MODES = 16
ROWS = 256
LANES = 128
GROUPS = 8
STEPS = 8
CHUNKS = ROWS // STEPS
PIECE = 64


def cyclic(block, shift):
    count = lax.axis_size("seq")
    return lax.ppermute(block, "seq", [(i, shift(i)) for i in range(count)])


def reset_place(starts_ref, flags_ref):
    place = jnp.int32(0)
    found = jnp.int32(0)
    for slot in range(4):
        hit = (flags_ref[0, slot] == 1) & (starts_ref[0, slot] < ROWS)
        place = jnp.where(hit, starts_ref[0, slot], place)
        found = jnp.where(hit, jnp.int32(1), found)
    return place, found


def row_slice(t):
    return pl.ds(pl.multiple_of(t * GROUPS, GROUPS), GROUPS)


def front_kernel(starts_ref, flags_ref, q_ref, k_ref, v_ref, halo_ref, taps_ref, rate_ref,
                 q_out, gated_out, state_out, wide):
    for feature, source in enumerate((k_ref, v_ref, q_ref)):
        which = (1, 2, 0)[feature]
        wide[feature, 8:, :] = source[...].astype(jnp.float32)
        wide[feature, 6:8, :] = halo_ref[2 * which : 2 * which + 2, :].astype(jnp.float32)
    for first in range(0, ROWS, PIECE):
        t = lax.broadcasted_iota(jnp.int32, (PIECE, LANES), 0) + first
        keep_one = jnp.ones((PIECE, LANES), jnp.float32)
        keep_two = keep_one
        for slot in range(4):
            at = starts_ref[0, slot]
            keep_one = jnp.where(t == at, 0.0, keep_one)
            keep_two = jnp.where((t == at) | (t == at + 1), 0.0, keep_two)
        for group in range(GROUPS):
            lanes = slice(group * LANES, (group + 1) * LANES)

            def short(feature, which):
                total = taps_ref[3 * which : 3 * which + 1, lanes] * wide[
                    feature, 8 + first : 8 + first + PIECE, lanes]
                total = total + (taps_ref[3 * which + 1 : 3 * which + 2, lanes] * keep_one) * wide[
                    feature, 7 + first : 7 + first + PIECE, lanes]
                total = total + (taps_ref[3 * which + 2 : 3 * which + 3, lanes] * keep_two) * wide[
                    feature, 6 + first : 6 + first + PIECE, lanes]
                return total.astype(jnp.bfloat16).astype(jnp.float32)

            rows = pl.ds(first * GROUPS + group, PIECE, stride=GROUPS)
            gated_out[rows, :] = short(0, 1) * short(1, 2)
            q_out[rows, :] = short(2, 0)
    place, found = reset_place(starts_ref, flags_ref)
    decay = [jnp.exp(-rate_ref[n * GROUPS : (n + 1) * GROUPS, :]) for n in range(MODES)]

    def chunk(index, state):
        for step in range(STEPS):
            t = index * STEPS + step
            row = jnp.where(t >= place, gated_out[row_slice(t), :], 0.0)
            state = tuple(decay[n] * state[n] + row for n in range(MODES))
        return state

    zero = jnp.zeros((GROUPS, LANES), jnp.float32)
    state = lax.fori_loop(place // STEPS, CHUNKS, chunk, (zero,) * MODES)
    for n in range(MODES):
        state_out[n * GROUPS : (n + 1) * GROUPS, :] = state[n]
    state_out[MODES * GROUPS :, :] = jnp.full((GROUPS, LANES), 1 - found, jnp.int32).astype(jnp.float32)


def inner_kernel(starts_ref, flags_ref, gated_ref, rate_ref, residue_ref, skip_ref, out_ref):
    place, found = reset_place(starts_ref, flags_ref)
    decay = [jnp.exp(-rate_ref[n * GROUPS : (n + 1) * GROUPS, :]) for n in range(MODES)]
    weight = [residue_ref[n * GROUPS : (n + 1) * GROUPS, :] for n in range(MODES)]
    skip = skip_ref[...]
    cut_chunk = jnp.where(found == 1, place // STEPS, CHUNKS)

    def run(index, state, cutting):
        for step in range(STEPS):
            t = index * STEPS + step
            row = gated_ref[row_slice(t), :]
            if cutting:
                state = tuple(jnp.where(t == place, 0.0, state[n]) for n in range(MODES))
            state = tuple(decay[n] * state[n] + row for n in range(MODES))
            terms = [weight[n] * state[n] for n in range(MODES)] + [skip * row]
            while len(terms) > 1:
                paired = [terms[i] + terms[i + 1] for i in range(0, len(terms) - 1, 2)]
                terms = paired + terms[len(terms) - len(terms) % 2 :]
            out_ref[row_slice(t), :] = terms[0]
        return state

    zero = jnp.zeros((GROUPS, LANES), jnp.float32)
    state = (zero,) * MODES
    state = lax.fori_loop(0, cut_chunk, lambda i, s: run(i, s, False), state)
    state = lax.fori_loop(
        cut_chunk, jnp.minimum(cut_chunk + 1, CHUNKS), lambda i, s: run(i, s, True), state)
    lax.fori_loop(cut_chunk + 1, CHUNKS, lambda i, s: run(i, s, False), state)


def mix_kernel(starts_ref, flags_ref, entering_ref, rate_ref, residue_ref, q_ref, inner_ref,
               mixed_out, rows_ref):
    place, found = reset_place(starts_ref, flags_ref)
    limit = jnp.where(found == 1, place, ROWS)
    decay = [jnp.exp(-rate_ref[n * GROUPS : (n + 1) * GROUPS, :]) for n in range(MODES)]
    carried = tuple(
        residue_ref[n * GROUPS : (n + 1) * GROUPS, :] * entering_ref[n * GROUPS : (n + 1) * GROUPS, :]
        for n in range(MODES))
    live_chunks = (limit + STEPS - 1) // STEPS

    def live(index, carried):
        for step in range(STEPS):
            t = index * STEPS + step
            carried = tuple(decay[n] * carried[n] for n in range(MODES))
            terms = list(carried)
            while len(terms) > 1:
                terms = [terms[i] + terms[i + 1] for i in range(0, len(terms), 2)]
            from_before = jnp.where(t < limit, terms[0], 0.0)
            rows_ref[row_slice(t), :] = q_ref[row_slice(t), :] * (inner_ref[row_slice(t), :] + from_before)
        return carried

    def rest(index, _):
        for step in range(STEPS):
            t = index * STEPS + step
            rows_ref[row_slice(t), :] = q_ref[row_slice(t), :] * inner_ref[row_slice(t), :]
        return 0

    lax.fori_loop(0, live_chunks, live, carried)
    lax.fori_loop(live_chunks, CHUNKS, rest, 0)
    for group in range(GROUPS):
        mixed_out[:, group * LANES : (group + 1) * LANES] = rows_ref[
            pl.ds(group, ROWS, stride=GROUPS), :].astype(jnp.bfloat16)


SMALL = pl.BlockSpec(memory_space=pltpu.SMEM)
WHOLE = pl.BlockSpec(memory_space=pltpu.VMEM)
LIMIT = 32 * 1024 * 1024


def call(kernel, outs, count, scratch=(), flops=0, moved=0):
    return pl.pallas_call(
        kernel,
        out_shape=outs,
        in_specs=[SMALL] * 2 + [WHOLE] * count,
        out_specs=jax.tree.map(lambda _: WHOLE, outs),
        scratch_shapes=scratch,
        compiler_params=pltpu.CompilerParams(vmem_limit_bytes=LIMIT),
        cost_estimate=pl.CostEstimate(flops=flops, bytes_accessed=moved, transcendentals=0),
    )


def f32(*shape):
    return jax.ShapeDtypeStruct(shape, jnp.float32)


STATE = MODES * GROUPS


def digit_round(message, pass_factor, digit, stride, last):
    def back(k):
        def target(i):
            d = (i // stride) % 4
            return i - d * stride + ((d + k) % 4) * stride
        return target

    count = lax.axis_size("seq")
    if last:
        got = {
            k: lax.ppermute(message, "seq", [(i, i + k * stride) for i in range(count - k * stride)])
            for k in (3, 2, 1)
        }
    else:
        got = {k: cyclic(message, back(k)) for k in (3, 2, 1)}
    mine = (lax.axis_index("seq") // stride) % 4

    def join(total, later):
        return later[:STATE] + pass_factor * later[STATE, 0] * total

    entering = jnp.zeros((STATE, LANES), jnp.float32)
    alive = jnp.float32(1)
    for k in (3, 2, 1):
        entering = jnp.where(k <= mine, join(entering, got[k]), 0.0)
        alive = alive * jnp.where(k <= mine, got[k][STATE, 0], 1.0)
    if last:
        return entering, alive, None
    total = join(entering, message)
    whole_alive = message[STATE, 0]
    for k in (3, 2, 1):
        total = jnp.where(k > mine, join(total, got[k]), total)
        whole_alive = whole_alive * got[k][STATE, 0]
    following = jnp.concatenate(
        [total, jnp.full((GROUPS, LANES), 1.0, jnp.float32) * whole_alive], axis=0)
    return entering, alive, following


def local(q_feat, k_feat, v_feat, short_taps, decay_rate, residue, skip_gain, out_weight,
          doc_starts, reset_flags):
    weight = lax.all_gather(out_weight, "seq", axis=0, tiled=True)
    ends = jnp.any(doc_starts[0] == ROWS - 1)
    scale = jnp.stack([jnp.where(ends, 0.0, 1.0), jnp.float32(1)]).astype(jnp.bfloat16)
    tails = jnp.concatenate(
        [part[ROWS - 2 :] * scale[:, None] for part in (q_feat, k_feat, v_feat)], axis=0)
    count = lax.axis_size("seq")
    halo = lax.ppermute(tails, "seq", [(i, i + 1) for i in range(count - 1)])
    rate = decay_rate.reshape(STATE, LANES)
    gain = residue.reshape(STATE, LANES)
    skip = skip_gain.reshape(GROUPS, LANES)
    taps = short_taps.reshape(9, GROUPS * LANES)
    q_rows, gated, message = call(
        front_kernel,
        (f32(ROWS * GROUPS, LANES), f32(ROWS * GROUPS, LANES), f32(STATE + GROUPS, LANES)),
        6,
        scratch=[pltpu.VMEM((3, ROWS + 8, GROUPS * LANES), jnp.float32)],
        flops=20_000_000,
        moved=4_000_000,
    )(doc_starts, reset_flags, q_feat, k_feat, v_feat, halo, taps, rate)
    inner = call(inner_kernel, f32(ROWS * GROUPS, LANES), 4, flops=20_000_000, moved=4_000_000)(
        doc_starts, reset_flags, gated, rate, gain, skip)
    seq = lax.axis_index("seq")
    enter_low, alive_low, next_message = digit_round(message, jnp.exp(-256.0 * rate), 0, 1, False)
    enter_mid, alive_mid, next_message = digit_round(
        next_message, jnp.exp(-1024.0 * rate), 1, 4, False)
    enter_high, _, _ = digit_round(next_message, jnp.exp(-4096.0 * rate), 2, 16, True)
    low = (seq % 4).astype(jnp.float32)
    mid = ((seq // 4) % 4).astype(jnp.float32)
    entering = enter_mid + jnp.exp(-1024.0 * mid * rate) * alive_mid * enter_high
    entering = enter_low + jnp.exp(-256.0 * low * rate) * alive_low * entering
    mixed = call(
        mix_kernel,
        jax.ShapeDtypeStruct((ROWS, GROUPS * LANES), jnp.bfloat16),
        5,
        scratch=[pltpu.VMEM((ROWS * GROUPS, LANES), jnp.float32)],
        flops=20_000_000,
        moved=4_000_000,
    )(doc_starts, reset_flags, entering, rate, gain, q_rows, inner)
    projected = lax.dot_general(
        mixed, weight, (((1,), (1,)), ((), ())), preferred_element_type=jnp.float32)
    return lax.psum_scatter(projected.astype(jnp.bfloat16), "ch", scatter_dimension=1, tiled=True)


def solution(mesh):
    placed = (
        P("seq", "ch"),
        P("seq", "ch"),
        P("seq", "ch"),
        P(None, None, "ch"),
        P(None, "ch"),
        P(None, "ch"),
        P("ch"),
        P("seq", "ch"),
        P("seq", None),
        P("seq", None),
    )
    return jax.shard_map(
        local, mesh=mesh, in_specs=placed, out_specs=P("seq", "ch"), check_vma=False
    )
```

time: 355 us -> 142 us (0.40)
  waiting for transfers between devices: 166 us -> 43.3 us
  other arithmetic: 91.6 us -> 13.6 us
  matrix products: 35.8 us -> 7.15 us
  starting transfers between devices: 4.89 us -> 26.9 us
  local copies, waits for them, and re-layouts: 36.3 us -> 18.4 us
  Pallas kernels: 0 us -> 8.85 us
  between operations: 14.8 us -> 22.4 us
    all_gather x3 -> x1, waiting for transfers between devices: 136 us -> 10 us  [local(): weight = lax.all_gather(out_weight, 'seq', axis=0, tiled=True)]
    select_n x63 -> x2, other arithmetic: 57.8 us -> 4.55 us  [digit_round(): total = jnp.where(k > mine, join(total, got[k]), total)]
    dot_general x6 -> x1, matrix products: 35.8 us -> 7.15 us  [local(): lax.dot_general(mixed, weight, (((1,), (1,)), ((), ())), preferred_elemen...]
    ppermute x1 -> x10, starting transfers between devices: 4.59 us -> 26.9 us  [the longest x3 12.9 us: digit_round(): lax.ppermute(message, 'seq', [(i, i + k * stride) for i in range(count -...]
    rev x2 -> x0, local copies, waits for them, and re-layouts: 17.6 us -> none  [local(): reversed_powers = powers[:, BLOCK - 1::-1]]
    mul x9 -> x1, other arithmetic: 10.9 us -> 0.83 us  [local(): part[ROWS - 2:] * scale[:, None]]
    mul x2 -> x0, local copies, waits for them, and re-layouts: 9.28 us -> none  [the longest x1 9.28 us: local(): weighted = residue[:, None, :] * powers[:, 1:]]
    pallas_call x0 -> x3, Pallas kernels: none -> 8.85 us  [the longest x1 3.67 us: local(): call(front_kernel, (f32(ROWS * GROUPS, LANES), f32(ROWS * GROUPS, LANES),...]
  transfers between devices with their start and end apart: 5 -> 12, of which waited for: 4 -> 6; matrix products, arithmetic and copies ran while one was open for 38% -> 17% of each run, Pallas kernels for 0% -> 6%
where the time goes in v1:
time: 142 us; the launch traced here: 141 us
  waiting for transfers between devices  43.3 us (30%)
  starting transfers between devices  26.9 us (19%)
  between operations  22.4 us (16%)
  local copies, waits for them, and re-layouts  18.4 us (13%)
  other arithmetic  13.6 us (10%)
  Pallas kernels  8.85 us (6%)
  matrix products  7.15 us (5%)
    reduce_scatter x1, waiting for transfers between devices, local(): lax.psum_scatter(projected.astype(jnp.bfloat16), 'ch', scatter_dimension=...  29.1 us
    ppermute x3, starting transfers between devices, digit_round(): lax.ppermute(message, 'seq', [(i, i + k * stride) for i in range(count -...  12.9 us
    all_gather x1, waiting for transfers between devices, local(): weight = lax.all_gather(out_weight, 'seq', axis=0, tiled=True)  10 us
    ppermute x6, starting transfers between devices, cyclic(): return lax.ppermute(block, 'seq', [(i, shift(i)) for i in range(count)])  9.37 us
    unnamed x24, local copies, waits for them, and re-layouts  7.74 us
    slice x10, local copies, waits for them, and re-layouts, join(): return later[:STATE] + pass_factor * later[STATE, 0] * total  7.48 us
    dot_general x1, matrix products, local(): lax.dot_general(mixed, weight, (((1,), (1,)), ((), ())), preferred_elemen...  7.15 us
    add x1, other arithmetic, local(): entering = enter_low + jnp.exp(-256.0 * low * rate) * alive_low * entering  6.8 us
  transfers between devices with their start and end apart: 12, of which 6 were waited for; matrix products, arithmetic and copies ran while one was open for 17% of the time, Pallas kernels for 6%

profile of v1, /device:TPU:1, one launch (start us, length us, event | category | flops | bytes accessed | tf_op | source)
XLA Modules:
  0.0 140.6 jit_solution(13100788398979144972)
XLA Ops:
  6.5 0.7 all-gather.2.cloned.1.call-update
  7.3 1.3 compare_reduce_fusion
  9.3 0.8 slice_multiply_fusion.2
  10.2 4.6 %collective-permute-start = (bf16[6,1024]{1,0:T(8,128)(2,1)S(1)}, bf16[6,1024]{1,0:T(8,128)(2,1)S(1)}, u32[]{:S(2)}, u32[]{:S(2)}) collective-permute-start(bf16[6,1024]{1,0:T(8,128)(2,1)S(1)} %pad_maximum_fusion), channel_id=1, source_target_pairs={{0,4},{4,8},{8,12},{12,16},{16,20},{20,24},{24,28},{28,32},{32,36}... | collective-permute-start | bytes 36872 | tf_op jit(solution)/shard_map/ppermute | solution.py:214
  14.8 0.9 reshape.33.rate_ref
  15.7 0.8 reshape.32.taps_ref
  16.5 1.0 copy-done
  17.5 1.0 copy-done.1
  18.6 1.0 copy-done.2
  20.9 3.7 %shard_map.100 = (f32[2048,128]{1,0:T(8,128)S(1)}, f32[2048,128]{1,0:T(8,128)S(1)}, f32[136,128]{1,0:T(8,128)S(1)}) custom-call(s32[1,4]{1,0:T(1,128)S(1)} %copy-done.3, s32[1,4]{1,0:T(1,128)S(1)} %copy-done.6, bf16[256,1024]{1,0:T(8,128)(2,1)S(1)} %copy-done, bf16[256,1024]{1,0:T(8,128)(2,1)S(1)} %copy-done.1, bf16[256,1024]{1,0:T(8,128)(2,1)S(1)} %copy-done.2, ...), custom_call_target="tpu_custom_call" | custom-call | flops 20000000 | bytes 4000000 | tf_op jit(solution)/shard_map/pallas_call | solution.py:219
  24.7 1.5 %collective-permute-start.2 = (f32[136,128]{1,0:T(8,128)S(1)}, f32[136,128]{1,0:T(8,128)S(1)}, u32[]{:S(2)}, u32[]{:S(2)}) collective-permute-start(f32[136,128]{1,0:T(8,128)S(1)} %get-tuple-element.8), channel_id=1, source_target_pairs={{0,8},{4,12},{8,0},{12,4},{16,24},{20,28},{24,16},{28,20},{32,40},... | collective-permute-start | bytes 208904 | tf_op jit(solution)/shard_map/ppermute | solution.py:19
  26.2 1.8 %collective-permute-start.1 = (f32[136,128]{1,0:T(8,128)S(1)}, f32[136,128]{1,0:T(8,128)S(1)}, u32[]{:S(2)}, u32[]{:S(2)}) collective-permute-start(f32[136,128]{1,0:T(8,128)S(1)} %get-tuple-element.8), channel_id=1, source_target_pairs={{0,4},{4,8},{8,12},{12,0},{16,20},{20,24},{24,28},{28,16},{32,36},... | collective-permute-start | bytes 208904 | tf_op jit(solution)/shard_map/ppermute | solution.py:19
  32.8 2.5 %add_select_fusion.2 = f32[128,128]{1,0:T(8,128)S(1)} fusion(f32[136,128]{1,0:T(8,128)S(1)} %get-tuple-element.8, f32[128,128]{1,0:T(8,128)S(1)} %reshape.33.rate_ref, f32[136,128]{1,0:T(8,128)S(1)} %collective-permute-done.3, f32[136,128]{1,0:T(8,128)S(1)} %collective-permute-done.2, f32[136,128]{1,0:T(8,128)S(1)} %collective-permute-done.1, f32[]{:T(128)} %bitcast.4, ...), kind=kLoop, calls=%fused_computation.16 | loop fusion | flops 409600 | bytes 393238 | tf_op jit(solution)/shard_map/jit(_where)/select_n | solution.py:199
  35.4 5.6 %collective-permute-start.6 = (f32[136,128]{1,0:T(8,128)S(1)}, f32[136,128]{1,0:T(8,128)S(1)}, u32[]{:S(2)}, u32[]{:S(2)}) collective-permute-start(f32[136,128]{1,0:T(8,128)S(1)} %concatenate.15), channel_id=1, source_target_pairs={{0,48},{4,52},{8,56},{12,60},{16,0},{20,4},{24,8},{28,12},{32,16},... | collective-permute-start | bytes 208904 | tf_op jit(solution)/shard_map/ppermute | solution.py:19
  41.4 1.8 %collective-permute-done.6 = f32[136,128]{1,0:T(8,128)S(1)} collective-permute-done((f32[136,128]{1,0:T(8,128)S(1)}, f32[136,128]{1,0:T(8,128)S(1)}, u32[]{:S(2)}, u32[]{:S(2)}) %collective-permute-start.6) | collective-permute-done | bytes 69664 | tf_op jit(solution)/shard_map/ppermute | solution.py:19
  46.2 0.8 collective-permute-done.4
  48.2 2.0 %add_select_fusion = f32[128,128]{1,0:T(8,128)S(1)} fusion(f32[128,128]{1,0:T(8,128)S(1)} %add_select_fusion.2, f32[128,128]{1,0:T(8,128)S(1)} %reshape.33.rate_ref, f32[136,128]{1,0:T(8,128)S(1)} %collective-permute-done.6, f32[136,128]{1,0:T(8,128)S(1)} %collective-permute-done.5, f32[136,128]{1,0:T(8,128)S(1)} %collective-permute-done.4, f32[]{:T(128)S(6)} %mul.265, ...), kind=kLoop, calls=%fused_computation.13 | loop fusion | flops 409600 | bytes 393238 | tf_op jit(solution)/shard_map/jit(_where)/select_n | solution.py:199
  50.9 7.6 %collective-permute-start.9 = (f32[136,128]{1,0:T(8,128)}, f32[136,128]{1,0:T(8,128)}, u32[]{:S(2)}, u32[]{:S(2)}) collective-permute-start(f32[136,128]{1,0:T(8,128)} %concatenate.16), channel_id=1, source_target_pairs={{0,192},{4,196},{8,200},{12,204},{16,208},{20,212},{24,216},{28,22... | collective-permute-start | bytes 208904 | tf_op jit(solution)/shard_map/ppermute | solution.py:179
  58.5 1.9 %collective-permute-start.7 = (f32[136,128]{1,0:T(8,128)}, f32[136,128]{1,0:T(8,128)}, u32[]{:S(2)}, u32[]{:S(2)}) collective-permute-start(f32[136,128]{1,0:T(8,128)} %concatenate.16), channel_id=1, source_target_pairs={{0,64},{4,68},{8,72},{12,76},{16,80},{20,84},{24,88},{28,92},{32,9... | collective-permute-start | bytes 208904 | tf_op jit(solution)/shard_map/ppermute | solution.py:179
  60.4 3.4 %collective-permute-start.8 = (f32[136,128]{1,0:T(8,128)}, f32[136,128]{1,0:T(8,128)}, u32[]{:S(2)}, u32[]{:S(2)}) collective-permute-start(f32[136,128]{1,0:T(8,128)} %concatenate.16), channel_id=1, source_target_pairs={{0,128},{4,132},{8,136},{12,140},{16,144},{20,148},{24,152},{28,15... | collective-permute-start | bytes 208904 | tf_op jit(solution)/shard_map/ppermute | solution.py:179
  63.8 0.9 reshape.34.residue_ref
  66.0 0.7 copy-done.9
  66.7 3.0 %shard_map.101.inner_ref = f32[2048,128]{1,0:T(8,128)S(1)} custom-call(s32[1,4]{1,0:T(1,128)S(1)} %copy-done.4, s32[1,4]{1,0:T(1,128)S(1)} %copy-done.7, f32[2048,128]{1,0:T(8,128)S(1)} %get-tuple-element.10.gated_ref, f32[128,128]{1,0:T(8,128)S(1)} %reshape.33.rate_ref, f32[128,128]{1,0:T(8,128)S(1)} %reshape.34.residue_ref, f32[8,128]{1,0:T(8,128)S(1)} %bitcast.14), custom_call_target="tpu_custom_call" | custom-call | flops 20000000 | bytes 4000000 | tf_op jit(solution)/shard_map/pallas_call | solution.py:227
  73.5 1.3 slice.136
  74.7 1.2 slice.132
  75.9 1.2 slice.134
  77.1 6.8 %fusion.10.entering_ref = f32[128,128]{1,0:T(8,128)S(1)} fusion(f32[136,128]{1,0:T(8,128)} %collective-permute-done.9, f32[136,128]{1,0:T(8,128)} %collective-permute-done.8, f32[136,128]{1,0:T(8,128)} %collective-permute-done.7, f32[128,128]{1,0:T(8,128)S(1)} %reshape.33.rate_ref, f32[136,128]{1,0:T(8,128)S(1)} %collective-permute-done.6, ...), kind=kLoop, calls=%fused_computation.12 | loop fusion | flops 770048 | bytes 720957 | tf_op jit(solution)/shard_map/add | solution.py:237
  84.6 0.7 copy-done.8
  85.2 2.2 %shard_map.102 = bf16[256,1024]{1,0:T(8,128)(2,1)S(1)} custom-call(s32[1,4]{1,0:T(1,128)S(1)} %copy-done.5, s32[1,4]{1,0:T(1,128)S(1)} %copy-done.8, f32[128,128]{1,0:T(8,128)S(1)} %fusion.10.entering_ref, f32[128,128]{1,0:T(8,128)S(1)} %reshape.33.rate_ref, f32[128,128]{1,0:T(8,128)S(1)} %reshape.34.residue_ref, f32[2048,128]{1,0:T(8,128)S(1)} %get-tuple-element.9.q_ref, ...), custom_call_target="tpu_custom_call" | custom-call | flops 20000000 | bytes 4000000 | tf_op jit(solution)/shard_map/pallas_call | solution.py:238
  87.4 10.0 %all-gather.2.cloned.1.call-done = bf16[4096,1024]{1,0:T(8,128)(2,1)} async-done(((bf16[64,1024]{1,0:T(8,128)(2,1)}), bf16[4096,1024]{1,0:T(8,128)(2,1)}) %all-gather.2.cloned.1.call-update) | async-done | bytes 8388624 | tf_op jit(solution)/shard_map/all_gather | solution.py:208
  97.4 7.2 %convolution_convert_fusion = bf16[256,4096]{1,0:T(8,128)(2,1)} fusion(bf16[256,1024]{1,0:T(8,128)(2,1)S(1)} %shard_map.102, bf16[4096,1024]{1,0:T(8,128)(2,1)} %all-gather.2.cloned.1.call-done), kind=kOutput, calls=%fused_computation | convolution fusion | flops 2148532224 | bytes 11010048 | tf_op jit(solution)/shard_map/dot_general | solution.py:246
  104.6 29.1 %reduce-scatter.2.cloned.1.call-done = bf16[256,1024]{1,0:T(8,128)(2,1)} async-done(((bf16[256,4096]{1,0:T(8,128)(2,1)}), bf16[256,1024]{1,0:T(8,128)(2,1)}) %reduce-scatter.2.cloned.1.call-update) | async-done | bytes 524304 | tf_op jit(solution)/shard_map/reduce_scatter | solution.py:248
  (44 shorter events, 9.2 us)
Async XLA Ops:
  6.5 90.9 %all-gather.2.cloned.1.call-start = ((), (), s32[]{:S(2)}) async-start(), calls=%async_computation.1 | async-start | bytes 8519680 | tf_op jit(solution)/shard_map/all_gather | solution.py:208
  7.3 126.5 %reduce-scatter.2.cloned.1.call-start = ((), (), s32[]{:S(2)}) async-start(), calls=%async_computation.2 | async-start | bytes 2621440 | tf_op jit(solution)/shard_map/reduce_scatter | solution.py:248
  10.2 6.3 %collective-permute-start = (bf16[6,1024]{1,0:T(8,128)(2,1)S(1)}, bf16[6,1024]{1,0:T(8,128)(2,1)S(1)}, u32[]{:S(2)}, u32[]{:S(2)}) collective-permute-start(bf16[6,1024]{1,0:T(8,128)(2,1)S(1)} %pad_maximum_fusion), channel_id=1, source_target_pairs={{0,4},{4,8},{8,12},{12,16},{16,20},{20,24},{24,28},{28,32},{32,36}... | collective-permute-start | bytes 36872 | tf_op jit(solution)/shard_map/ppermute | solution.py:214
  16.5 1.0 copy-start
  17.5 1.0 copy-start.1
  18.6 1.0 copy-start.2
  19.6 0.7 copy-start.3
  20.3 0.7 copy-start.6
  24.6 4.1 %collective-permute-start.3 = (f32[136,128]{1,0:T(8,128)S(1)}, f32[136,128]{1,0:T(8,128)S(1)}, u32[]{:S(2)}, u32[]{:S(2)}) collective-permute-start(f32[136,128]{1,0:T(8,128)S(1)} %get-tuple-element.8), channel_id=1, source_target_pairs={{0,12},{4,0},{8,4},{12,8},{16,28},{20,16},{24,20},{28,24},{32,44},... | collective-permute-start | bytes 208904 | tf_op jit(solution)/shard_map/ppermute | solution.py:19
  24.7 5.9 %collective-permute-start.2 = (f32[136,128]{1,0:T(8,128)S(1)}, f32[136,128]{1,0:T(8,128)S(1)}, u32[]{:S(2)}, u32[]{:S(2)}) collective-permute-start(f32[136,128]{1,0:T(8,128)S(1)} %get-tuple-element.8), channel_id=1, source_target_pairs={{0,8},{4,12},{8,0},{12,4},{16,24},{20,28},{24,16},{28,20},{32,40},... | collective-permute-start | bytes 208904 | tf_op jit(solution)/shard_map/ppermute | solution.py:19
  26.2 5.5 %collective-permute-start.1 = (f32[136,128]{1,0:T(8,128)S(1)}, f32[136,128]{1,0:T(8,128)S(1)}, u32[]{:S(2)}, u32[]{:S(2)}) collective-permute-start(f32[136,128]{1,0:T(8,128)S(1)} %get-tuple-element.8), channel_id=1, source_target_pairs={{0,4},{4,8},{8,12},{12,0},{16,20},{20,24},{24,28},{28,16},{32,36},... | collective-permute-start | bytes 208904 | tf_op jit(solution)/shard_map/ppermute | solution.py:19
  35.4 7.8 %collective-permute-start.6 = (f32[136,128]{1,0:T(8,128)S(1)}, f32[136,128]{1,0:T(8,128)S(1)}, u32[]{:S(2)}, u32[]{:S(2)}) collective-permute-start(f32[136,128]{1,0:T(8,128)S(1)} %concatenate.15), channel_id=1, source_target_pairs={{0,48},{4,52},{8,56},{12,60},{16,0},{20,4},{24,8},{28,12},{32,16},... | collective-permute-start | bytes 208904 | tf_op jit(solution)/shard_map/ppermute | solution.py:19
  41.0 3.9 %collective-permute-start.5 = (f32[136,128]{1,0:T(8,128)S(1)}, f32[136,128]{1,0:T(8,128)S(1)}, u32[]{:S(2)}, u32[]{:S(2)}) collective-permute-start(f32[136,128]{1,0:T(8,128)S(1)} %concatenate.15), channel_id=1, source_target_pairs={{0,32},{4,36},{8,40},{12,44},{16,48},{20,52},{24,56},{28,60},{32,0... | collective-permute-start | bytes 208904 | tf_op jit(solution)/shard_map/ppermute | solution.py:19
  41.0 6.1 %collective-permute-start.4 = (f32[136,128]{1,0:T(8,128)S(1)}, f32[136,128]{1,0:T(8,128)S(1)}, u32[]{:S(2)}, u32[]{:S(2)}) collective-permute-start(f32[136,128]{1,0:T(8,128)S(1)} %concatenate.15), channel_id=1, source_target_pairs={{0,16},{4,20},{8,24},{12,28},{16,32},{20,36},{24,40},{28,44},{32,4... | collective-permute-start | bytes 208904 | tf_op jit(solution)/shard_map/ppermute | solution.py:19
  44.9 19.7 %copy-start.10 = (f32[136,128]{1,0:T(8,128)}, f32[136,128]{1,0:T(8,128)S(1)}, u32[]{:S(2)}) copy-start(f32[136,128]{1,0:T(8,128)S(1)} %collective-permute-done.5) | copy-start | bytes 208900
  47.0 17.6 %copy-start.11 = (f32[136,128]{1,0:T(8,128)}, f32[136,128]{1,0:T(8,128)S(1)}, u32[]{:S(2)}) copy-start(f32[136,128]{1,0:T(8,128)S(1)} %collective-permute-done.4) | copy-start | bytes 208900
  50.9 22.6 %collective-permute-start.9 = (f32[136,128]{1,0:T(8,128)}, f32[136,128]{1,0:T(8,128)}, u32[]{:S(2)}, u32[]{:S(2)}) collective-permute-start(f32[136,128]{1,0:T(8,128)} %concatenate.16), channel_id=1, source_target_pairs={{0,192},{4,196},{8,200},{12,204},{16,208},{20,212},{24,216},{28,22... | collective-permute-start | bytes 208904 | tf_op jit(solution)/shard_map/ppermute | solution.py:179
  58.5 16.2 %collective-permute-start.7 = (f32[136,128]{1,0:T(8,128)}, f32[136,128]{1,0:T(8,128)}, u32[]{:S(2)}, u32[]{:S(2)}) collective-permute-start(f32[136,128]{1,0:T(8,128)} %concatenate.16), channel_id=1, source_target_pairs={{0,64},{4,68},{8,72},{12,76},{16,80},{20,84},{24,88},{28,92},{32,9... | collective-permute-start | bytes 208904 | tf_op jit(solution)/shard_map/ppermute | solution.py:179
  60.4 15.5 %collective-permute-start.8 = (f32[136,128]{1,0:T(8,128)}, f32[136,128]{1,0:T(8,128)}, u32[]{:S(2)}, u32[]{:S(2)}) collective-permute-start(f32[136,128]{1,0:T(8,128)} %concatenate.16), channel_id=1, source_target_pairs={{0,128},{4,132},{8,136},{12,140},{16,144},{20,148},{24,152},{28,15... | collective-permute-start | bytes 208904 | tf_op jit(solution)/shard_map/ppermute | solution.py:179
  64.7 0.7 copy-start.4
  65.3 0.7 copy-start.7
  66.0 0.7 copy-start.9
  83.9 0.7 copy-start.5
  84.6 0.7 copy-start.8
Sparse Core Ops, SparseCore 0:
  10.1 87.2 all-gather.1
  104.7 28.9 reduce-scatter.1

commit v2 on v1

v2 whole, which is shorter than its diff:
```python
import jax
import jax.numpy as jnp
from jax import lax
from jax.experimental import pallas as pl
from jax.experimental.pallas import tpu as pltpu
from jax.sharding import PartitionSpec as P

MODES = 16
ROWS = 256
LANES = 128
GROUPS = 8
WIDTH = GROUPS * LANES
STEPS = 8
CHUNKS = ROWS // STEPS
PIECE = 64
STATE = MODES * GROUPS
SHARD = 64
HALF = WIDTH // 2
QUARTER = WIDTH // 4


def reset_place(starts_ref, flags_ref):
    place = jnp.int32(0)
    found = jnp.int32(0)
    for slot in range(4):
        hit = (flags_ref[0, slot] == 1) & (starts_ref[0, slot] < ROWS)
        place = jnp.where(hit, starts_ref[0, slot], place)
        found = jnp.where(hit, jnp.int32(1), found)
    return place, found


def row_slice(t):
    return pl.ds(pl.multiple_of(t * GROUPS, GROUPS), GROUPS)


def spread(source, scratch):
    for group in range(GROUPS):
        scratch[pl.ds(group, MODES, stride=GROUPS), :] = source[:, group * LANES : (group + 1) * LANES]


def poles(ref):
    return [ref[n * GROUPS : (n + 1) * GROUPS, :] for n in range(MODES)]


def tail_kernel(starts_ref, q_ref, k_ref, v_ref, shard_ref, out_ref, shard_out):
    ends = starts_ref[0, 0] == ROWS - 1
    for slot in range(1, 4):
        ends = ends | (starts_ref[0, slot] == ROWS - 1)
    scale = jnp.where(ends, 0.0, 1.0)
    for which, source in enumerate((q_ref, k_ref, v_ref)):
        rows = source[...].astype(jnp.float32)
        out_ref[2 * which : 2 * which + 1, :] = rows[14:15, :] * scale
        out_ref[2 * which + 1 : 2 * which + 2, :] = rows[15:16, :]
    out_ref[6:8, :] = jnp.zeros((2, WIDTH), jnp.float32)
    shard_out[...] = shard_ref[...]


def column_kernel(shard_ref, far_ref, halo_ref, out_ref):
    del halo_ref
    out_ref[:SHARD, :] = shard_ref[...]
    out_ref[SHARD:, :] = far_ref[...]


def front_kernel(starts_ref, flags_ref, q_hbm, k_hbm, v_hbm, halo_ref, taps_ref, rate_ref,
                 q_out, gated_out, state_out, held, wide, spread_rate, sems):
    copies = [
        pltpu.make_async_copy(source, held.at[feature], sems.at[feature])
        for feature, source in enumerate((k_hbm, v_hbm, q_hbm))
    ]
    for copy in copies:
        copy.start()
    spread(rate_ref, spread_rate)
    for feature in range(3):
        which = (1, 2, 0)[feature]
        wide[feature, 6:8, :] = halo_ref[2 * which : 2 * which + 2, :]
        copies[feature].wait()
        wide[feature, 8:, :] = held[feature].astype(jnp.float32)
    for first in range(0, ROWS, PIECE):
        t = lax.broadcasted_iota(jnp.int32, (PIECE, LANES), 0) + first
        keep_one = jnp.ones((PIECE, LANES), jnp.float32)
        keep_two = keep_one
        for slot in range(4):
            at = starts_ref[0, slot]
            keep_one = jnp.where(t == at, 0.0, keep_one)
            keep_two = jnp.where((t == at) | (t == at + 1), 0.0, keep_two)
        for group in range(GROUPS):
            lanes = slice(group * LANES, (group + 1) * LANES)

            def short(feature, which):
                total = taps_ref[which, 0:1, lanes] * wide[feature, 8 + first : 8 + first + PIECE, lanes]
                total = total + (taps_ref[which, 1:2, lanes] * keep_one) * wide[
                    feature, 7 + first : 7 + first + PIECE, lanes]
                total = total + (taps_ref[which, 2:3, lanes] * keep_two) * wide[
                    feature, 6 + first : 6 + first + PIECE, lanes]
                return total.astype(jnp.bfloat16).astype(jnp.float32)

            rows = pl.ds(first * GROUPS + group, PIECE, stride=GROUPS)
            gated_out[rows, :] = short(0, 1) * short(1, 2)
            q_out[rows, :] = short(2, 0)
    place, found = reset_place(starts_ref, flags_ref)
    decay = [jnp.exp(-rate) for rate in poles(spread_rate)]

    def chunk(index, state):
        for step in range(STEPS):
            t = index * STEPS + step
            row = jnp.where(t >= place, gated_out[row_slice(t), :], 0.0)
            state = tuple(decay[n] * state[n] + row for n in range(MODES))
        return state

    zero = jnp.zeros((GROUPS, LANES), jnp.float32)
    state = lax.fori_loop(place // STEPS, CHUNKS, chunk, (zero,) * MODES)
    for n in range(MODES):
        state_out[n * GROUPS : (n + 1) * GROUPS, :] = state[n]
    state_out[STATE:, :] = jnp.full((GROUPS, LANES), 1 - found, jnp.int32).astype(jnp.float32)


def digit_join(mine, got, length, spread_rate, total=None, own=None):
    entering, whole = [], []
    alive = jnp.ones((GROUPS, LANES), jnp.float32)
    whole_alive = alive
    flags = [ref[STATE:, :] for ref in got]
    for k, flag in zip((3, 2, 1), flags):
        alive = alive * jnp.where(k <= mine, flag, 1.0)
    for n in range(MODES):
        rows = slice(n * GROUPS, (n + 1) * GROUPS)
        passing = jnp.exp(-length * spread_rate[rows, :])
        value = jnp.zeros((GROUPS, LANES), jnp.float32)
        for k, ref, flag in zip((3, 2, 1), got, flags):
            value = jnp.where(k <= mine, ref[rows, :] + passing * flag * value, 0.0)
        entering.append(value)
        if own is not None:
            value = own[rows, :] + passing * own[STATE:, :] * value
            for k, ref, flag in zip((3, 2, 1), got, flags):
                value = jnp.where(k > mine, ref[rows, :] + passing * flag * value, value)
            whole.append(value)
    if own is not None:
        whole_alive = own[STATE:, :] * flags[0] * flags[1] * flags[2]
    return entering, alive, whole, whole_alive


def low_kernel(own, got3, got2, got1, rate_ref, enter_out, next_out, spread_rate):
    spread(rate_ref, spread_rate)
    mine = lax.axis_index("seq") % 4
    entering, alive, whole, whole_alive = digit_join(
        mine, (got3, got2, got1), 256.0, spread_rate, own=own)
    for n in range(MODES):
        enter_out[n * GROUPS : (n + 1) * GROUPS, :] = entering[n]
        next_out[n * GROUPS : (n + 1) * GROUPS, :] = whole[n]
    enter_out[STATE:, :] = alive
    next_out[STATE:, :] = whole_alive


def middle_kernel(own, got3, got2, got1, low, rate_ref, enter_out, next_out, spread_rate):
    spread(rate_ref, spread_rate)
    seq = lax.axis_index("seq")
    entering, alive, whole, whole_alive = digit_join(
        (seq // 4) % 4, (got3, got2, got1), 1024.0, spread_rate, own=own)
    span = (seq % 4).astype(jnp.float32) * 256.0
    low_alive = low[STATE:, :]
    for n in range(MODES):
        rows = slice(n * GROUPS, (n + 1) * GROUPS)
        reach = jnp.exp(-span * spread_rate[rows, :]) * low_alive
        enter_out[rows, :] = low[rows, :] + reach * entering[n]
        next_out[rows, :] = whole[n]
    enter_out[STATE:, :] = alive * low_alive
    next_out[STATE:, :] = whole_alive


def mix_kernel(starts_ref, flags_ref, got3, got2, got1, before, rate_ref, residue_ref, skip_ref,
               q_ref, gated_ref, mixed_out, spread_rate, spread_gain, rows_ref):
    spread(rate_ref, spread_rate)
    spread(residue_ref, spread_gain)
    skip = jnp.concatenate(
        [skip_ref[:, group * LANES : (group + 1) * LANES] for group in range(GROUPS)], axis=0)
    seq = lax.axis_index("seq")
    entering, _, _, _ = digit_join(seq // 16, (got3, got2, got1), 4096.0, spread_rate)
    span = (seq % 16).astype(jnp.float32) * 256.0
    before_alive = before[STATE:, :]
    state, decay = [], []
    for n, rate in enumerate(poles(spread_rate)):
        rows = slice(n * GROUPS, (n + 1) * GROUPS)
        state.append(before[rows, :] + jnp.exp(-span * rate) * before_alive * entering[n])
        decay.append(jnp.exp(-rate))
    state = tuple(state)
    weight = poles(spread_gain)
    place, found = reset_place(starts_ref, flags_ref)
    cut_chunk = jnp.where(found == 1, place // STEPS, CHUNKS)

    def run(index, state, cutting):
        for step in range(STEPS):
            t = index * STEPS + step
            row = gated_ref[row_slice(t), :]
            if cutting:
                state = tuple(jnp.where(t == place, 0.0, state[n]) for n in range(MODES))
            state = tuple(decay[n] * state[n] + row for n in range(MODES))
            terms = [weight[n] * state[n] for n in range(MODES)] + [skip * row]
            while len(terms) > 1:
                paired = [terms[i] + terms[i + 1] for i in range(0, len(terms) - 1, 2)]
                terms = paired + terms[len(terms) - len(terms) % 2 :]
            rows_ref[row_slice(t), :] = q_ref[row_slice(t), :] * terms[0]
        return state

    state = lax.fori_loop(0, cut_chunk, lambda i, s: run(i, s, False), state)
    state = lax.fori_loop(
        cut_chunk, jnp.minimum(cut_chunk + 1, CHUNKS), lambda i, s: run(i, s, True), state)
    lax.fori_loop(cut_chunk + 1, CHUNKS, lambda i, s: run(i, s, False), state)
    for group in range(GROUPS):
        mixed_out[:, group * LANES : (group + 1) * LANES] = rows_ref[
            pl.ds(group, ROWS, stride=GROUPS), :].astype(jnp.bfloat16)


def project_kernel(turns, mixed_ref, gathered, other, earlier, before, *refs):
    del earlier, before
    outs, weight = refs[: 2 * len(turns)], refs[2 * len(turns)]
    seq, ch = lax.axis_index("seq"), lax.axis_index("ch")
    z, y, core = seq // 8, (seq // 2) % 4, seq % 2
    for slot, turn in enumerate(turns):
        target = (ch + turn) % 4
        for side, source in enumerate((gathered, other)):
            at_core = (core + side) % 2
            for half in range(2):
                age = (z - 2 * target - half + 16) % 8
                for gap in range(2):
                    at_y = (y // 2 + gap) % 2
                    row = pl.multiple_of(((half * 2 + at_y) * 2 + at_core) * SHARD, SHARD)
                    start = pl.multiple_of((age * 2 + gap) * SHARD, SHARD)
                    weight[slot, pl.ds(row, SHARD), :] = source[pl.ds(start, SHARD), :]
        for part in range(2):
            outs[2 * slot + part][...] = lax.dot_general(
                mixed_ref[...], weight[slot, part * QUARTER : (part + 1) * QUARTER, :],
                (((1,), (1,)), ((), ())), preferred_element_type=jnp.float32).astype(jnp.bfloat16)


def add_kernel(right_ref, right_own, left_ref, left_own, right_out, left_out):
    right_out[...] = (right_ref[...].astype(jnp.float32) + right_own[...].astype(jnp.float32)).astype(jnp.bfloat16)
    left_out[...] = (left_ref[...].astype(jnp.float32) + left_own[...].astype(jnp.float32)).astype(jnp.bfloat16)


def summed(own_a, own_b, sum_a, sum_b, one_a, one_b, part):
    chosen = ((own_a, sum_a, one_a), (own_b, sum_b, one_b))[part]
    first, second, third = [ref[...].astype(jnp.float32) for ref in chosen]
    return (first + second + third).astype(jnp.bfloat16)


def total_kernel(*refs):
    for part in range(2):
        refs[6][:, part * QUARTER : (part + 1) * QUARTER] = summed(*refs[:6], part)


def last_kernel(*refs):
    mate, out_ref = refs[6], refs[7]
    parity = (lax.axis_index("seq") // 2) % 2
    for part in range(2):
        mine = summed(*refs[:6], part)
        for at_y in range(2):
            block = 4 * part + 2 * at_y
            lanes = slice(at_y * LANES, (at_y + 1) * LANES)
            out_ref[:, pl.ds(pl.multiple_of((block + parity) * LANES, LANES), LANES)] = mine[:, lanes]
            lanes = slice((2 * part + at_y) * LANES, (2 * part + at_y + 1) * LANES)
            out_ref[:, pl.ds(pl.multiple_of((block + 1 - parity) * LANES, LANES), LANES)] = mate[:, lanes]


SMALL = pl.BlockSpec(memory_space=pltpu.SMEM)
WHOLE = pl.BlockSpec(memory_space=pltpu.VMEM)
FAR = pl.BlockSpec(memory_space=pl.ANY)
LIMIT = 40 * 1024 * 1024


def call(kernel, outs, specs, scratch=(), flops=4_000_000, moved=2_000_000):
    return pl.pallas_call(
        kernel,
        out_shape=outs,
        in_specs=specs,
        out_specs=jax.tree.map(lambda _: WHOLE, outs),
        scratch_shapes=scratch,
        compiler_params=pltpu.CompilerParams(vmem_limit_bytes=LIMIT),
        cost_estimate=pl.CostEstimate(flops=flops, bytes_accessed=moved, transcendentals=0),
    )


def f32(*shape):
    return jax.ShapeDtypeStruct(shape, jnp.float32)


def b16(*shape):
    return jax.ShapeDtypeStruct(shape, jnp.bfloat16)


def move(block, target):
    count = lax.axis_size("seq")
    return lax.ppermute(block, "seq", [(i, target(i)) for i in range(count)])


def along_y(block, gap):
    return move(block, lambda i: (i // 8) * 8 + ((i // 2 + gap) % 4) * 2 + i % 2)


def along_z(block, gap):
    return move(block, lambda i: (i + 8 * gap) % 64)


def across(block):
    return move(block, lambda i: i ^ 1)


def digit_moves(message, stride):
    return [
        move(message, lambda i: i - ((i // stride) % 4) * stride + ((i // stride + k) % 4) * stride)
        for k in (3, 2, 1)
    ]


def around(block, gap):
    return lax.ppermute(block, "ch", [(i, (i + gap) % 4) for i in range(4)])


def after(parts, earlier):
    return lax.optimization_barrier((parts, earlier))[0]


def project(turns, mixed, gathered, other, earlier):
    return pl.pallas_call(
        lambda *refs: project_kernel(turns, *refs),
        out_shape=(b16(ROWS, QUARTER),) * (2 * len(turns)),
        in_specs=[WHOLE] * 3 + [FAR] * 2,
        out_specs=(WHOLE,) * (2 * len(turns)),
        scratch_shapes=[pltpu.VMEM((len(turns), HALF, WIDTH), jnp.bfloat16)],
        compiler_params=pltpu.CompilerParams(vmem_limit_bytes=LIMIT),
        cost_estimate=pl.CostEstimate(
            flops=len(turns) * 2 * ROWS * HALF * WIDTH,
            bytes_accessed=len(turns) * 4 * HALF * WIDTH, transcendentals=0),
    )(mixed, gathered, other, *earlier)


def reduced(mixed, gathered, other, orders):
    opposite_a, opposite_b = project((2,), mixed, gathered, other, orders[0])
    from_left, from_right = around(opposite_a, 1), around(opposite_b, -1)
    next_a, next_b, previous_a, previous_b = project(
        (1, 3), mixed, gathered, other, orders[1] or (opposite_a, opposite_b))
    one_b, one_a = around(next_b, 1), around(previous_a, -1)
    own_a, own_b = project((0,), mixed, gathered, other, orders[2] or (next_a, next_b))
    to_right, to_left = call(add_kernel, (b16(ROWS, QUARTER),) * 2, [WHOLE] * 4)(
        from_left, next_a, from_right, previous_b)
    sum_a, sum_b = around(to_right, 1), around(to_left, -1)
    return (own_a, own_b, sum_a, sum_b, one_a, one_b), to_right


def local(q_feat, k_feat, v_feat, short_taps, decay_rate, residue, skip_gain, out_weight,
          doc_starts, reset_flags):
    count = lax.axis_size("seq")
    tail_rows = pl.BlockSpec((16, WIDTH), lambda i: (ROWS // 16 - 1, 0))
    whole_shard = pl.BlockSpec((SHARD, WIDTH), lambda i: (0, 0))
    tails, shard = pl.pallas_call(
        tail_kernel,
        grid=(1,),
        out_shape=(f32(8, WIDTH), b16(SHARD, WIDTH)),
        in_specs=[SMALL] + [tail_rows] * 3 + [whole_shard],
        out_specs=(pl.BlockSpec((8, WIDTH), lambda i: (0, 0)), whole_shard),
    )(doc_starts, q_feat, k_feat, v_feat, out_weight)
    halo = lax.ppermute(tails, "seq", [(i, i + 1) for i in range(count - 1)])

    column = call(column_kernel, b16(2 * SHARD, WIDTH), [WHOLE] * 2 + [FAR])(
        shard, along_y(shard, 2), halo)
    right, left = [along_z(column, 1)], [along_z(column, 7)]

    def relay(earlier):
        ahead, behind = after((right[-1], left[-1]), earlier)
        right.append(along_z(ahead, 1))
        left.append(along_z(behind, 7))

    q_rows, gated, message = call(
        front_kernel,
        (f32(ROWS * GROUPS, LANES), f32(ROWS * GROUPS, LANES), f32(STATE + GROUPS, LANES)),
        [SMALL] * 2 + [FAR] * 3 + [WHOLE] * 3,
        scratch=[
            pltpu.VMEM((3, ROWS, WIDTH), jnp.bfloat16),
            pltpu.VMEM((3, ROWS + 8, WIDTH), jnp.float32),
            pltpu.VMEM((STATE, LANES), jnp.float32),
            pltpu.SemaphoreType.DMA((3,)),
        ],
        flops=20_000_000,
        moved=4_000_000,
    )(doc_starts, reset_flags, q_feat, k_feat, v_feat, halo, short_taps, decay_rate)

    pole_scratch = pltpu.VMEM((STATE, LANES), jnp.float32)
    two_messages = (f32(STATE + GROUPS, LANES), f32(STATE + GROUPS, LANES))
    low, following = call(low_kernel, two_messages, [WHOLE] * 5, scratch=[pole_scratch])(
        message, *digit_moves(message, 1), decay_rate)
    relay(message)
    relay(following)
    before, final = call(middle_kernel, two_messages, [WHOLE] * 6, scratch=[pole_scratch])(
        following, *digit_moves(following, 4), low, decay_rate)
    high = [
        lax.ppermute(final, "seq", [(i, i + k * 16) for i in range(count - k * 16)])
        for k in (3, 2, 1)
    ]
    ahead, behind = after((right[-1][:SHARD], left[-1][SHARD:]), final)
    parts = [column] + right + [along_z(ahead, 1), along_z(behind, 7)] + left[::-1]
    gathered = jnp.concatenate(after(parts, high), axis=0)
    other = across(gathered)
    mixed = call(
        mix_kernel,
        b16(ROWS, WIDTH),
        [SMALL] * 2 + [WHOLE] * 9,
        scratch=[pole_scratch, pole_scratch, pltpu.VMEM((ROWS * GROUPS, LANES), jnp.float32)],
        flops=20_000_000,
        moved=4_000_000,
    )(doc_starts, reset_flags, *high, before, decay_rate, residue, skip_gain[None, :], q_rows, gated)

    mate = move(mixed, lambda i: i ^ 2)
    mine, done = reduced(mixed, gathered, other, ((decay_rate, residue), None, None))
    parts, _ = reduced(mate, gathered, other, ((done, mine[0]), mine[4:], mine[2:4]))
    theirs = call(total_kernel, b16(ROWS, HALF), [WHOLE] * 6)(*parts)
    back = move(theirs, lambda i: i ^ 2)
    return call(last_kernel, b16(ROWS, WIDTH), [WHOLE] * 7)(*mine, back)


def solution(mesh):
    placed = (
        P("seq", "ch"),
        P("seq", "ch"),
        P("seq", "ch"),
        P(None, None, "ch"),
        P(None, "ch"),
        P(None, "ch"),
        P("ch"),
        P("seq", "ch"),
        P("seq", None),
        P("seq", None),
    )
    return jax.shard_map(
        local, mesh=mesh, in_specs=placed, out_specs=P("seq", "ch"), check_vma=False
    )
```

time: 142 us -> 104 us (0.73)
  the two profiles are of different devices: /device:TPU:1 before, /device:TPU:6 now
where the time goes in v2:
time: 104 us
  starting transfers between devices  58.2 us (56%)
  waiting for transfers between devices  30.3 us (29%)
  Pallas kernels  14.1 us (14%)
  local copies, waits for them, and re-layouts  1.12 us (1%)
    ppermute x18, starting transfers between devices, move(): return lax.ppermute(block, 'seq', [(i, target(i)) for i in range(count)])  33.2 us
    ppermute x18, waiting for transfers between devices, move(): return lax.ppermute(block, 'seq', [(i, target(i)) for i in range(count)])  20.8 us
    ppermute x12, starting transfers between devices, around(): return lax.ppermute(block, 'ch', [(i, (i + gap) % 4) for i in range(4)])  14.8 us
    ppermute x3, starting transfers between devices, local(): lax.ppermute(final, 'seq', [(i, i + k * 16) for i in range(count - k * 16)])  8.75 us
    ppermute x12, waiting for transfers between devices, around(): return lax.ppermute(block, 'ch', [(i, (i + gap) % 4) for i in range(4)])  6.52 us
    pallas_call x6, Pallas kernels, project(): pl.pallas_call(lambda *refs: project_kernel(turns, *refs), out_shape=(b16...  3.87 us
    pallas_call x1, Pallas kernels, local(): call(front_kernel, (f32(ROWS * GROUPS, LANES), f32(ROWS * GROUPS, LANES),...  3.82 us
    pallas_call x1, Pallas kernels, local(): call(mix_kernel, b16(ROWS, WIDTH), [SMALL] * 2 + [WHOLE] * 9, scratch=[po...  3.29 us
  transfers between devices with their start and end apart: 34, of which 18 were waited for; matrix products, arithmetic and copies ran while one was open for 0% of the time, Pallas kernels for 11%

profile of v2, /device:TPU:6, one launch (start us, length us, event | category | flops | bytes accessed | tf_op | source)
XLA Modules:
  0.0 104.2 jit_solution(13814824776567100426)
XLA Ops:
  0.0 1.7 %shard_map.100 = (f32[8,1024]{1,0:T(8,128)}, bf16[64,1024]{1,0:T(8,128)(2,1)}) custom-call(s32[1,4]{1,0:T(1,128)} %starts_ref.5, bf16[256,1024]{1,0:T(8,128)(2,1)} %q_hbm.1, bf16[256,1024]{1,0:T(8,128)(2,1)} %k_hbm.1, bf16[256,1024]{1,0:T(8,128)(2,1)} %v_hbm.1, bf16[64,1024]{1,0:T(8,128)(2,1)} %shard_ref.1), custom_call_target="tpu_custom_call" | custom-call | tf_op jit(solution)/shard_map/pallas_call | solution.py:353
  1.8 3.2 %collective-permute-start.10 = (bf16[64,1024]{1,0:T(8,128)(2,1)}, bf16[64,1024]{1,0:T(8,128)(2,1)S(1)}, u32[]{:S(2)}, u32[]{:S(2)}) collective-permute-start(bf16[64,1024]{1,0:T(8,128)(2,1)} %get-tuple-element.57.shard_ref), channel_id=1, source_target_pairs={{0,16},{4,20},{8,24},{12,28},{16,0},{20,4},{24,8},{28,12},{32,48},... | collective-permute-start | bytes 393224 | tf_op jit(solution)/shard_map/ppermute | solution.py:291
  5.0 1.4 %collective-permute-start = (f32[8,1024]{1,0:T(8,128)}, f32[8,1024]{1,0:T(8,128)S(1)}, u32[]{:S(2)}, u32[]{:S(2)}) collective-permute-start(f32[8,1024]{1,0:T(8,128)} %get-tuple-element.49), channel_id=1, source_target_pairs={{0,4},{4,8},{8,12},{12,16},{16,20},{20,24},{24,28},{28,32},{32,36}... | collective-permute-start | bytes 98312 | tf_op jit(solution)/shard_map/ppermute | solution.py:360
  7.5 1.2 %collective-permute-done.10.far_ref = bf16[64,1024]{1,0:T(8,128)(2,1)S(1)} collective-permute-done((bf16[64,1024]{1,0:T(8,128)(2,1)}, bf16[64,1024]{1,0:T(8,128)(2,1)S(1)}, u32[]{:S(2)}, u32[]{:S(2)}) %collective-permute-start.10) | collective-permute-done | bytes 131104 | tf_op jit(solution)/shard_map/ppermute | solution.py:291
  9.7 5.8 %collective-permute-start.11 = (bf16[128,1024]{1,0:T(8,128)(2,1)S(1)}, bf16[128,1024]{1,0:T(8,128)(2,1)S(1)}, u32[]{:S(2)}, u32[]{:S(2)}) collective-permute-start(bf16[128,1024]{1,0:T(8,128)(2,1)S(1)} %shard_map.105), channel_id=1, source_target_pairs={{0,32},{4,36},{8,40},{12,44},{16,48},{20,52},{24,56},{28,60},{32,6... | collective-permute-start | bytes 786440 | tf_op jit(solution)/shard_map/ppermute | solution.py:291
  15.5 4.0 %collective-permute-start.12 = (bf16[128,1024]{1,0:T(8,128)(2,1)S(1)}, bf16[128,1024]{1,0:T(8,128)(2,1)S(1)}, u32[]{:S(2)}, u32[]{:S(2)}) collective-permute-start(bf16[128,1024]{1,0:T(8,128)(2,1)S(1)} %shard_map.105), channel_id=1, source_target_pairs={{0,224},{4,228},{8,232},{12,236},{16,240},{20,244},{24,248},{28,25... | collective-permute-start | bytes 786440 | tf_op jit(solution)/shard_map/ppermute | solution.py:291
  19.5 3.8 %shard_map.101 = (f32[2048,128]{1,0:T(8,128)S(1)}, f32[2048,128]{1,0:T(8,128)S(1)}, f32[136,128]{1,0:T(8,128)S(1)}) custom-call(s32[1,4]{1,0:T(1,128)S(1)} %copy-done.7, s32[1,4]{1,0:T(1,128)S(1)} %copy-done.9, bf16[256,1024]{1,0:T(8,128)(2,1)S(1)} %copy-done, bf16[256,1024]{1,0:T(8,128)(2,1)S(1)} %copy-done.1, bf16[256,1024]{1,0:T(8,128)(2,1)S(1)} %copy-done.2, ...), custom_call_target="tpu_custom_call" | custom-call | flops 20000000 | bytes 4000000 | tf_op jit(solution)/shard_map/pallas_call | solution.py:371
  24.0 3.7 %collective-permute-start.14 = (bf16[128,1024]{1,0:T(8,128)(2,1)S(1)}, bf16[128,1024]{1,0:T(8,128)(2,1)S(1)}, u32[]{:S(2)}, u32[]{:S(2)}) collective-permute-start(bf16[128,1024]{1,0:T(8,128)(2,1)S(1)} %collective-permute-done.12), channel_id=1, source_target_pairs={{0,224},{4,228},{8,232},{12,236},{16,240},{20,244},{24,248},{28,25... | collective-permute-start | bytes 786440 | tf_op jit(solution)/shard_map/ppermute | solution.py:291
  28.2 1.9 %collective-permute-done.1.got3 = f32[136,128]{1,0:T(8,128)S(1)} collective-permute-done((f32[136,128]{1,0:T(8,128)S(1)}, f32[136,128]{1,0:T(8,128)S(1)}, u32[]{:S(2)}, u32[]{:S(2)}) %collective-permute-start.1) | collective-permute-done | bytes 69664 | tf_op jit(solution)/shard_map/ppermute | solution.py:291
  30.1 2.6 %collective-permute-done.2.got2 = f32[136,128]{1,0:T(8,128)S(1)} collective-permute-done((f32[136,128]{1,0:T(8,128)S(1)}, f32[136,128]{1,0:T(8,128)S(1)}, u32[]{:S(2)}, u32[]{:S(2)}) %collective-permute-start.2) | collective-permute-done | bytes 69664 | tf_op jit(solution)/shard_map/ppermute | solution.py:291
  33.1 4.6 %collective-permute-start.15 = (bf16[128,1024]{1,0:T(8,128)(2,1)S(1)}, bf16[128,1024]{1,0:T(8,128)(2,1)S(1)}, u32[]{:S(2)}, u32[]{:S(2)}) collective-permute-start(bf16[128,1024]{1,0:T(8,128)(2,1)S(1)} %collective-permute-done.13), channel_id=1, source_target_pairs={{0,32},{4,36},{8,40},{12,44},{16,48},{20,52},{24,56},{28,60},{32,6... | collective-permute-start | bytes 786440 | tf_op jit(solution)/shard_map/ppermute | solution.py:291
  37.8 2.0 %collective-permute-start.5 = (f32[136,128]{1,0:T(8,128)S(1)}, f32[136,128]{1,0:T(8,128)S(1)}, u32[]{:S(2)}, u32[]{:S(2)}) collective-permute-start(f32[136,128]{1,0:T(8,128)S(1)} %get-tuple-element.51.own), channel_id=1, source_target_pairs={{0,32},{4,36},{8,40},{12,44},{16,48},{20,52},{24,56},{28,60},{32,0... | collective-permute-start | bytes 208904 | tf_op jit(solution)/shard_map/ppermute | solution.py:291
  39.8 3.5 %collective-permute-start.6 = (f32[136,128]{1,0:T(8,128)S(1)}, f32[136,128]{1,0:T(8,128)S(1)}, u32[]{:S(2)}, u32[]{:S(2)}) collective-permute-start(f32[136,128]{1,0:T(8,128)S(1)} %get-tuple-element.51.own), channel_id=1, source_target_pairs={{0,16},{4,20},{8,24},{12,28},{16,32},{20,36},{24,40},{28,44},{32,4... | collective-permute-start | bytes 208904 | tf_op jit(solution)/shard_map/ppermute | solution.py:291
  43.9 3.2 %collective-permute-done.5.got2 = f32[136,128]{1,0:T(8,128)S(1)} collective-permute-done((f32[136,128]{1,0:T(8,128)S(1)}, f32[136,128]{1,0:T(8,128)S(1)}, u32[]{:S(2)}, u32[]{:S(2)}) %collective-permute-start.5) | collective-permute-done | bytes 69664 | tf_op jit(solution)/shard_map/ppermute | solution.py:291
  48.3 2.6 %collective-permute-start.18 = (bf16[64,1024]{1,0:T(8,128)(2,1)S(1)}, bf16[64,1024]{1,0:T(8,128)(2,1)S(1)}, u32[]{:S(2)}, u32[]{:S(2)}) collective-permute-start(bf16[64,1024]{1,0:T(8,128)(2,1)S(1)} %slice.9), channel_id=1, source_target_pairs={{0,224},{4,228},{8,232},{12,236},{16,240},{20,244},{24,248},{28,25... | collective-permute-start | bytes 393224 | tf_op jit(solution)/shard_map/ppermute | solution.py:291
  50.8 3.2 %collective-permute-start.7 = (f32[136,128]{1,0:T(8,128)S(1)}, f32[136,128]{1,0:T(8,128)S(1)}, u32[]{:S(2)}, u32[]{:S(2)}) collective-permute-start(f32[136,128]{1,0:T(8,128)S(1)} %get-tuple-element.53), channel_id=1, source_target_pairs={{0,192},{4,196},{8,200},{12,204},{16,208},{20,212},{24,216},{28,22... | collective-permute-start | bytes 208904 | tf_op jit(solution)/shard_map/ppermute | solution.py:394
  54.0 4.0 %collective-permute-start.8 = (f32[136,128]{1,0:T(8,128)S(1)}, f32[136,128]{1,0:T(8,128)S(1)}, u32[]{:S(2)}, u32[]{:S(2)}) collective-permute-start(f32[136,128]{1,0:T(8,128)S(1)} %get-tuple-element.53), channel_id=1, source_target_pairs={{0,128},{4,132},{8,136},{12,140},{16,144},{20,148},{24,152},{28,15... | collective-permute-start | bytes 208904 | tf_op jit(solution)/shard_map/ppermute | solution.py:394
  58.0 1.6 %collective-permute-start.9 = (f32[136,128]{1,0:T(8,128)S(1)}, f32[136,128]{1,0:T(8,128)S(1)}, u32[]{:S(2)}, u32[]{:S(2)}) collective-permute-start(f32[136,128]{1,0:T(8,128)S(1)} %get-tuple-element.53), channel_id=1, source_target_pairs={{0,64},{4,68},{8,72},{12,76},{16,80},{20,84},{24,88},{28,92},{32,9... | collective-permute-start | bytes 208904 | tf_op jit(solution)/shard_map/ppermute | solution.py:394
  59.9 1.6 %collective-permute-done.9.got1 = f32[136,128]{1,0:T(8,128)S(1)} collective-permute-done((f32[136,128]{1,0:T(8,128)S(1)}, f32[136,128]{1,0:T(8,128)S(1)}, u32[]{:S(2)}, u32[]{:S(2)}) %collective-permute-start.9) | collective-permute-done | bytes 69664 | tf_op jit(solution)/shard_map/ppermute | solution.py:394
  61.9 3.3 %shard_map.104.refs_0_ = bf16[256,1024]{1,0:T(8,128)(2,1)S(1)} custom-call(s32[1,4]{1,0:T(1,128)S(1)} %copy-done.7, s32[1,4]{1,0:T(1,128)S(1)} %copy-done.9, f32[136,128]{1,0:T(8,128)S(1)} %collective-permute-done.7.got3, f32[136,128]{1,0:T(8,128)S(1)} %collective-permute-done.8.got2, f32[136,128]{1,0:T(8,128)S(1)} %collective-permute-done.9.got1, ...), custom_call_target="tpu_custom_call" | custom-call | flops 20000000 | bytes 4000000 | tf_op jit(solution)/shard_map/pallas_call | solution.py:401
  67.4 1.5 %collective-permute-start.21 = (bf16[256,256]{1,0:T(8,128)(2,1)S(1)}, bf16[256,256]{1,0:T(8,128)(2,1)S(1)}, u32[]{:S(2)}, u32[]{:S(2)}) collective-permute-start(bf16[256,256]{1,0:T(8,128)(2,1)S(1)} %get-tuple-element.74.refs_4_), channel_id=1, source_target_pairs={{0,3},{1,0},{2,1},{3,2},{4,7},{5,4},{6,5},{7,6},{8,11},{9,8},{10,9... | collective-permute-start | bytes 393224 | tf_op jit(solution)/shard_map/ppermute | solution.py:314
  70.7 2.4 %collective-permute-start.25 = (bf16[256,256]{1,0:T(8,128)(2,1)S(1)}, bf16[256,256]{1,0:T(8,128)(2,1)S(1)}, u32[]{:S(2)}, u32[]{:S(2)}) collective-permute-start(bf16[256,256]{1,0:T(8,128)(2,1)S(1)} %get-tuple-element.76.refs_4_), channel_id=1, source_target_pairs={{0,1},{1,2},{2,3},{3,0},{4,5},{5,6},{6,7},{7,4},{8,9},{9,10},{10,1... | collective-permute-start | bytes 393224 | tf_op jit(solution)/shard_map/ppermute | solution.py:314
  74.6 5.0 %collective-permute-done.26.refs_0_ = bf16[256,1024]{1,0:T(8,128)(2,1)S(1)} collective-permute-done((bf16[256,1024]{1,0:T(8,128)(2,1)S(1)}, bf16[256,1024]{1,0:T(8,128)(2,1)S(1)}, u32[]{:S(2)}, u32[]{:S(2)}) %collective-permute-start.26) | collective-permute-done | bytes 524320 | tf_op jit(solution)/shard_map/ppermute | solution.py:291
  80.7 1.6 %collective-permute-start.28 = (bf16[256,256]{1,0:T(8,128)(2,1)S(1)}, bf16[256,256]{1,0:T(8,128)(2,1)S(1)}, u32[]{:S(2)}, u32[]{:S(2)}) collective-permute-start(bf16[256,256]{1,0:T(8,128)(2,1)S(1)} %get-tuple-element.87), channel_id=1, source_target_pairs={{0,3},{1,0},{2,1},{3,2},{4,7},{5,4},{6,5},{7,6},{8,11},{9,8},{10,9... | collective-permute-start | bytes 393224 | tf_op jit(solution)/shard_map/ppermute | solution.py:314
  82.2 1.7 %collective-permute-start.22 = (bf16[256,256]{1,0:T(8,128)(2,1)S(1)}, bf16[256,256]{1,0:T(8,128)(2,1)S(1)}, u32[]{:S(2)}, u32[]{:S(2)}) collective-permute-start(bf16[256,256]{1,0:T(8,128)(2,1)S(1)} %get-tuple-element.80.refs_3_), channel_id=1, source_target_pairs={{0,1},{1,2},{2,3},{3,0},{4,5},{5,6},{6,7},{7,4},{8,9},{9,10},{10,1... | collective-permute-start | bytes 393224 | tf_op jit(solution)/shard_map/ppermute | solution.py:314
  85.1 1.1 %collective-permute-start.31 = (bf16[256,256]{1,0:T(8,128)(2,1)S(1)}, bf16[256,256]{1,0:T(8,128)(2,1)S(1)}, u32[]{:S(2)}, u32[]{:S(2)}) collective-permute-start(bf16[256,256]{1,0:T(8,128)(2,1)S(1)} %get-tuple-element.91), channel_id=1, source_target_pairs={{0,3},{1,0},{2,1},{3,2},{4,7},{5,4},{6,5},{7,6},{8,11},{9,8},{10,9... | collective-permute-start | bytes 393224 | tf_op jit(solution)/shard_map/ppermute | solution.py:314
  86.6 2.0 %collective-permute-start.32 = (bf16[256,256]{1,0:T(8,128)(2,1)S(1)}, bf16[256,256]{1,0:T(8,128)(2,1)S(1)}, u32[]{:S(2)}, u32[]{:S(2)}) collective-permute-start(bf16[256,256]{1,0:T(8,128)(2,1)S(1)} %get-tuple-element.92), channel_id=1, source_target_pairs={{0,1},{1,2},{2,3},{3,0},{4,5},{5,6},{6,7},{7,4},{8,9},{9,10},{10,1... | collective-permute-start | bytes 393224 | tf_op jit(solution)/shard_map/ppermute | solution.py:314
  88.7 1.8 %collective-permute-start.29 = (bf16[256,256]{1,0:T(8,128)(2,1)S(1)}, bf16[256,256]{1,0:T(8,128)(2,1)S(1)}, u32[]{:S(2)}, u32[]{:S(2)}) collective-permute-start(bf16[256,256]{1,0:T(8,128)(2,1)S(1)} %get-tuple-element.89), channel_id=1, source_target_pairs={{0,1},{1,2},{2,3},{3,0},{4,5},{5,6},{6,7},{7,4},{8,9},{9,10},{10,1... | collective-permute-start | bytes 393224 | tf_op jit(solution)/shard_map/ppermute | solution.py:314
  91.6 1.2 %collective-permute-done.31.refs_4_ = bf16[256,256]{1,0:T(8,128)(2,1)S(1)} collective-permute-done((bf16[256,256]{1,0:T(8,128)(2,1)S(1)}, bf16[256,256]{1,0:T(8,128)(2,1)S(1)}, u32[]{:S(2)}, u32[]{:S(2)}) %collective-permute-start.31) | collective-permute-done | bytes 131104 | tf_op jit(solution)/shard_map/ppermute | solution.py:314
  93.8 2.9 %collective-permute-done.30.refs_3_ = bf16[256,256]{1,0:T(8,128)(2,1)S(1)} collective-permute-done((bf16[256,256]{1,0:T(8,128)(2,1)S(1)}, bf16[256,256]{1,0:T(8,128)(2,1)S(1)}, u32[]{:S(2)}, u32[]{:S(2)}) %collective-permute-start.30) | collective-permute-done | bytes 131104 | tf_op jit(solution)/shard_map/ppermute | solution.py:314
  96.8 1.1 %collective-permute-start.33 = (bf16[256,512]{1,0:T(8,128)(2,1)S(1)}, bf16[256,512]{1,0:T(8,128)(2,1)S(1)}, u32[]{:S(2)}, u32[]{:S(2)}) collective-permute-start(bf16[256,512]{1,0:T(8,128)(2,1)S(1)} %shard_map.114), channel_id=1, source_target_pairs={{0,8},{4,12},{8,0},{12,4},{16,24},{20,28},{24,16},{28,20},{32,40},... | collective-permute-start | bytes 786440 | tf_op jit(solution)/shard_map/ppermute | solution.py:291
  97.9 5.3 %collective-permute-done.33.refs_6_ = bf16[256,512]{1,0:T(8,128)(2,1)S(1)} collective-permute-done((bf16[256,512]{1,0:T(8,128)(2,1)S(1)}, bf16[256,512]{1,0:T(8,128)(2,1)S(1)}, u32[]{:S(2)}, u32[]{:S(2)}) %collective-permute-start.33) | collective-permute-done | bytes 262176 | tf_op jit(solution)/shard_map/ppermute | solution.py:291
  (83 shorter events, 17.1 us)
Async XLA Ops:
  1.8 7.0 %collective-permute-start.10 = (bf16[64,1024]{1,0:T(8,128)(2,1)}, bf16[64,1024]{1,0:T(8,128)(2,1)S(1)}, u32[]{:S(2)}, u32[]{:S(2)}) collective-permute-start(bf16[64,1024]{1,0:T(8,128)(2,1)} %get-tuple-element.57.shard_ref), channel_id=1, source_target_pairs={{0,16},{4,20},{8,24},{12,28},{16,0},{20,4},{24,8},{28,12},{32,48},... | collective-permute-start | bytes 393224 | tf_op jit(solution)/shard_map/ppermute | solution.py:291
  9.7 14.3 %collective-permute-start.11 = (bf16[128,1024]{1,0:T(8,128)(2,1)S(1)}, bf16[128,1024]{1,0:T(8,128)(2,1)S(1)}, u32[]{:S(2)}, u32[]{:S(2)}) collective-permute-start(bf16[128,1024]{1,0:T(8,128)(2,1)S(1)} %shard_map.105), channel_id=1, source_target_pairs={{0,32},{4,36},{8,40},{12,44},{16,48},{20,52},{24,56},{28,60},{32,6... | collective-permute-start | bytes 786440 | tf_op jit(solution)/shard_map/ppermute | solution.py:291
  15.5 8.5 %collective-permute-start.12 = (bf16[128,1024]{1,0:T(8,128)(2,1)S(1)}, bf16[128,1024]{1,0:T(8,128)(2,1)S(1)}, u32[]{:S(2)}, u32[]{:S(2)}) collective-permute-start(bf16[128,1024]{1,0:T(8,128)(2,1)S(1)} %shard_map.105), channel_id=1, source_target_pairs={{0,224},{4,228},{8,232},{12,236},{16,240},{20,244},{24,248},{28,25... | collective-permute-start | bytes 786440 | tf_op jit(solution)/shard_map/ppermute | solution.py:291
  24.0 9.1 %collective-permute-start.13 = (bf16[128,1024]{1,0:T(8,128)(2,1)S(1)}, bf16[128,1024]{1,0:T(8,128)(2,1)S(1)}, u32[]{:S(2)}, u32[]{:S(2)}) collective-permute-start(bf16[128,1024]{1,0:T(8,128)(2,1)S(1)} %collective-permute-done.11), channel_id=1, source_target_pairs={{0,32},{4,36},{8,40},{12,44},{16,48},{20,52},{24,56},{28,60},{32,6... | collective-permute-start | bytes 786440 | tf_op jit(solution)/shard_map/ppermute | solution.py:291
  24.0 9.1 %collective-permute-start.14 = (bf16[128,1024]{1,0:T(8,128)(2,1)S(1)}, bf16[128,1024]{1,0:T(8,128)(2,1)S(1)}, u32[]{:S(2)}, u32[]{:S(2)}) collective-permute-start(bf16[128,1024]{1,0:T(8,128)(2,1)S(1)} %collective-permute-done.12), channel_id=1, source_target_pairs={{0,224},{4,228},{8,232},{12,236},{16,240},{20,244},{24,248},{28,25... | collective-permute-start | bytes 786440 | tf_op jit(solution)/shard_map/ppermute | solution.py:291
  27.7 5.0 %collective-permute-start.2 = (f32[136,128]{1,0:T(8,128)S(1)}, f32[136,128]{1,0:T(8,128)S(1)}, u32[]{:S(2)}, u32[]{:S(2)}) collective-permute-start(f32[136,128]{1,0:T(8,128)S(1)} %get-tuple-element.50.own), channel_id=1, source_target_pairs={{0,8},{4,12},{8,0},{12,4},{16,24},{20,28},{24,16},{28,20},{32,40},... | collective-permute-start | bytes 208904 | tf_op jit(solution)/shard_map/ppermute | solution.py:291
  27.7 5.3 %collective-permute-start.3 = (f32[136,128]{1,0:T(8,128)S(1)}, f32[136,128]{1,0:T(8,128)S(1)}, u32[]{:S(2)}, u32[]{:S(2)}) collective-permute-start(f32[136,128]{1,0:T(8,128)S(1)} %get-tuple-element.50.own), channel_id=1, source_target_pairs={{0,4},{4,8},{8,12},{12,0},{16,20},{20,24},{24,28},{28,16},{32,36},... | collective-permute-start | bytes 208904 | tf_op jit(solution)/shard_map/ppermute | solution.py:291
  33.1 14.1 %collective-permute-start.15 = (bf16[128,1024]{1,0:T(8,128)(2,1)S(1)}, bf16[128,1024]{1,0:T(8,128)(2,1)S(1)}, u32[]{:S(2)}, u32[]{:S(2)}) collective-permute-start(bf16[128,1024]{1,0:T(8,128)(2,1)S(1)} %collective-permute-done.13), channel_id=1, source_target_pairs={{0,32},{4,36},{8,40},{12,44},{16,48},{20,52},{24,56},{28,60},{32,6... | collective-permute-start | bytes 786440 | tf_op jit(solution)/shard_map/ppermute | solution.py:291
  37.8 9.5 %collective-permute-start.16 = (bf16[128,1024]{1,0:T(8,128)(2,1)S(1)}, bf16[128,1024]{1,0:T(8,128)(2,1)S(1)}, u32[]{:S(2)}, u32[]{:S(2)}) collective-permute-start(bf16[128,1024]{1,0:T(8,128)(2,1)S(1)} %collective-permute-done.14), channel_id=1, source_target_pairs={{0,224},{4,228},{8,232},{12,236},{16,240},{20,244},{24,248},{28,25... | collective-permute-start | bytes 786440 | tf_op jit(solution)/shard_map/ppermute | solution.py:291
  37.8 6.1 %collective-permute-start.4 = (f32[136,128]{1,0:T(8,128)S(1)}, f32[136,128]{1,0:T(8,128)S(1)}, u32[]{:S(2)}, u32[]{:S(2)}) collective-permute-start(f32[136,128]{1,0:T(8,128)S(1)} %get-tuple-element.51.own), channel_id=1, source_target_pairs={{0,48},{4,52},{8,56},{12,60},{16,0},{20,4},{24,8},{28,12},{32,16},... | collective-permute-start | bytes 208904 | tf_op jit(solution)/shard_map/ppermute | solution.py:291
  37.8 9.4 %collective-permute-start.5 = (f32[136,128]{1,0:T(8,128)S(1)}, f32[136,128]{1,0:T(8,128)S(1)}, u32[]{:S(2)}, u32[]{:S(2)}) collective-permute-start(f32[136,128]{1,0:T(8,128)S(1)} %get-tuple-element.51.own), channel_id=1, source_target_pairs={{0,32},{4,36},{8,40},{12,44},{16,48},{20,52},{24,56},{28,60},{32,0... | collective-permute-start | bytes 208904 | tf_op jit(solution)/shard_map/ppermute | solution.py:291
  39.8 7.3 %collective-permute-start.6 = (f32[136,128]{1,0:T(8,128)S(1)}, f32[136,128]{1,0:T(8,128)S(1)}, u32[]{:S(2)}, u32[]{:S(2)}) collective-permute-start(f32[136,128]{1,0:T(8,128)S(1)} %get-tuple-element.51.own), channel_id=1, source_target_pairs={{0,16},{4,20},{8,24},{12,28},{16,32},{20,36},{24,40},{28,44},{32,4... | collective-permute-start | bytes 208904 | tf_op jit(solution)/shard_map/ppermute | solution.py:291
  47.3 14.2 %collective-permute-start.17 = (bf16[64,1024]{1,0:T(8,128)(2,1)S(1)}, bf16[64,1024]{1,0:T(8,128)(2,1)S(1)}, u32[]{:S(2)}, u32[]{:S(2)}) collective-permute-start(bf16[64,1024]{1,0:T(8,128)(2,1)S(1)} %slice.8), channel_id=1, source_target_pairs={{0,32},{4,36},{8,40},{12,44},{16,48},{20,52},{24,56},{28,60},{32,6... | collective-permute-start | bytes 393224 | tf_op jit(solution)/shard_map/ppermute | solution.py:291
  48.3 13.3 %collective-permute-start.18 = (bf16[64,1024]{1,0:T(8,128)(2,1)S(1)}, bf16[64,1024]{1,0:T(8,128)(2,1)S(1)}, u32[]{:S(2)}, u32[]{:S(2)}) collective-permute-start(bf16[64,1024]{1,0:T(8,128)(2,1)S(1)} %slice.9), channel_id=1, source_target_pairs={{0,224},{4,228},{8,232},{12,236},{16,240},{20,244},{24,248},{28,25... | collective-permute-start | bytes 393224 | tf_op jit(solution)/shard_map/ppermute | solution.py:291
  50.8 8.8 %collective-permute-start.7 = (f32[136,128]{1,0:T(8,128)S(1)}, f32[136,128]{1,0:T(8,128)S(1)}, u32[]{:S(2)}, u32[]{:S(2)}) collective-permute-start(f32[136,128]{1,0:T(8,128)S(1)} %get-tuple-element.53), channel_id=1, source_target_pairs={{0,192},{4,196},{8,200},{12,204},{16,208},{20,212},{24,216},{28,22... | collective-permute-start | bytes 208904 | tf_op jit(solution)/shard_map/ppermute | solution.py:394
  54.0 5.9 %collective-permute-start.8 = (f32[136,128]{1,0:T(8,128)S(1)}, f32[136,128]{1,0:T(8,128)S(1)}, u32[]{:S(2)}, u32[]{:S(2)}) collective-permute-start(f32[136,128]{1,0:T(8,128)S(1)} %get-tuple-element.53), channel_id=1, source_target_pairs={{0,128},{4,132},{8,136},{12,140},{16,144},{20,148},{24,152},{28,15... | collective-permute-start | bytes 208904 | tf_op jit(solution)/shard_map/ppermute | solution.py:394
  58.0 3.5 %collective-permute-start.9 = (f32[136,128]{1,0:T(8,128)S(1)}, f32[136,128]{1,0:T(8,128)S(1)}, u32[]{:S(2)}, u32[]{:S(2)}) collective-permute-start(f32[136,128]{1,0:T(8,128)S(1)} %get-tuple-element.53), channel_id=1, source_target_pairs={{0,64},{4,68},{8,72},{12,76},{16,80},{20,84},{24,88},{28,92},{32,9... | collective-permute-start | bytes 208904 | tf_op jit(solution)/shard_map/ppermute | solution.py:394
  61.7 4.5 %collective-permute-start.19 = (bf16[1024,1024]{1,0:T(8,128)(2,1)S(1)}, bf16[1024,1024]{1,0:T(8,128)(2,1)S(1)}, u32[]{:S(2)}, u32[]{:S(2)}) collective-permute-start(bf16[1024,1024]{1,0:T(8,128)(2,1)S(1)} %constant_dynamic-update-slice_fusion.refs_1_), channel_id=1, source_target_pairs={{0,4},{4,0},{8,12},{12,8},{16,20},{20,16},{24,28},{28,24},{32,36},... | collective-permute-start | bytes 6291464 | tf_op jit(solution)/shard_map/ppermute | solution.py:291
  65.2 14.4 %collective-permute-start.26 = (bf16[256,1024]{1,0:T(8,128)(2,1)S(1)}, bf16[256,1024]{1,0:T(8,128)(2,1)S(1)}, u32[]{:S(2)}, u32[]{:S(2)}) collective-permute-start(bf16[256,1024]{1,0:T(8,128)(2,1)S(1)} %shard_map.104.refs_0_), channel_id=1, source_target_pairs={{0,8},{4,12},{8,0},{12,4},{16,24},{20,28},{24,16},{28,20},{32,40},... | collective-permute-start | bytes 1572872 | tf_op jit(solution)/shard_map/ppermute | solution.py:291
  66.8 6.8 %collective-permute-start.20 = (bf16[256,256]{1,0:T(8,128)(2,1)S(1)}, bf16[256,256]{1,0:T(8,128)(2,1)S(1)}, u32[]{:S(2)}, u32[]{:S(2)}) collective-permute-start(bf16[256,256]{1,0:T(8,128)(2,1)S(1)} %get-tuple-element.73.refs_3_), channel_id=1, source_target_pairs={{0,1},{1,2},{2,3},{3,0},{4,5},{5,6},{6,7},{7,4},{8,9},{9,10},{10,1... | collective-permute-start | bytes 393224 | tf_op jit(solution)/shard_map/ppermute | solution.py:314
  67.4 7.1 %collective-permute-start.21 = (bf16[256,256]{1,0:T(8,128)(2,1)S(1)}, bf16[256,256]{1,0:T(8,128)(2,1)S(1)}, u32[]{:S(2)}, u32[]{:S(2)}) collective-permute-start(bf16[256,256]{1,0:T(8,128)(2,1)S(1)} %get-tuple-element.74.refs_4_), channel_id=1, source_target_pairs={{0,3},{1,0},{2,1},{3,2},{4,7},{5,4},{6,5},{7,6},{8,11},{9,8},{10,9... | collective-permute-start | bytes 393224 | tf_op jit(solution)/shard_map/ppermute | solution.py:314
  69.8 14.1 %collective-permute-start.24 = (bf16[256,256]{1,0:T(8,128)(2,1)S(1)}, bf16[256,256]{1,0:T(8,128)(2,1)S(1)}, u32[]{:S(2)}, u32[]{:S(2)}) collective-permute-start(bf16[256,256]{1,0:T(8,128)(2,1)S(1)} %get-tuple-element.82), channel_id=1, source_target_pairs={{0,3},{1,0},{2,1},{3,2},{4,7},{5,4},{6,5},{7,6},{8,11},{9,8},{10,9... | collective-permute-start | bytes 393224 | tf_op jit(solution)/shard_map/ppermute | solution.py:314
  70.7 13.6 %collective-permute-start.25 = (bf16[256,256]{1,0:T(8,128)(2,1)S(1)}, bf16[256,256]{1,0:T(8,128)(2,1)S(1)}, u32[]{:S(2)}, u32[]{:S(2)}) collective-permute-start(bf16[256,256]{1,0:T(8,128)(2,1)S(1)} %get-tuple-element.76.refs_4_), channel_id=1, source_target_pairs={{0,1},{1,2},{2,3},{3,0},{4,5},{5,6},{6,7},{7,4},{8,9},{9,10},{10,1... | collective-permute-start | bytes 393224 | tf_op jit(solution)/shard_map/ppermute | solution.py:314
  80.1 6.5 %collective-permute-start.27 = (bf16[256,256]{1,0:T(8,128)(2,1)S(1)}, bf16[256,256]{1,0:T(8,128)(2,1)S(1)}, u32[]{:S(2)}, u32[]{:S(2)}) collective-permute-start(bf16[256,256]{1,0:T(8,128)(2,1)S(1)} %get-tuple-element.85), channel_id=1, source_target_pairs={{0,1},{1,2},{2,3},{3,0},{4,5},{5,6},{6,7},{7,4},{8,9},{9,10},{10,1... | collective-permute-start | bytes 393224 | tf_op jit(solution)/shard_map/ppermute | solution.py:314
  80.7 8.0 %collective-permute-start.28 = (bf16[256,256]{1,0:T(8,128)(2,1)S(1)}, bf16[256,256]{1,0:T(8,128)(2,1)S(1)}, u32[]{:S(2)}, u32[]{:S(2)}) collective-permute-start(bf16[256,256]{1,0:T(8,128)(2,1)S(1)} %get-tuple-element.87), channel_id=1, source_target_pairs={{0,3},{1,0},{2,1},{3,2},{4,7},{5,4},{6,5},{7,6},{8,11},{9,8},{10,9... | collective-permute-start | bytes 393224 | tf_op jit(solution)/shard_map/ppermute | solution.py:314
  82.2 8.3 %collective-permute-start.22 = (bf16[256,256]{1,0:T(8,128)(2,1)S(1)}, bf16[256,256]{1,0:T(8,128)(2,1)S(1)}, u32[]{:S(2)}, u32[]{:S(2)}) collective-permute-start(bf16[256,256]{1,0:T(8,128)(2,1)S(1)} %get-tuple-element.80.refs_3_), channel_id=1, source_target_pairs={{0,1},{1,2},{2,3},{3,0},{4,5},{5,6},{6,7},{7,4},{8,9},{9,10},{10,1... | collective-permute-start | bytes 393224 | tf_op jit(solution)/shard_map/ppermute | solution.py:314
  83.9 7.2 %collective-permute-start.23 = (bf16[256,256]{1,0:T(8,128)(2,1)S(1)}, bf16[256,256]{1,0:T(8,128)(2,1)S(1)}, u32[]{:S(2)}, u32[]{:S(2)}) collective-permute-start(bf16[256,256]{1,0:T(8,128)(2,1)S(1)} %get-tuple-element.81), channel_id=1, source_target_pairs={{0,3},{1,0},{2,1},{3,2},{4,7},{5,4},{6,5},{7,6},{8,11},{9,8},{10,9... | collective-permute-start | bytes 393224 | tf_op jit(solution)/shard_map/ppermute | solution.py:314
  85.1 7.7 %collective-permute-start.31 = (bf16[256,256]{1,0:T(8,128)(2,1)S(1)}, bf16[256,256]{1,0:T(8,128)(2,1)S(1)}, u32[]{:S(2)}, u32[]{:S(2)}) collective-permute-start(bf16[256,256]{1,0:T(8,128)(2,1)S(1)} %get-tuple-element.91), channel_id=1, source_target_pairs={{0,3},{1,0},{2,1},{3,2},{4,7},{5,4},{6,5},{7,6},{8,11},{9,8},{10,9... | collective-permute-start | bytes 393224 | tf_op jit(solution)/shard_map/ppermute | solution.py:314
  86.6 6.2 %collective-permute-start.32 = (bf16[256,256]{1,0:T(8,128)(2,1)S(1)}, bf16[256,256]{1,0:T(8,128)(2,1)S(1)}, u32[]{:S(2)}, u32[]{:S(2)}) collective-permute-start(bf16[256,256]{1,0:T(8,128)(2,1)S(1)} %get-tuple-element.92), channel_id=1, source_target_pairs={{0,1},{1,2},{2,3},{3,0},{4,5},{5,6},{6,7},{7,4},{8,9},{9,10},{10,1... | collective-permute-start | bytes 393224 | tf_op jit(solution)/shard_map/ppermute | solution.py:314
  88.7 5.0 %collective-permute-start.29 = (bf16[256,256]{1,0:T(8,128)(2,1)S(1)}, bf16[256,256]{1,0:T(8,128)(2,1)S(1)}, u32[]{:S(2)}, u32[]{:S(2)}) collective-permute-start(bf16[256,256]{1,0:T(8,128)(2,1)S(1)} %get-tuple-element.89), channel_id=1, source_target_pairs={{0,1},{1,2},{2,3},{3,0},{4,5},{5,6},{6,7},{7,4},{8,9},{9,10},{10,1... | collective-permute-start | bytes 393224 | tf_op jit(solution)/shard_map/ppermute | solution.py:314
  90.5 6.2 %collective-permute-start.30 = (bf16[256,256]{1,0:T(8,128)(2,1)S(1)}, bf16[256,256]{1,0:T(8,128)(2,1)S(1)}, u32[]{:S(2)}, u32[]{:S(2)}) collective-permute-start(bf16[256,256]{1,0:T(8,128)(2,1)S(1)} %get-tuple-element.90), channel_id=1, source_target_pairs={{0,3},{1,0},{2,1},{3,2},{4,7},{5,4},{6,5},{7,6},{8,11},{9,8},{10,9... | collective-permute-start | bytes 393224 | tf_op jit(solution)/shard_map/ppermute | solution.py:314
  96.8 6.5 %collective-permute-start.33 = (bf16[256,512]{1,0:T(8,128)(2,1)S(1)}, bf16[256,512]{1,0:T(8,128)(2,1)S(1)}, u32[]{:S(2)}, u32[]{:S(2)}) collective-permute-start(bf16[256,512]{1,0:T(8,128)(2,1)S(1)} %shard_map.114), channel_id=1, source_target_pairs={{0,8},{4,12},{8,0},{12,4},{16,24},{20,28},{24,16},{28,20},{32,40},... | collective-permute-start | bytes 786440 | tf_op jit(solution)/shard_map/ppermute | solution.py:291
  (12 other events, 171.3 us)

commit v3 on v2

--- a/solution.py
+++ b/solution.py
@@ -386,16 +386,17 @@
     two_messages = (f32(STATE + GROUPS, LANES), f32(STATE + GROUPS, LANES))
     low, following = call(low_kernel, two_messages, [WHOLE] * 5, scratch=[pole_scratch])(
         message, *digit_moves(message, 1), decay_rate)
-    relay(message)
+    middle_moves = digit_moves(following, 4)
+    relay(following)
+    opposite = [along_z(after(right[1][:SHARD], following), 2), along_z(after(left[1][SHARD:], following), 6)]
     relay(following)
     before, final = call(middle_kernel, two_messages, [WHOLE] * 6, scratch=[pole_scratch])(
-        following, *digit_moves(following, 4), low, decay_rate)
+        following, *middle_moves, low, decay_rate)
     high = [
         lax.ppermute(final, "seq", [(i, i + k * 16) for i in range(count - k * 16)])
         for k in (3, 2, 1)
     ]
-    ahead, behind = after((right[-1][:SHARD], left[-1][SHARD:]), final)
-    parts = [column] + right + [along_z(ahead, 1), along_z(behind, 7)] + left[::-1]
+    parts = [column] + right + opposite + left[::-1]
     gathered = jnp.concatenate(after(parts, high), axis=0)
     other = across(gathered)
     mixed = call(

time: 104 us -> 104 us (level)
  the two profiles are of different devices: /device:TPU:6 before, /device:TPU:166 now
where the time goes in v3:
time: 104 us
  starting transfers between devices  45.4 us (44%)
  waiting for transfers between devices  42.5 us (41%)
  Pallas kernels  14.1 us (14%)
  local copies, waits for them, and re-layouts  1.12 us (1%)
    ppermute x18, starting transfers between devices, move(): return lax.ppermute(block, 'seq', [(i, target(i)) for i in range(count)])  24.8 us
    ppermute x18, waiting for transfers between devices, move(): return lax.ppermute(block, 'seq', [(i, target(i)) for i in range(count)])  17.3 us
    ppermute x12, starting transfers between devices, around(): return lax.ppermute(block, 'ch', [(i, (i + gap) % 4) for i in range(4)])  14.8 us
    ppermute x3, waiting for transfers between devices, local(): lax.ppermute(final, 'seq', [(i, i + k * 16) for i in range(count - k * 16)])  13.1 us
    ppermute x12, waiting for transfers between devices, around(): return lax.ppermute(block, 'ch', [(i, (i + gap) % 4) for i in range(4)])  6.53 us
    ppermute x1, waiting for transfers between devices, local(): halo = lax.ppermute(tails, 'seq', [(i, i + 1) for i in range(count - 1)])  5.63 us
    ppermute x3, starting transfers between devices, local(): lax.ppermute(final, 'seq', [(i, i + k * 16) for i in range(count - k * 16)])  3.87 us
    pallas_call x6, Pallas kernels, project(): pl.pallas_call(lambda *refs: project_kernel(turns, *refs), out_shape=(b16...  3.87 us
  transfers between devices with their start and end apart: 34, of which 17 were waited for; matrix products, arithmetic and copies ran while one was open for 0% of the time, Pallas kernels for 11%

profile of v3, /device:TPU:166, one launch (start us, length us, event | category | flops | bytes accessed | tf_op | source)
XLA Modules:
  0.0 103.6 jit_solution(16856183916862416983)
XLA Ops:
  0.0 1.7 %shard_map.100 = (f32[8,1024]{1,0:T(8,128)}, bf16[64,1024]{1,0:T(8,128)(2,1)}) custom-call(s32[1,4]{1,0:T(1,128)} %starts_ref.5, bf16[256,1024]{1,0:T(8,128)(2,1)} %q_hbm.1, bf16[256,1024]{1,0:T(8,128)(2,1)} %k_hbm.1, bf16[256,1024]{1,0:T(8,128)(2,1)} %v_hbm.1, bf16[64,1024]{1,0:T(8,128)(2,1)} %shard_ref.1), custom_call_target="tpu_custom_call" | custom-call | tf_op jit(solution)/shard_map/pallas_call | solution.py:353
  1.8 3.2 %collective-permute-start.10 = (bf16[64,1024]{1,0:T(8,128)(2,1)}, bf16[64,1024]{1,0:T(8,128)(2,1)S(1)}, u32[]{:S(2)}, u32[]{:S(2)}) collective-permute-start(bf16[64,1024]{1,0:T(8,128)(2,1)} %get-tuple-element.57.shard_ref), channel_id=1, source_target_pairs={{0,16},{4,20},{8,24},{12,28},{16,0},{20,4},{24,8},{28,12},{32,48},... | collective-permute-start | bytes 393224 | tf_op jit(solution)/shard_map/ppermute | solution.py:291
  5.0 1.9 %collective-permute-start = (f32[8,1024]{1,0:T(8,128)}, f32[8,1024]{1,0:T(8,128)S(1)}, u32[]{:S(2)}, u32[]{:S(2)}) collective-permute-start(f32[8,1024]{1,0:T(8,128)} %get-tuple-element.49), channel_id=1, source_target_pairs={{0,4},{4,8},{8,12},{12,16},{16,20},{20,24},{24,28},{28,32},{32,36}... | collective-permute-start | bytes 98312 | tf_op jit(solution)/shard_map/ppermute | solution.py:360
  6.9 5.6 %collective-permute-done.halo_ref = f32[8,1024]{1,0:T(8,128)S(1)} collective-permute-done((f32[8,1024]{1,0:T(8,128)}, f32[8,1024]{1,0:T(8,128)S(1)}, u32[]{:S(2)}, u32[]{:S(2)}) %collective-permute-start) | collective-permute-done | bytes 32800 | tf_op jit(solution)/shard_map/ppermute | solution.py:360
  13.5 1.1 %collective-permute-start.11 = (bf16[128,1024]{1,0:T(8,128)(2,1)S(1)}, bf16[128,1024]{1,0:T(8,128)(2,1)S(1)}, u32[]{:S(2)}, u32[]{:S(2)}) collective-permute-start(bf16[128,1024]{1,0:T(8,128)(2,1)S(1)} %shard_map.105), channel_id=1, source_target_pairs={{0,32},{4,36},{8,40},{12,44},{16,48},{20,52},{24,56},{28,60},{32,6... | collective-permute-start | bytes 786440 | tf_op jit(solution)/shard_map/ppermute | solution.py:291
  14.6 1.3 %collective-permute-start.12 = (bf16[128,1024]{1,0:T(8,128)(2,1)S(1)}, bf16[128,1024]{1,0:T(8,128)(2,1)S(1)}, u32[]{:S(2)}, u32[]{:S(2)}) collective-permute-start(bf16[128,1024]{1,0:T(8,128)(2,1)S(1)} %shard_map.105), channel_id=1, source_target_pairs={{0,224},{4,228},{8,232},{12,236},{16,240},{20,244},{24,248},{28,25... | collective-permute-start | bytes 786440 | tf_op jit(solution)/shard_map/ppermute | solution.py:291
  15.9 3.8 %shard_map.101 = (f32[2048,128]{1,0:T(8,128)S(1)}, f32[2048,128]{1,0:T(8,128)S(1)}, f32[136,128]{1,0:T(8,128)S(1)}) custom-call(s32[1,4]{1,0:T(1,128)S(1)} %copy-done.7, s32[1,4]{1,0:T(1,128)S(1)} %copy-done.9, bf16[256,1024]{1,0:T(8,128)(2,1)S(1)} %copy-done, bf16[256,1024]{1,0:T(8,128)(2,1)S(1)} %copy-done.1, bf16[256,1024]{1,0:T(8,128)(2,1)S(1)} %copy-done.2, ...), custom_call_target="tpu_custom_call" | custom-call | flops 20000000 | bytes 4000000 | tf_op jit(solution)/shard_map/pallas_call | solution.py:371
  20.3 1.9 %collective-permute-done.1.got3 = f32[136,128]{1,0:T(8,128)S(1)} collective-permute-done((f32[136,128]{1,0:T(8,128)S(1)}, f32[136,128]{1,0:T(8,128)S(1)}, u32[]{:S(2)}, u32[]{:S(2)}) %collective-permute-start.1) | collective-permute-done | bytes 69664 | tf_op jit(solution)/shard_map/ppermute | solution.py:291
  22.2 2.7 %collective-permute-done.2.got2 = f32[136,128]{1,0:T(8,128)S(1)} collective-permute-done((f32[136,128]{1,0:T(8,128)S(1)}, f32[136,128]{1,0:T(8,128)S(1)}, u32[]{:S(2)}, u32[]{:S(2)}) %collective-permute-start.2) | collective-permute-done | bytes 69664 | tf_op jit(solution)/shard_map/ppermute | solution.py:291
  25.4 3.2 %collective-permute-start.14 = (bf16[128,1024]{1,0:T(8,128)(2,1)S(1)}, bf16[128,1024]{1,0:T(8,128)(2,1)S(1)}, u32[]{:S(2)}, u32[]{:S(2)}) collective-permute-start(bf16[128,1024]{1,0:T(8,128)(2,1)S(1)} %collective-permute-done.12), channel_id=1, source_target_pairs={{0,224},{4,228},{8,232},{12,236},{16,240},{20,244},{24,248},{28,25... | collective-permute-start | bytes 786440 | tf_op jit(solution)/shard_map/ppermute | solution.py:291
  28.6 1.2 %collective-permute-start.4 = (f32[136,128]{1,0:T(8,128)S(1)}, f32[136,128]{1,0:T(8,128)S(1)}, u32[]{:S(2)}, u32[]{:S(2)}) collective-permute-start(f32[136,128]{1,0:T(8,128)S(1)} %get-tuple-element.51.own), channel_id=1, source_target_pairs={{0,48},{4,52},{8,56},{12,60},{16,0},{20,4},{24,8},{28,12},{32,16},... | collective-permute-start | bytes 208904 | tf_op jit(solution)/shard_map/ppermute | solution.py:291
  29.8 1.9 %collective-permute-start.5 = (f32[136,128]{1,0:T(8,128)S(1)}, f32[136,128]{1,0:T(8,128)S(1)}, u32[]{:S(2)}, u32[]{:S(2)}) collective-permute-start(f32[136,128]{1,0:T(8,128)S(1)} %get-tuple-element.51.own), channel_id=1, source_target_pairs={{0,32},{4,36},{8,40},{12,44},{16,48},{20,52},{24,56},{28,60},{32,0... | collective-permute-start | bytes 208904 | tf_op jit(solution)/shard_map/ppermute | solution.py:291
  31.7 3.5 %collective-permute-start.6 = (f32[136,128]{1,0:T(8,128)S(1)}, f32[136,128]{1,0:T(8,128)S(1)}, u32[]{:S(2)}, u32[]{:S(2)}) collective-permute-start(f32[136,128]{1,0:T(8,128)S(1)} %get-tuple-element.51.own), channel_id=1, source_target_pairs={{0,16},{4,20},{8,24},{12,28},{16,32},{20,36},{24,40},{28,44},{32,4... | collective-permute-start | bytes 208904 | tf_op jit(solution)/shard_map/ppermute | solution.py:291
  35.4 2.0 %collective-permute-start.18 = (bf16[128,1024]{1,0:T(8,128)(2,1)S(1)}, bf16[128,1024]{1,0:T(8,128)(2,1)S(1)}, u32[]{:S(2)}, u32[]{:S(2)}) collective-permute-start(bf16[128,1024]{1,0:T(8,128)(2,1)S(1)} %collective-permute-done.14), channel_id=1, source_target_pairs={{0,224},{4,228},{8,232},{12,236},{16,240},{20,244},{24,248},{28,25... | collective-permute-start | bytes 786440 | tf_op jit(solution)/shard_map/ppermute | solution.py:291
  38.0 1.3 %collective-permute-done.6.got1 = f32[136,128]{1,0:T(8,128)S(1)} collective-permute-done((f32[136,128]{1,0:T(8,128)S(1)}, f32[136,128]{1,0:T(8,128)S(1)}, u32[]{:S(2)}, u32[]{:S(2)}) %collective-permute-start.6) | collective-permute-done | bytes 69664 | tf_op jit(solution)/shard_map/ppermute | solution.py:291
  40.1 1.3 %collective-permute-start.8 = (f32[136,128]{1,0:T(8,128)S(1)}, f32[136,128]{1,0:T(8,128)S(1)}, u32[]{:S(2)}, u32[]{:S(2)}) collective-permute-start(f32[136,128]{1,0:T(8,128)S(1)} %get-tuple-element.53), channel_id=1, source_target_pairs={{0,128},{4,132},{8,136},{12,140},{16,144},{20,148},{24,152},{28,15... | collective-permute-start | bytes 208904 | tf_op jit(solution)/shard_map/ppermute | solution.py:396
  41.7 4.2 %collective-permute-start.17 = (bf16[64,1024]{1,0:T(8,128)(2,1)S(1)}, bf16[64,1024]{1,0:T(8,128)(2,1)S(1)}, u32[]{:S(2)}, u32[]{:S(2)}) collective-permute-start(bf16[64,1024]{1,0:T(8,128)(2,1)S(1)} %slice.9), channel_id=1, source_target_pairs={{0,192},{4,196},{8,200},{12,204},{16,208},{20,212},{24,216},{28,22... | collective-permute-start | bytes 393224 | tf_op jit(solution)/shard_map/ppermute | solution.py:291
  45.9 6.3 %collective-permute-done.8.got2 = f32[136,128]{1,0:T(8,128)S(1)} collective-permute-done((f32[136,128]{1,0:T(8,128)S(1)}, f32[136,128]{1,0:T(8,128)S(1)}, u32[]{:S(2)}, u32[]{:S(2)}) %collective-permute-start.8) | collective-permute-done | bytes 69664 | tf_op jit(solution)/shard_map/ppermute | solution.py:396
  52.2 1.9 %collective-permute-start.9 = (f32[136,128]{1,0:T(8,128)S(1)}, f32[136,128]{1,0:T(8,128)S(1)}, u32[]{:S(2)}, u32[]{:S(2)}) collective-permute-start(f32[136,128]{1,0:T(8,128)S(1)} %get-tuple-element.53), channel_id=1, source_target_pairs={{0,64},{4,68},{8,72},{12,76},{16,80},{20,84},{24,88},{28,92},{32,9... | collective-permute-start | bytes 208904 | tf_op jit(solution)/shard_map/ppermute | solution.py:396
  54.1 6.8 %collective-permute-done.9.got1 = f32[136,128]{1,0:T(8,128)S(1)} collective-permute-done((f32[136,128]{1,0:T(8,128)S(1)}, f32[136,128]{1,0:T(8,128)S(1)}, u32[]{:S(2)}, u32[]{:S(2)}) %collective-permute-start.9) | collective-permute-done | bytes 69664 | tf_op jit(solution)/shard_map/ppermute | solution.py:396
  61.3 3.3 %shard_map.104.refs_0_ = bf16[256,1024]{1,0:T(8,128)(2,1)S(1)} custom-call(s32[1,4]{1,0:T(1,128)S(1)} %copy-done.7, s32[1,4]{1,0:T(1,128)S(1)} %copy-done.9, f32[136,128]{1,0:T(8,128)S(1)} %collective-permute-done.7.got3, f32[136,128]{1,0:T(8,128)S(1)} %collective-permute-done.8.got2, f32[136,128]{1,0:T(8,128)S(1)} %collective-permute-done.9.got1, ...), custom_call_target="tpu_custom_call" | custom-call | flops 20000000 | bytes 4000000 | tf_op jit(solution)/shard_map/pallas_call | solution.py:402
  66.8 1.5 %collective-permute-start.21 = (bf16[256,256]{1,0:T(8,128)(2,1)S(1)}, bf16[256,256]{1,0:T(8,128)(2,1)S(1)}, u32[]{:S(2)}, u32[]{:S(2)}) collective-permute-start(bf16[256,256]{1,0:T(8,128)(2,1)S(1)} %get-tuple-element.74.refs_4_), channel_id=1, source_target_pairs={{0,3},{1,0},{2,1},{3,2},{4,7},{5,4},{6,5},{7,6},{8,11},{9,8},{10,9... | collective-permute-start | bytes 393224 | tf_op jit(solution)/shard_map/ppermute | solution.py:314
  70.1 2.4 %collective-permute-start.25 = (bf16[256,256]{1,0:T(8,128)(2,1)S(1)}, bf16[256,256]{1,0:T(8,128)(2,1)S(1)}, u32[]{:S(2)}, u32[]{:S(2)}) collective-permute-start(bf16[256,256]{1,0:T(8,128)(2,1)S(1)} %get-tuple-element.76.refs_4_), channel_id=1, source_target_pairs={{0,1},{1,2},{2,3},{3,0},{4,5},{5,6},{6,7},{7,4},{8,9},{9,10},{10,1... | collective-permute-start | bytes 393224 | tf_op jit(solution)/shard_map/ppermute | solution.py:314
  74.0 5.0 %collective-permute-done.26.refs_0_ = bf16[256,1024]{1,0:T(8,128)(2,1)S(1)} collective-permute-done((bf16[256,1024]{1,0:T(8,128)(2,1)S(1)}, bf16[256,1024]{1,0:T(8,128)(2,1)S(1)}, u32[]{:S(2)}, u32[]{:S(2)}) %collective-permute-start.26) | collective-permute-done | bytes 524320 | tf_op jit(solution)/shard_map/ppermute | solution.py:291
  80.1 1.5 %collective-permute-start.28 = (bf16[256,256]{1,0:T(8,128)(2,1)S(1)}, bf16[256,256]{1,0:T(8,128)(2,1)S(1)}, u32[]{:S(2)}, u32[]{:S(2)}) collective-permute-start(bf16[256,256]{1,0:T(8,128)(2,1)S(1)} %get-tuple-element.87), channel_id=1, source_target_pairs={{0,3},{1,0},{2,1},{3,2},{4,7},{5,4},{6,5},{7,6},{8,11},{9,8},{10,9... | collective-permute-start | bytes 393224 | tf_op jit(solution)/shard_map/ppermute | solution.py:314
  81.6 1.7 %collective-permute-start.22 = (bf16[256,256]{1,0:T(8,128)(2,1)S(1)}, bf16[256,256]{1,0:T(8,128)(2,1)S(1)}, u32[]{:S(2)}, u32[]{:S(2)}) collective-permute-start(bf16[256,256]{1,0:T(8,128)(2,1)S(1)} %get-tuple-element.80.refs_3_), channel_id=1, source_target_pairs={{0,1},{1,2},{2,3},{3,0},{4,5},{5,6},{6,7},{7,4},{8,9},{9,10},{10,1... | collective-permute-start | bytes 393224 | tf_op jit(solution)/shard_map/ppermute | solution.py:314
  84.5 1.1 %collective-permute-start.31 = (bf16[256,256]{1,0:T(8,128)(2,1)S(1)}, bf16[256,256]{1,0:T(8,128)(2,1)S(1)}, u32[]{:S(2)}, u32[]{:S(2)}) collective-permute-start(bf16[256,256]{1,0:T(8,128)(2,1)S(1)} %get-tuple-element.91), channel_id=1, source_target_pairs={{0,3},{1,0},{2,1},{3,2},{4,7},{5,4},{6,5},{7,6},{8,11},{9,8},{10,9... | collective-permute-start | bytes 393224 | tf_op jit(solution)/shard_map/ppermute | solution.py:314
  86.0 2.0 %collective-permute-start.32 = (bf16[256,256]{1,0:T(8,128)(2,1)S(1)}, bf16[256,256]{1,0:T(8,128)(2,1)S(1)}, u32[]{:S(2)}, u32[]{:S(2)}) collective-permute-start(bf16[256,256]{1,0:T(8,128)(2,1)S(1)} %get-tuple-element.92), channel_id=1, source_target_pairs={{0,1},{1,2},{2,3},{3,0},{4,5},{5,6},{6,7},{7,4},{8,9},{9,10},{10,1... | collective-permute-start | bytes 393224 | tf_op jit(solution)/shard_map/ppermute | solution.py:314
  88.1 1.8 %collective-permute-start.29 = (bf16[256,256]{1,0:T(8,128)(2,1)S(1)}, bf16[256,256]{1,0:T(8,128)(2,1)S(1)}, u32[]{:S(2)}, u32[]{:S(2)}) collective-permute-start(bf16[256,256]{1,0:T(8,128)(2,1)S(1)} %get-tuple-element.89), channel_id=1, source_target_pairs={{0,1},{1,2},{2,3},{3,0},{4,5},{5,6},{6,7},{7,4},{8,9},{9,10},{10,1... | collective-permute-start | bytes 393224 | tf_op jit(solution)/shard_map/ppermute | solution.py:314
  91.0 1.2 %collective-permute-done.31.refs_4_ = bf16[256,256]{1,0:T(8,128)(2,1)S(1)} collective-permute-done((bf16[256,256]{1,0:T(8,128)(2,1)S(1)}, bf16[256,256]{1,0:T(8,128)(2,1)S(1)}, u32[]{:S(2)}, u32[]{:S(2)}) %collective-permute-start.31) | collective-permute-done | bytes 131104 | tf_op jit(solution)/shard_map/ppermute | solution.py:314
  93.2 2.9 %collective-permute-done.30.refs_3_ = bf16[256,256]{1,0:T(8,128)(2,1)S(1)} collective-permute-done((bf16[256,256]{1,0:T(8,128)(2,1)S(1)}, bf16[256,256]{1,0:T(8,128)(2,1)S(1)}, u32[]{:S(2)}, u32[]{:S(2)}) %collective-permute-start.30) | collective-permute-done | bytes 131104 | tf_op jit(solution)/shard_map/ppermute | solution.py:314
  97.2 5.4 %collective-permute-done.33.refs_6_ = bf16[256,512]{1,0:T(8,128)(2,1)S(1)} collective-permute-done((bf16[256,512]{1,0:T(8,128)(2,1)S(1)}, bf16[256,512]{1,0:T(8,128)(2,1)S(1)}, u32[]{:S(2)}, u32[]{:S(2)}) %collective-permute-start.33) | collective-permute-done | bytes 262176 | tf_op jit(solution)/shard_map/ppermute | solution.py:291
  (83 shorter events, 16.3 us)
Async XLA Ops:
  1.8 10.7 %collective-permute-start.10 = (bf16[64,1024]{1,0:T(8,128)(2,1)}, bf16[64,1024]{1,0:T(8,128)(2,1)S(1)}, u32[]{:S(2)}, u32[]{:S(2)}) collective-permute-start(bf16[64,1024]{1,0:T(8,128)(2,1)} %get-tuple-element.57.shard_ref), channel_id=1, source_target_pairs={{0,16},{4,20},{8,24},{12,28},{16,0},{20,4},{24,8},{28,12},{32,48},... | collective-permute-start | bytes 393224 | tf_op jit(solution)/shard_map/ppermute | solution.py:291
  5.0 7.5 %collective-permute-start = (f32[8,1024]{1,0:T(8,128)}, f32[8,1024]{1,0:T(8,128)S(1)}, u32[]{:S(2)}, u32[]{:S(2)}) collective-permute-start(f32[8,1024]{1,0:T(8,128)} %get-tuple-element.49), channel_id=1, source_target_pairs={{0,4},{4,8},{8,12},{12,16},{16,20},{20,24},{24,28},{28,32},{32,36}... | collective-permute-start | bytes 98312 | tf_op jit(solution)/shard_map/ppermute | solution.py:360
  13.5 11.8 %collective-permute-start.11 = (bf16[128,1024]{1,0:T(8,128)(2,1)S(1)}, bf16[128,1024]{1,0:T(8,128)(2,1)S(1)}, u32[]{:S(2)}, u32[]{:S(2)}) collective-permute-start(bf16[128,1024]{1,0:T(8,128)(2,1)S(1)} %shard_map.105), channel_id=1, source_target_pairs={{0,32},{4,36},{8,40},{12,44},{16,48},{20,52},{24,56},{28,60},{32,6... | collective-permute-start | bytes 786440 | tf_op jit(solution)/shard_map/ppermute | solution.py:291
  14.6 10.7 %collective-permute-start.12 = (bf16[128,1024]{1,0:T(8,128)(2,1)S(1)}, bf16[128,1024]{1,0:T(8,128)(2,1)S(1)}, u32[]{:S(2)}, u32[]{:S(2)}) collective-permute-start(bf16[128,1024]{1,0:T(8,128)(2,1)S(1)} %shard_map.105), channel_id=1, source_target_pairs={{0,224},{4,228},{8,232},{12,236},{16,240},{20,244},{24,248},{28,25... | collective-permute-start | bytes 786440 | tf_op jit(solution)/shard_map/ppermute | solution.py:291
  19.8 5.1 %collective-permute-start.2 = (f32[136,128]{1,0:T(8,128)S(1)}, f32[136,128]{1,0:T(8,128)S(1)}, u32[]{:S(2)}, u32[]{:S(2)}) collective-permute-start(f32[136,128]{1,0:T(8,128)S(1)} %get-tuple-element.50.own), channel_id=1, source_target_pairs={{0,8},{4,12},{8,0},{12,4},{16,24},{20,28},{24,16},{28,20},{32,40},... | collective-permute-start | bytes 208904 | tf_op jit(solution)/shard_map/ppermute | solution.py:291
  19.9 5.2 %collective-permute-start.3 = (f32[136,128]{1,0:T(8,128)S(1)}, f32[136,128]{1,0:T(8,128)S(1)}, u32[]{:S(2)}, u32[]{:S(2)}) collective-permute-start(f32[136,128]{1,0:T(8,128)S(1)} %get-tuple-element.50.own), channel_id=1, source_target_pairs={{0,4},{4,8},{8,12},{12,0},{16,20},{20,24},{24,28},{28,16},{32,36},... | collective-permute-start | bytes 208904 | tf_op jit(solution)/shard_map/ppermute | solution.py:291
  25.3 10.1 %collective-permute-start.13 = (bf16[128,1024]{1,0:T(8,128)(2,1)S(1)}, bf16[128,1024]{1,0:T(8,128)(2,1)S(1)}, u32[]{:S(2)}, u32[]{:S(2)}) collective-permute-start(bf16[128,1024]{1,0:T(8,128)(2,1)S(1)} %collective-permute-done.11), channel_id=1, source_target_pairs={{0,32},{4,36},{8,40},{12,44},{16,48},{20,52},{24,56},{28,60},{32,6... | collective-permute-start | bytes 786440 | tf_op jit(solution)/shard_map/ppermute | solution.py:291
  25.4 10.0 %collective-permute-start.14 = (bf16[128,1024]{1,0:T(8,128)(2,1)S(1)}, bf16[128,1024]{1,0:T(8,128)(2,1)S(1)}, u32[]{:S(2)}, u32[]{:S(2)}) collective-permute-start(bf16[128,1024]{1,0:T(8,128)(2,1)S(1)} %collective-permute-done.12), channel_id=1, source_target_pairs={{0,224},{4,228},{8,232},{12,236},{16,240},{20,244},{24,248},{28,25... | collective-permute-start | bytes 786440 | tf_op jit(solution)/shard_map/ppermute | solution.py:291
  28.6 8.8 %collective-permute-start.4 = (f32[136,128]{1,0:T(8,128)S(1)}, f32[136,128]{1,0:T(8,128)S(1)}, u32[]{:S(2)}, u32[]{:S(2)}) collective-permute-start(f32[136,128]{1,0:T(8,128)S(1)} %get-tuple-element.51.own), channel_id=1, source_target_pairs={{0,48},{4,52},{8,56},{12,60},{16,0},{20,4},{24,8},{28,12},{32,16},... | collective-permute-start | bytes 208904 | tf_op jit(solution)/shard_map/ppermute | solution.py:291
  29.8 8.2 %collective-permute-start.5 = (f32[136,128]{1,0:T(8,128)S(1)}, f32[136,128]{1,0:T(8,128)S(1)}, u32[]{:S(2)}, u32[]{:S(2)}) collective-permute-start(f32[136,128]{1,0:T(8,128)S(1)} %get-tuple-element.51.own), channel_id=1, source_target_pairs={{0,32},{4,36},{8,40},{12,44},{16,48},{20,52},{24,56},{28,60},{32,0... | collective-permute-start | bytes 208904 | tf_op jit(solution)/shard_map/ppermute | solution.py:291
  31.7 7.5 %collective-permute-start.6 = (f32[136,128]{1,0:T(8,128)S(1)}, f32[136,128]{1,0:T(8,128)S(1)}, u32[]{:S(2)}, u32[]{:S(2)}) collective-permute-start(f32[136,128]{1,0:T(8,128)S(1)} %get-tuple-element.51.own), channel_id=1, source_target_pairs={{0,16},{4,20},{8,24},{12,28},{16,32},{20,36},{24,40},{28,44},{32,4... | collective-permute-start | bytes 208904 | tf_op jit(solution)/shard_map/ppermute | solution.py:291
  35.4 25.6 %collective-permute-start.15 = (bf16[128,1024]{1,0:T(8,128)(2,1)S(1)}, bf16[128,1024]{1,0:T(8,128)(2,1)S(1)}, u32[]{:S(2)}, u32[]{:S(2)}) collective-permute-start(bf16[128,1024]{1,0:T(8,128)(2,1)S(1)} %collective-permute-done.13), channel_id=1, source_target_pairs={{0,32},{4,36},{8,40},{12,44},{16,48},{20,52},{24,56},{28,60},{32,6... | collective-permute-start | bytes 786440 | tf_op jit(solution)/shard_map/ppermute | solution.py:291
  35.4 25.5 %collective-permute-start.18 = (bf16[128,1024]{1,0:T(8,128)(2,1)S(1)}, bf16[128,1024]{1,0:T(8,128)(2,1)S(1)}, u32[]{:S(2)}, u32[]{:S(2)}) collective-permute-start(bf16[128,1024]{1,0:T(8,128)(2,1)S(1)} %collective-permute-done.14), channel_id=1, source_target_pairs={{0,224},{4,228},{8,232},{12,236},{16,240},{20,244},{24,248},{28,25... | collective-permute-start | bytes 786440 | tf_op jit(solution)/shard_map/ppermute | solution.py:291
  40.1 12.1 %collective-permute-start.8 = (f32[136,128]{1,0:T(8,128)S(1)}, f32[136,128]{1,0:T(8,128)S(1)}, u32[]{:S(2)}, u32[]{:S(2)}) collective-permute-start(f32[136,128]{1,0:T(8,128)S(1)} %get-tuple-element.53), channel_id=1, source_target_pairs={{0,128},{4,132},{8,136},{12,140},{16,144},{20,148},{24,152},{28,15... | collective-permute-start | bytes 208904 | tf_op jit(solution)/shard_map/ppermute | solution.py:396
  41.4 19.5 %collective-permute-start.16 = (bf16[64,1024]{1,0:T(8,128)(2,1)S(1)}, bf16[64,1024]{1,0:T(8,128)(2,1)S(1)}, u32[]{:S(2)}, u32[]{:S(2)}) collective-permute-start(bf16[64,1024]{1,0:T(8,128)(2,1)S(1)} %slice.8), channel_id=1, source_target_pairs={{0,64},{4,68},{8,72},{12,76},{16,80},{20,84},{24,88},{28,92},{32,9... | collective-permute-start | bytes 393224 | tf_op jit(solution)/shard_map/ppermute | solution.py:291
  41.7 19.2 %collective-permute-start.17 = (bf16[64,1024]{1,0:T(8,128)(2,1)S(1)}, bf16[64,1024]{1,0:T(8,128)(2,1)S(1)}, u32[]{:S(2)}, u32[]{:S(2)}) collective-permute-start(bf16[64,1024]{1,0:T(8,128)(2,1)S(1)} %slice.9), channel_id=1, source_target_pairs={{0,192},{4,196},{8,200},{12,204},{16,208},{20,212},{24,216},{28,22... | collective-permute-start | bytes 393224 | tf_op jit(solution)/shard_map/ppermute | solution.py:291
  52.2 8.7 %collective-permute-start.9 = (f32[136,128]{1,0:T(8,128)S(1)}, f32[136,128]{1,0:T(8,128)S(1)}, u32[]{:S(2)}, u32[]{:S(2)}) collective-permute-start(f32[136,128]{1,0:T(8,128)S(1)} %get-tuple-element.53), channel_id=1, source_target_pairs={{0,64},{4,68},{8,72},{12,76},{16,80},{20,84},{24,88},{28,92},{32,9... | collective-permute-start | bytes 208904 | tf_op jit(solution)/shard_map/ppermute | solution.py:396
  61.2 4.5 %collective-permute-start.19 = (bf16[1024,1024]{1,0:T(8,128)(2,1)S(1)}, bf16[1024,1024]{1,0:T(8,128)(2,1)S(1)}, u32[]{:S(2)}, u32[]{:S(2)}) collective-permute-start(bf16[1024,1024]{1,0:T(8,128)(2,1)S(1)} %constant_dynamic-update-slice_fusion.refs_1_), channel_id=1, source_target_pairs={{0,4},{4,0},{8,12},{12,8},{16,20},{20,16},{24,28},{28,24},{32,36},... | collective-permute-start | bytes 6291464 | tf_op jit(solution)/shard_map/ppermute | solution.py:291
  64.6 14.4 %collective-permute-start.26 = (bf16[256,1024]{1,0:T(8,128)(2,1)S(1)}, bf16[256,1024]{1,0:T(8,128)(2,1)S(1)}, u32[]{:S(2)}, u32[]{:S(2)}) collective-permute-start(bf16[256,1024]{1,0:T(8,128)(2,1)S(1)} %shard_map.104.refs_0_), channel_id=1, source_target_pairs={{0,8},{4,12},{8,0},{12,4},{16,24},{20,28},{24,16},{28,20},{32,40},... | collective-permute-start | bytes 1572872 | tf_op jit(solution)/shard_map/ppermute | solution.py:291
  66.2 6.8 %collective-permute-start.20 = (bf16[256,256]{1,0:T(8,128)(2,1)S(1)}, bf16[256,256]{1,0:T(8,128)(2,1)S(1)}, u32[]{:S(2)}, u32[]{:S(2)}) collective-permute-start(bf16[256,256]{1,0:T(8,128)(2,1)S(1)} %get-tuple-element.73.refs_3_), channel_id=1, source_target_pairs={{0,1},{1,2},{2,3},{3,0},{4,5},{5,6},{6,7},{7,4},{8,9},{9,10},{10,1... | collective-permute-start | bytes 393224 | tf_op jit(solution)/shard_map/ppermute | solution.py:314
  66.8 7.1 %collective-permute-start.21 = (bf16[256,256]{1,0:T(8,128)(2,1)S(1)}, bf16[256,256]{1,0:T(8,128)(2,1)S(1)}, u32[]{:S(2)}, u32[]{:S(2)}) collective-permute-start(bf16[256,256]{1,0:T(8,128)(2,1)S(1)} %get-tuple-element.74.refs_4_), channel_id=1, source_target_pairs={{0,3},{1,0},{2,1},{3,2},{4,7},{5,4},{6,5},{7,6},{8,11},{9,8},{10,9... | collective-permute-start | bytes 393224 | tf_op jit(solution)/shard_map/ppermute | solution.py:314
  69.2 14.2 %collective-permute-start.24 = (bf16[256,256]{1,0:T(8,128)(2,1)S(1)}, bf16[256,256]{1,0:T(8,128)(2,1)S(1)}, u32[]{:S(2)}, u32[]{:S(2)}) collective-permute-start(bf16[256,256]{1,0:T(8,128)(2,1)S(1)} %get-tuple-element.82), channel_id=1, source_target_pairs={{0,3},{1,0},{2,1},{3,2},{4,7},{5,4},{6,5},{7,6},{8,11},{9,8},{10,9... | collective-permute-start | bytes 393224 | tf_op jit(solution)/shard_map/ppermute | solution.py:314
  70.1 13.6 %collective-permute-start.25 = (bf16[256,256]{1,0:T(8,128)(2,1)S(1)}, bf16[256,256]{1,0:T(8,128)(2,1)S(1)}, u32[]{:S(2)}, u32[]{:S(2)}) collective-permute-start(bf16[256,256]{1,0:T(8,128)(2,1)S(1)} %get-tuple-element.76.refs_4_), channel_id=1, source_target_pairs={{0,1},{1,2},{2,3},{3,0},{4,5},{5,6},{6,7},{7,4},{8,9},{9,10},{10,1... | collective-permute-start | bytes 393224 | tf_op jit(solution)/shard_map/ppermute | solution.py:314
  79.5 6.5 %collective-permute-start.27 = (bf16[256,256]{1,0:T(8,128)(2,1)S(1)}, bf16[256,256]{1,0:T(8,128)(2,1)S(1)}, u32[]{:S(2)}, u32[]{:S(2)}) collective-permute-start(bf16[256,256]{1,0:T(8,128)(2,1)S(1)} %get-tuple-element.85), channel_id=1, source_target_pairs={{0,1},{1,2},{2,3},{3,0},{4,5},{5,6},{6,7},{7,4},{8,9},{9,10},{10,1... | collective-permute-start | bytes 393224 | tf_op jit(solution)/shard_map/ppermute | solution.py:314
  80.1 8.0 %collective-permute-start.28 = (bf16[256,256]{1,0:T(8,128)(2,1)S(1)}, bf16[256,256]{1,0:T(8,128)(2,1)S(1)}, u32[]{:S(2)}, u32[]{:S(2)}) collective-permute-start(bf16[256,256]{1,0:T(8,128)(2,1)S(1)} %get-tuple-element.87), channel_id=1, source_target_pairs={{0,3},{1,0},{2,1},{3,2},{4,7},{5,4},{6,5},{7,6},{8,11},{9,8},{10,9... | collective-permute-start | bytes 393224 | tf_op jit(solution)/shard_map/ppermute | solution.py:314
  81.6 8.3 %collective-permute-start.22 = (bf16[256,256]{1,0:T(8,128)(2,1)S(1)}, bf16[256,256]{1,0:T(8,128)(2,1)S(1)}, u32[]{:S(2)}, u32[]{:S(2)}) collective-permute-start(bf16[256,256]{1,0:T(8,128)(2,1)S(1)} %get-tuple-element.80.refs_3_), channel_id=1, source_target_pairs={{0,1},{1,2},{2,3},{3,0},{4,5},{5,6},{6,7},{7,4},{8,9},{9,10},{10,1... | collective-permute-start | bytes 393224 | tf_op jit(solution)/shard_map/ppermute | solution.py:314
  83.3 7.2 %collective-permute-start.23 = (bf16[256,256]{1,0:T(8,128)(2,1)S(1)}, bf16[256,256]{1,0:T(8,128)(2,1)S(1)}, u32[]{:S(2)}, u32[]{:S(2)}) collective-permute-start(bf16[256,256]{1,0:T(8,128)(2,1)S(1)} %get-tuple-element.81), channel_id=1, source_target_pairs={{0,3},{1,0},{2,1},{3,2},{4,7},{5,4},{6,5},{7,6},{8,11},{9,8},{10,9... | collective-permute-start | bytes 393224 | tf_op jit(solution)/shard_map/ppermute | solution.py:314
  84.5 7.7 %collective-permute-start.31 = (bf16[256,256]{1,0:T(8,128)(2,1)S(1)}, bf16[256,256]{1,0:T(8,128)(2,1)S(1)}, u32[]{:S(2)}, u32[]{:S(2)}) collective-permute-start(bf16[256,256]{1,0:T(8,128)(2,1)S(1)} %get-tuple-element.91), channel_id=1, source_target_pairs={{0,3},{1,0},{2,1},{3,2},{4,7},{5,4},{6,5},{7,6},{8,11},{9,8},{10,9... | collective-permute-start | bytes 393224 | tf_op jit(solution)/shard_map/ppermute | solution.py:314
  86.0 6.3 %collective-permute-start.32 = (bf16[256,256]{1,0:T(8,128)(2,1)S(1)}, bf16[256,256]{1,0:T(8,128)(2,1)S(1)}, u32[]{:S(2)}, u32[]{:S(2)}) collective-permute-start(bf16[256,256]{1,0:T(8,128)(2,1)S(1)} %get-tuple-element.92), channel_id=1, source_target_pairs={{0,1},{1,2},{2,3},{3,0},{4,5},{5,6},{6,7},{7,4},{8,9},{9,10},{10,1... | collective-permute-start | bytes 393224 | tf_op jit(solution)/shard_map/ppermute | solution.py:314
  88.1 5.0 %collective-permute-start.29 = (bf16[256,256]{1,0:T(8,128)(2,1)S(1)}, bf16[256,256]{1,0:T(8,128)(2,1)S(1)}, u32[]{:S(2)}, u32[]{:S(2)}) collective-permute-start(bf16[256,256]{1,0:T(8,128)(2,1)S(1)} %get-tuple-element.89), channel_id=1, source_target_pairs={{0,1},{1,2},{2,3},{3,0},{4,5},{5,6},{6,7},{7,4},{8,9},{9,10},{10,1... | collective-permute-start | bytes 393224 | tf_op jit(solution)/shard_map/ppermute | solution.py:314
  89.9 6.2 %collective-permute-start.30 = (bf16[256,256]{1,0:T(8,128)(2,1)S(1)}, bf16[256,256]{1,0:T(8,128)(2,1)S(1)}, u32[]{:S(2)}, u32[]{:S(2)}) collective-permute-start(bf16[256,256]{1,0:T(8,128)(2,1)S(1)} %get-tuple-element.90), channel_id=1, source_target_pairs={{0,3},{1,0},{2,1},{3,2},{4,7},{5,4},{6,5},{7,6},{8,11},{9,8},{10,9... | collective-permute-start | bytes 393224 | tf_op jit(solution)/shard_map/ppermute | solution.py:314
  96.2 6.5 %collective-permute-start.33 = (bf16[256,512]{1,0:T(8,128)(2,1)S(1)}, bf16[256,512]{1,0:T(8,128)(2,1)S(1)}, u32[]{:S(2)}, u32[]{:S(2)}) collective-permute-start(bf16[256,512]{1,0:T(8,128)(2,1)S(1)} %shard_map.114), channel_id=1, source_target_pairs={{0,8},{4,12},{8,0},{12,4},{16,24},{20,28},{24,16},{28,20},{32,40},... | collective-permute-start | bytes 786440 | tf_op jit(solution)/shard_map/ppermute | solution.py:291
  (12 other events, 155.8 us)

commit v4 on v3

--- a/solution.py
+++ b/solution.py
@@ -10,7 +10,7 @@
 LANES = 128
 GROUPS = 8
 WIDTH = GROUPS * LANES
-STEPS = 8
+STEPS = 16
 CHUNKS = ROWS // STEPS
 PIECE = 64
 STATE = MODES * GROUPS
@@ -335,10 +335,9 @@
 def reduced(mixed, gathered, other, orders):
     opposite_a, opposite_b = project((2,), mixed, gathered, other, orders[0])
     from_left, from_right = around(opposite_a, 1), around(opposite_b, -1)
-    next_a, next_b, previous_a, previous_b = project(
-        (1, 3), mixed, gathered, other, orders[1] or (opposite_a, opposite_b))
+    next_a, next_b, previous_a, previous_b, own_a, own_b = project(
+        (1, 3, 0), mixed, gathered, other, orders[1] or (opposite_a, opposite_b))
     one_b, one_a = around(next_b, 1), around(previous_a, -1)
-    own_a, own_b = project((0,), mixed, gathered, other, orders[2] or (next_a, next_b))
     to_right, to_left = call(add_kernel, (b16(ROWS, QUARTER),) * 2, [WHOLE] * 4)(
         from_left, next_a, from_right, previous_b)
     sum_a, sum_b = around(to_right, 1), around(to_left, -1)

time: 104 us -> 103 us (level)
    ppermute x18, waiting for transfers between devices: 17.3 us -> 12.2 us  [move(): return lax.ppermute(block, 'seq', [(i, target(i)) for i in range(count)])]
    ppermute x12, waiting for transfers between devices: 6.53 us -> 11.1 us  [around(): return lax.ppermute(block, 'ch', [(i, (i + gap) % 4) for i in range(4)])]
    pallas_call x6 -> x4, Pallas kernels: 3.87 us -> 3.4 us  [project(): pl.pallas_call(lambda *refs: project_kernel(turns, *refs), out_shape=(b16...]
  transfers between devices with their start and end apart: 34 -> 34, of which waited for: 17 -> 18; matrix products, arithmetic and copies ran while one was open for 0% -> 0% of each run, Pallas kernels for 11% -> 10%
where the time goes in v4:
time: 103 us
  starting transfers between devices  45.6 us (44%)
  waiting for transfers between devices  42.1 us (41%)
  Pallas kernels  13.5 us (13%)
  local copies, waits for them, and re-layouts  1.12 us (1%)
    ppermute x18, starting transfers between devices, move(): return lax.ppermute(block, 'seq', [(i, target(i)) for i in range(count)])  24.8 us
    ppermute x12, starting transfers between devices, around(): return lax.ppermute(block, 'ch', [(i, (i + gap) % 4) for i in range(4)])  15 us
    ppermute x3, waiting for transfers between devices, local(): lax.ppermute(final, 'seq', [(i, i + k * 16) for i in range(count - k * 16)])  13.1 us
    ppermute x18, waiting for transfers between devices, move(): return lax.ppermute(block, 'seq', [(i, target(i)) for i in range(count)])  12.2 us
    ppermute x12, waiting for transfers between devices, around(): return lax.ppermute(block, 'ch', [(i, (i + gap) % 4) for i in range(4)])  11.1 us
    ppermute x1, waiting for transfers between devices, local(): halo = lax.ppermute(tails, 'seq', [(i, i + 1) for i in range(count - 1)])  5.63 us
    ppermute x3, starting transfers between devices, local(): lax.ppermute(final, 'seq', [(i, i + k * 16) for i in range(count - k * 16)])  3.87 us
    pallas_call x1, Pallas kernels, local(): call(front_kernel, (f32(ROWS * GROUPS, LANES), f32(ROWS * GROUPS, LANES),...  3.77 us
  transfers between devices with their start and end apart: 34, of which 18 were waited for; matrix products, arithmetic and copies ran while one was open for 0% of the time, Pallas kernels for 10%

profile of v4, /device:TPU:166, one launch (start us, length us, event | category | flops | bytes accessed | tf_op | source)
XLA Modules:
  0.0 102.6 jit_solution(13949263468937630368)
XLA Ops:
  0.0 1.7 %shard_map.100 = (f32[8,1024]{1,0:T(8,128)}, bf16[64,1024]{1,0:T(8,128)(2,1)}) custom-call(s32[1,4]{1,0:T(1,128)} %starts_ref.5, bf16[256,1024]{1,0:T(8,128)(2,1)} %q_hbm.1, bf16[256,1024]{1,0:T(8,128)(2,1)} %k_hbm.1, bf16[256,1024]{1,0:T(8,128)(2,1)} %v_hbm.1, bf16[64,1024]{1,0:T(8,128)(2,1)} %shard_ref.1), custom_call_target="tpu_custom_call" | custom-call | tf_op jit(solution)/shard_map/pallas_call | solution.py:352
  1.8 3.2 %collective-permute-start.10 = (bf16[64,1024]{1,0:T(8,128)(2,1)}, bf16[64,1024]{1,0:T(8,128)(2,1)S(1)}, u32[]{:S(2)}, u32[]{:S(2)}) collective-permute-start(bf16[64,1024]{1,0:T(8,128)(2,1)} %get-tuple-element.57.shard_ref), channel_id=1, source_target_pairs={{0,16},{4,20},{8,24},{12,28},{16,0},{20,4},{24,8},{28,12},{32,48},... | collective-permute-start | bytes 393224 | tf_op jit(solution)/shard_map/ppermute | solution.py:291
  5.0 1.9 %collective-permute-start = (f32[8,1024]{1,0:T(8,128)}, f32[8,1024]{1,0:T(8,128)S(1)}, u32[]{:S(2)}, u32[]{:S(2)}) collective-permute-start(f32[8,1024]{1,0:T(8,128)} %get-tuple-element.49), channel_id=1, source_target_pairs={{0,4},{4,8},{8,12},{12,16},{16,20},{20,24},{24,28},{28,32},{32,36}... | collective-permute-start | bytes 98312 | tf_op jit(solution)/shard_map/ppermute | solution.py:359
  6.9 5.6 %collective-permute-done.halo_ref = f32[8,1024]{1,0:T(8,128)S(1)} collective-permute-done((f32[8,1024]{1,0:T(8,128)}, f32[8,1024]{1,0:T(8,128)S(1)}, u32[]{:S(2)}, u32[]{:S(2)}) %collective-permute-start) | collective-permute-done | bytes 32800 | tf_op jit(solution)/shard_map/ppermute | solution.py:359
  14.6 1.3 %collective-permute-start.12 = (bf16[128,1024]{1,0:T(8,128)(2,1)S(1)}, bf16[128,1024]{1,0:T(8,128)(2,1)S(1)}, u32[]{:S(2)}, u32[]{:S(2)}) collective-permute-start(bf16[128,1024]{1,0:T(8,128)(2,1)S(1)} %shard_map.105), channel_id=1, source_target_pairs={{0,224},{4,228},{8,232},{12,236},{16,240},{20,244},{24,248},{28,25... | collective-permute-start | bytes 786440 | tf_op jit(solution)/shard_map/ppermute | solution.py:291
  15.9 3.8 %shard_map.101 = (f32[2048,128]{1,0:T(8,128)S(1)}, f32[2048,128]{1,0:T(8,128)S(1)}, f32[136,128]{1,0:T(8,128)S(1)}) custom-call(s32[1,4]{1,0:T(1,128)S(1)} %copy-done.7, s32[1,4]{1,0:T(1,128)S(1)} %copy-done.9, bf16[256,1024]{1,0:T(8,128)(2,1)S(1)} %copy-done, bf16[256,1024]{1,0:T(8,128)(2,1)S(1)} %copy-done.1, bf16[256,1024]{1,0:T(8,128)(2,1)S(1)} %copy-done.2, ...), custom_call_target="tpu_custom_call" | custom-call | flops 20000000 | bytes 4000000 | tf_op jit(solution)/shard_map/pallas_call | solution.py:370
  20.3 1.9 %collective-permute-done.1.got3 = f32[136,128]{1,0:T(8,128)S(1)} collective-permute-done((f32[136,128]{1,0:T(8,128)S(1)}, f32[136,128]{1,0:T(8,128)S(1)}, u32[]{:S(2)}, u32[]{:S(2)}) %collective-permute-start.1) | collective-permute-done | bytes 69664 | tf_op jit(solution)/shard_map/ppermute | solution.py:291
  22.2 2.7 %collective-permute-done.2.got2 = f32[136,128]{1,0:T(8,128)S(1)} collective-permute-done((f32[136,128]{1,0:T(8,128)S(1)}, f32[136,128]{1,0:T(8,128)S(1)}, u32[]{:S(2)}, u32[]{:S(2)}) %collective-permute-start.2) | collective-permute-done | bytes 69664 | tf_op jit(solution)/shard_map/ppermute | solution.py:291
  26.0 2.5 %collective-permute-start.14 = (bf16[128,1024]{1,0:T(8,128)(2,1)S(1)}, bf16[128,1024]{1,0:T(8,128)(2,1)S(1)}, u32[]{:S(2)}, u32[]{:S(2)}) collective-permute-start(bf16[128,1024]{1,0:T(8,128)(2,1)S(1)} %collective-permute-done.12), channel_id=1, source_target_pairs={{0,224},{4,228},{8,232},{12,236},{16,240},{20,244},{24,248},{28,25... | collective-permute-start | bytes 786440 | tf_op jit(solution)/shard_map/ppermute | solution.py:291
  28.5 1.2 %collective-permute-start.4 = (f32[136,128]{1,0:T(8,128)S(1)}, f32[136,128]{1,0:T(8,128)S(1)}, u32[]{:S(2)}, u32[]{:S(2)}) collective-permute-start(f32[136,128]{1,0:T(8,128)S(1)} %get-tuple-element.51.own), channel_id=1, source_target_pairs={{0,48},{4,52},{8,56},{12,60},{16,0},{20,4},{24,8},{28,12},{32,16},... | collective-permute-start | bytes 208904 | tf_op jit(solution)/shard_map/ppermute | solution.py:291
  29.8 1.9 %collective-permute-start.5 = (f32[136,128]{1,0:T(8,128)S(1)}, f32[136,128]{1,0:T(8,128)S(1)}, u32[]{:S(2)}, u32[]{:S(2)}) collective-permute-start(f32[136,128]{1,0:T(8,128)S(1)} %get-tuple-element.51.own), channel_id=1, source_target_pairs={{0,32},{4,36},{8,40},{12,44},{16,48},{20,52},{24,56},{28,60},{32,0... | collective-permute-start | bytes 208904 | tf_op jit(solution)/shard_map/ppermute | solution.py:291
  31.7 3.5 %collective-permute-start.6 = (f32[136,128]{1,0:T(8,128)S(1)}, f32[136,128]{1,0:T(8,128)S(1)}, u32[]{:S(2)}, u32[]{:S(2)}) collective-permute-start(f32[136,128]{1,0:T(8,128)S(1)} %get-tuple-element.51.own), channel_id=1, source_target_pairs={{0,16},{4,20},{8,24},{12,28},{16,32},{20,36},{24,40},{28,44},{32,4... | collective-permute-start | bytes 208904 | tf_op jit(solution)/shard_map/ppermute | solution.py:291
  35.4 2.0 %collective-permute-start.18 = (bf16[128,1024]{1,0:T(8,128)(2,1)S(1)}, bf16[128,1024]{1,0:T(8,128)(2,1)S(1)}, u32[]{:S(2)}, u32[]{:S(2)}) collective-permute-start(bf16[128,1024]{1,0:T(8,128)(2,1)S(1)} %collective-permute-done.14), channel_id=1, source_target_pairs={{0,224},{4,228},{8,232},{12,236},{16,240},{20,244},{24,248},{28,25... | collective-permute-start | bytes 786440 | tf_op jit(solution)/shard_map/ppermute | solution.py:291
  37.9 1.3 %collective-permute-done.6.got1 = f32[136,128]{1,0:T(8,128)S(1)} collective-permute-done((f32[136,128]{1,0:T(8,128)S(1)}, f32[136,128]{1,0:T(8,128)S(1)}, u32[]{:S(2)}, u32[]{:S(2)}) %collective-permute-start.6) | collective-permute-done | bytes 69664 | tf_op jit(solution)/shard_map/ppermute | solution.py:291
  40.0 1.3 %collective-permute-start.8 = (f32[136,128]{1,0:T(8,128)S(1)}, f32[136,128]{1,0:T(8,128)S(1)}, u32[]{:S(2)}, u32[]{:S(2)}) collective-permute-start(f32[136,128]{1,0:T(8,128)S(1)} %get-tuple-element.53), channel_id=1, source_target_pairs={{0,128},{4,132},{8,136},{12,140},{16,144},{20,148},{24,152},{28,15... | collective-permute-start | bytes 208904 | tf_op jit(solution)/shard_map/ppermute | solution.py:395
  41.7 4.2 %collective-permute-start.17 = (bf16[64,1024]{1,0:T(8,128)(2,1)S(1)}, bf16[64,1024]{1,0:T(8,128)(2,1)S(1)}, u32[]{:S(2)}, u32[]{:S(2)}) collective-permute-start(bf16[64,1024]{1,0:T(8,128)(2,1)S(1)} %slice.9), channel_id=1, source_target_pairs={{0,192},{4,196},{8,200},{12,204},{16,208},{20,212},{24,216},{28,22... | collective-permute-start | bytes 393224 | tf_op jit(solution)/shard_map/ppermute | solution.py:291
  45.9 6.5 %collective-permute-done.8.got2 = f32[136,128]{1,0:T(8,128)S(1)} collective-permute-done((f32[136,128]{1,0:T(8,128)S(1)}, f32[136,128]{1,0:T(8,128)S(1)}, u32[]{:S(2)}, u32[]{:S(2)}) %collective-permute-start.8) | collective-permute-done | bytes 69664 | tf_op jit(solution)/shard_map/ppermute | solution.py:395
  52.3 1.9 %collective-permute-start.9 = (f32[136,128]{1,0:T(8,128)S(1)}, f32[136,128]{1,0:T(8,128)S(1)}, u32[]{:S(2)}, u32[]{:S(2)}) collective-permute-start(f32[136,128]{1,0:T(8,128)S(1)} %get-tuple-element.53), channel_id=1, source_target_pairs={{0,64},{4,68},{8,72},{12,76},{16,80},{20,84},{24,88},{28,92},{32,9... | collective-permute-start | bytes 208904 | tf_op jit(solution)/shard_map/ppermute | solution.py:395
  54.2 6.6 %collective-permute-done.9.got1 = f32[136,128]{1,0:T(8,128)S(1)} collective-permute-done((f32[136,128]{1,0:T(8,128)S(1)}, f32[136,128]{1,0:T(8,128)S(1)}, u32[]{:S(2)}, u32[]{:S(2)}) %collective-permute-start.9) | collective-permute-done | bytes 69664 | tf_op jit(solution)/shard_map/ppermute | solution.py:395
  61.2 3.2 %shard_map.104.refs_0_ = bf16[256,1024]{1,0:T(8,128)(2,1)S(1)} custom-call(s32[1,4]{1,0:T(1,128)S(1)} %copy-done.7, s32[1,4]{1,0:T(1,128)S(1)} %copy-done.9, f32[136,128]{1,0:T(8,128)S(1)} %collective-permute-done.7.got3, f32[136,128]{1,0:T(8,128)S(1)} %collective-permute-done.8.got2, f32[136,128]{1,0:T(8,128)S(1)} %collective-permute-done.9.got1, ...), custom_call_target="tpu_custom_call" | custom-call | flops 20000000 | bytes 4000000 | tf_op jit(solution)/shard_map/pallas_call | solution.py:401
  66.6 1.5 %collective-permute-start.21 = (bf16[256,256]{1,0:T(8,128)(2,1)S(1)}, bf16[256,256]{1,0:T(8,128)(2,1)S(1)}, u32[]{:S(2)}, u32[]{:S(2)}) collective-permute-start(bf16[256,256]{1,0:T(8,128)(2,1)S(1)} %get-tuple-element.74.refs_4_), channel_id=1, source_target_pairs={{0,3},{1,0},{2,1},{3,2},{4,7},{5,4},{6,5},{7,6},{8,11},{9,8},{10,9... | collective-permute-start | bytes 393224 | tf_op jit(solution)/shard_map/ppermute | solution.py:314
  70.2 2.4 %collective-permute-start.25 = (bf16[256,256]{1,0:T(8,128)(2,1)S(1)}, bf16[256,256]{1,0:T(8,128)(2,1)S(1)}, u32[]{:S(2)}, u32[]{:S(2)}) collective-permute-start(bf16[256,256]{1,0:T(8,128)(2,1)S(1)} %get-tuple-element.82), channel_id=1, source_target_pairs={{0,1},{1,2},{2,3},{3,0},{4,5},{5,6},{6,7},{7,4},{8,9},{9,10},{10,1... | collective-permute-start | bytes 393224 | tf_op jit(solution)/shard_map/ppermute | solution.py:314
  73.5 5.4 %collective-permute-done.26.refs_0_ = bf16[256,1024]{1,0:T(8,128)(2,1)S(1)} collective-permute-done((bf16[256,1024]{1,0:T(8,128)(2,1)S(1)}, bf16[256,1024]{1,0:T(8,128)(2,1)S(1)}, u32[]{:S(2)}, u32[]{:S(2)}) %collective-permute-start.26) | collective-permute-done | bytes 524320 | tf_op jit(solution)/shard_map/ppermute | solution.py:291
  79.9 1.5 %collective-permute-start.28 = (bf16[256,256]{1,0:T(8,128)(2,1)S(1)}, bf16[256,256]{1,0:T(8,128)(2,1)S(1)}, u32[]{:S(2)}, u32[]{:S(2)}) collective-permute-start(bf16[256,256]{1,0:T(8,128)(2,1)S(1)} %get-tuple-element.87), channel_id=1, source_target_pairs={{0,3},{1,0},{2,1},{3,2},{4,7},{5,4},{6,5},{7,6},{8,11},{9,8},{10,9... | collective-permute-start | bytes 393224 | tf_op jit(solution)/shard_map/ppermute | solution.py:314
  81.5 1.2 %shard_map.109 = (bf16[256,256]{1,0:T(8,128)(2,1)S(1)}, bf16[256,256]{1,0:T(8,128)(2,1)S(1)}, bf16[256,256]{1,0:T(8,128)(2,1)S(1)}, bf16[256,256]{1,0:T(8,128)(2...) custom-call(bf16[256,1024]{1,0:T(8,128)(2,1)S(1)} %collective-permute-done.26.refs_0_, ...), custom_call_target="tpu_custom_call" | custom-call | flops 805306368 | bytes 6291456 | tf_op jit(solution)/shard_map/pallas_call | solution.py:322
  83.6 2.4 %collective-permute-start.32 = (bf16[256,256]{1,0:T(8,128)(2,1)S(1)}, bf16[256,256]{1,0:T(8,128)(2,1)S(1)}, u32[]{:S(2)}, u32[]{:S(2)}) collective-permute-start(bf16[256,256]{1,0:T(8,128)(2,1)S(1)} %get-tuple-element.92), channel_id=1, source_target_pairs={{0,1},{1,2},{2,3},{3,0},{4,5},{5,6},{6,7},{7,4},{8,9},{9,10},{10,1... | collective-permute-start | bytes 393224 | tf_op jit(solution)/shard_map/ppermute | solution.py:314
  86.8 2.0 %collective-permute-start.30 = (bf16[256,256]{1,0:T(8,128)(2,1)S(1)}, bf16[256,256]{1,0:T(8,128)(2,1)S(1)}, u32[]{:S(2)}, u32[]{:S(2)}) collective-permute-start(bf16[256,256]{1,0:T(8,128)(2,1)S(1)} %get-tuple-element.90), channel_id=1, source_target_pairs={{0,3},{1,0},{2,1},{3,2},{4,7},{5,4},{6,5},{7,6},{8,11},{9,8},{10,9... | collective-permute-start | bytes 393224 | tf_op jit(solution)/shard_map/ppermute | solution.py:314
  89.8 1.9 %collective-permute-done.29.refs_2_ = bf16[256,256]{1,0:T(8,128)(2,1)S(1)} collective-permute-done((bf16[256,256]{1,0:T(8,128)(2,1)S(1)}, bf16[256,256]{1,0:T(8,128)(2,1)S(1)}, u32[]{:S(2)}, u32[]{:S(2)}) %collective-permute-start.29) | collective-permute-done | bytes 131104 | tf_op jit(solution)/shard_map/ppermute | solution.py:314
  91.7 1.3 %collective-permute-done.30.refs_3_ = bf16[256,256]{1,0:T(8,128)(2,1)S(1)} collective-permute-done((bf16[256,256]{1,0:T(8,128)(2,1)S(1)}, bf16[256,256]{1,0:T(8,128)(2,1)S(1)}, u32[]{:S(2)}, u32[]{:S(2)}) %collective-permute-start.30) | collective-permute-done | bytes 131104 | tf_op jit(solution)/shard_map/ppermute | solution.py:314
  94.1 1.4 %collective-permute-start.22 = (bf16[256,256]{1,0:T(8,128)(2,1)S(1)}, bf16[256,256]{1,0:T(8,128)(2,1)S(1)}, u32[]{:S(2)}, u32[]{:S(2)}) collective-permute-start(bf16[256,256]{1,0:T(8,128)(2,1)S(1)} %get-tuple-element.79.refs_3_), channel_id=1, source_target_pairs={{0,1},{1,2},{2,3},{3,0},{4,5},{5,6},{6,7},{7,4},{8,9},{9,10},{10,1... | collective-permute-start | bytes 393224 | tf_op jit(solution)/shard_map/ppermute | solution.py:314
  96.2 2.9 %collective-permute-done.22.refs_2_ = bf16[256,256]{1,0:T(8,128)(2,1)S(1)} collective-permute-done((bf16[256,256]{1,0:T(8,128)(2,1)S(1)}, bf16[256,256]{1,0:T(8,128)(2,1)S(1)}, u32[]{:S(2)}, u32[]{:S(2)}) %collective-permute-start.22) | collective-permute-done | bytes 131104 | tf_op jit(solution)/shard_map/ppermute | solution.py:314
  99.1 2.6 %collective-permute-done.23.refs_3_ = bf16[256,256]{1,0:T(8,128)(2,1)S(1)} collective-permute-done((bf16[256,256]{1,0:T(8,128)(2,1)S(1)}, bf16[256,256]{1,0:T(8,128)(2,1)S(1)}, u32[]{:S(2)}, u32[]{:S(2)}) %collective-permute-start.23) | collective-permute-done | bytes 131104 | tf_op jit(solution)/shard_map/ppermute | solution.py:314
  (81 shorter events, 17.5 us)
Async XLA Ops:
  1.8 10.7 %collective-permute-start.10 = (bf16[64,1024]{1,0:T(8,128)(2,1)}, bf16[64,1024]{1,0:T(8,128)(2,1)S(1)}, u32[]{:S(2)}, u32[]{:S(2)}) collective-permute-start(bf16[64,1024]{1,0:T(8,128)(2,1)} %get-tuple-element.57.shard_ref), channel_id=1, source_target_pairs={{0,16},{4,20},{8,24},{12,28},{16,0},{20,4},{24,8},{28,12},{32,48},... | collective-permute-start | bytes 393224 | tf_op jit(solution)/shard_map/ppermute | solution.py:291
  5.0 7.5 %collective-permute-start = (f32[8,1024]{1,0:T(8,128)}, f32[8,1024]{1,0:T(8,128)S(1)}, u32[]{:S(2)}, u32[]{:S(2)}) collective-permute-start(f32[8,1024]{1,0:T(8,128)} %get-tuple-element.49), channel_id=1, source_target_pairs={{0,4},{4,8},{8,12},{12,16},{16,20},{20,24},{24,28},{28,32},{32,36}... | collective-permute-start | bytes 98312 | tf_op jit(solution)/shard_map/ppermute | solution.py:359
  13.5 11.7 %collective-permute-start.11 = (bf16[128,1024]{1,0:T(8,128)(2,1)S(1)}, bf16[128,1024]{1,0:T(8,128)(2,1)S(1)}, u32[]{:S(2)}, u32[]{:S(2)}) collective-permute-start(bf16[128,1024]{1,0:T(8,128)(2,1)S(1)} %shard_map.105), channel_id=1, source_target_pairs={{0,32},{4,36},{8,40},{12,44},{16,48},{20,52},{24,56},{28,60},{32,6... | collective-permute-start | bytes 786440 | tf_op jit(solution)/shard_map/ppermute | solution.py:291
  14.6 10.7 %collective-permute-start.12 = (bf16[128,1024]{1,0:T(8,128)(2,1)S(1)}, bf16[128,1024]{1,0:T(8,128)(2,1)S(1)}, u32[]{:S(2)}, u32[]{:S(2)}) collective-permute-start(bf16[128,1024]{1,0:T(8,128)(2,1)S(1)} %shard_map.105), channel_id=1, source_target_pairs={{0,224},{4,228},{8,232},{12,236},{16,240},{20,244},{24,248},{28,25... | collective-permute-start | bytes 786440 | tf_op jit(solution)/shard_map/ppermute | solution.py:291
  19.8 5.1 %collective-permute-start.2 = (f32[136,128]{1,0:T(8,128)S(1)}, f32[136,128]{1,0:T(8,128)S(1)}, u32[]{:S(2)}, u32[]{:S(2)}) collective-permute-start(f32[136,128]{1,0:T(8,128)S(1)} %get-tuple-element.50.own), channel_id=1, source_target_pairs={{0,8},{4,12},{8,0},{12,4},{16,24},{20,28},{24,16},{28,20},{32,40},... | collective-permute-start | bytes 208904 | tf_op jit(solution)/shard_map/ppermute | solution.py:291
  19.9 5.2 %collective-permute-start.3 = (f32[136,128]{1,0:T(8,128)S(1)}, f32[136,128]{1,0:T(8,128)S(1)}, u32[]{:S(2)}, u32[]{:S(2)}) collective-permute-start(f32[136,128]{1,0:T(8,128)S(1)} %get-tuple-element.50.own), channel_id=1, source_target_pairs={{0,4},{4,8},{8,12},{12,0},{16,20},{20,24},{24,28},{28,16},{32,36},... | collective-permute-start | bytes 208904 | tf_op jit(solution)/shard_map/ppermute | solution.py:291
  25.2 10.1 %collective-permute-start.13 = (bf16[128,1024]{1,0:T(8,128)(2,1)S(1)}, bf16[128,1024]{1,0:T(8,128)(2,1)S(1)}, u32[]{:S(2)}, u32[]{:S(2)}) collective-permute-start(bf16[128,1024]{1,0:T(8,128)(2,1)S(1)} %collective-permute-done.11), channel_id=1, source_target_pairs={{0,32},{4,36},{8,40},{12,44},{16,48},{20,52},{24,56},{28,60},{32,6... | collective-permute-start | bytes 786440 | tf_op jit(solution)/shard_map/ppermute | solution.py:291
  26.0 9.3 %collective-permute-start.14 = (bf16[128,1024]{1,0:T(8,128)(2,1)S(1)}, bf16[128,1024]{1,0:T(8,128)(2,1)S(1)}, u32[]{:S(2)}, u32[]{:S(2)}) collective-permute-start(bf16[128,1024]{1,0:T(8,128)(2,1)S(1)} %collective-permute-done.12), channel_id=1, source_target_pairs={{0,224},{4,228},{8,232},{12,236},{16,240},{20,244},{24,248},{28,25... | collective-permute-start | bytes 786440 | tf_op jit(solution)/shard_map/ppermute | solution.py:291
  28.5 8.8 %collective-permute-start.4 = (f32[136,128]{1,0:T(8,128)S(1)}, f32[136,128]{1,0:T(8,128)S(1)}, u32[]{:S(2)}, u32[]{:S(2)}) collective-permute-start(f32[136,128]{1,0:T(8,128)S(1)} %get-tuple-element.51.own), channel_id=1, source_target_pairs={{0,48},{4,52},{8,56},{12,60},{16,0},{20,4},{24,8},{28,12},{32,16},... | collective-permute-start | bytes 208904 | tf_op jit(solution)/shard_map/ppermute | solution.py:291
  29.8 8.2 %collective-permute-start.5 = (f32[136,128]{1,0:T(8,128)S(1)}, f32[136,128]{1,0:T(8,128)S(1)}, u32[]{:S(2)}, u32[]{:S(2)}) collective-permute-start(f32[136,128]{1,0:T(8,128)S(1)} %get-tuple-element.51.own), channel_id=1, source_target_pairs={{0,32},{4,36},{8,40},{12,44},{16,48},{20,52},{24,56},{28,60},{32,0... | collective-permute-start | bytes 208904 | tf_op jit(solution)/shard_map/ppermute | solution.py:291
  31.7 7.5 %collective-permute-start.6 = (f32[136,128]{1,0:T(8,128)S(1)}, f32[136,128]{1,0:T(8,128)S(1)}, u32[]{:S(2)}, u32[]{:S(2)}) collective-permute-start(f32[136,128]{1,0:T(8,128)S(1)} %get-tuple-element.51.own), channel_id=1, source_target_pairs={{0,16},{4,20},{8,24},{12,28},{16,32},{20,36},{24,40},{28,44},{32,4... | collective-permute-start | bytes 208904 | tf_op jit(solution)/shard_map/ppermute | solution.py:291
  35.3 25.6 %collective-permute-start.15 = (bf16[128,1024]{1,0:T(8,128)(2,1)S(1)}, bf16[128,1024]{1,0:T(8,128)(2,1)S(1)}, u32[]{:S(2)}, u32[]{:S(2)}) collective-permute-start(bf16[128,1024]{1,0:T(8,128)(2,1)S(1)} %collective-permute-done.13), channel_id=1, source_target_pairs={{0,32},{4,36},{8,40},{12,44},{16,48},{20,52},{24,56},{28,60},{32,6... | collective-permute-start | bytes 786440 | tf_op jit(solution)/shard_map/ppermute | solution.py:291
  35.4 25.5 %collective-permute-start.18 = (bf16[128,1024]{1,0:T(8,128)(2,1)S(1)}, bf16[128,1024]{1,0:T(8,128)(2,1)S(1)}, u32[]{:S(2)}, u32[]{:S(2)}) collective-permute-start(bf16[128,1024]{1,0:T(8,128)(2,1)S(1)} %collective-permute-done.14), channel_id=1, source_target_pairs={{0,224},{4,228},{8,232},{12,236},{16,240},{20,244},{24,248},{28,25... | collective-permute-start | bytes 786440 | tf_op jit(solution)/shard_map/ppermute | solution.py:291
  40.0 12.3 %collective-permute-start.8 = (f32[136,128]{1,0:T(8,128)S(1)}, f32[136,128]{1,0:T(8,128)S(1)}, u32[]{:S(2)}, u32[]{:S(2)}) collective-permute-start(f32[136,128]{1,0:T(8,128)S(1)} %get-tuple-element.53), channel_id=1, source_target_pairs={{0,128},{4,132},{8,136},{12,140},{16,144},{20,148},{24,152},{28,15... | collective-permute-start | bytes 208904 | tf_op jit(solution)/shard_map/ppermute | solution.py:395
  41.3 19.5 %collective-permute-start.16 = (bf16[64,1024]{1,0:T(8,128)(2,1)S(1)}, bf16[64,1024]{1,0:T(8,128)(2,1)S(1)}, u32[]{:S(2)}, u32[]{:S(2)}) collective-permute-start(bf16[64,1024]{1,0:T(8,128)(2,1)S(1)} %slice.8), channel_id=1, source_target_pairs={{0,64},{4,68},{8,72},{12,76},{16,80},{20,84},{24,88},{28,92},{32,9... | collective-permute-start | bytes 393224 | tf_op jit(solution)/shard_map/ppermute | solution.py:291
  41.7 19.2 %collective-permute-start.17 = (bf16[64,1024]{1,0:T(8,128)(2,1)S(1)}, bf16[64,1024]{1,0:T(8,128)(2,1)S(1)}, u32[]{:S(2)}, u32[]{:S(2)}) collective-permute-start(bf16[64,1024]{1,0:T(8,128)(2,1)S(1)} %slice.9), channel_id=1, source_target_pairs={{0,192},{4,196},{8,200},{12,204},{16,208},{20,212},{24,216},{28,22... | collective-permute-start | bytes 393224 | tf_op jit(solution)/shard_map/ppermute | solution.py:291
  52.3 8.6 %collective-permute-start.9 = (f32[136,128]{1,0:T(8,128)S(1)}, f32[136,128]{1,0:T(8,128)S(1)}, u32[]{:S(2)}, u32[]{:S(2)}) collective-permute-start(f32[136,128]{1,0:T(8,128)S(1)} %get-tuple-element.53), channel_id=1, source_target_pairs={{0,64},{4,68},{8,72},{12,76},{16,80},{20,84},{24,88},{28,92},{32,9... | collective-permute-start | bytes 208904 | tf_op jit(solution)/shard_map/ppermute | solution.py:395
  61.1 4.4 %collective-permute-start.19 = (bf16[1024,1024]{1,0:T(8,128)(2,1)S(1)}, bf16[1024,1024]{1,0:T(8,128)(2,1)S(1)}, u32[]{:S(2)}, u32[]{:S(2)}) collective-permute-start(bf16[1024,1024]{1,0:T(8,128)(2,1)S(1)} %constant_dynamic-update-slice_fusion.refs_1_), channel_id=1, source_target_pairs={{0,4},{4,0},{8,12},{12,8},{16,20},{20,16},{24,28},{28,24},{32,36},... | collective-permute-start | bytes 6291464 | tf_op jit(solution)/shard_map/ppermute | solution.py:291
  64.4 14.4 %collective-permute-start.26 = (bf16[256,1024]{1,0:T(8,128)(2,1)S(1)}, bf16[256,1024]{1,0:T(8,128)(2,1)S(1)}, u32[]{:S(2)}, u32[]{:S(2)}) collective-permute-start(bf16[256,1024]{1,0:T(8,128)(2,1)S(1)} %shard_map.104.refs_0_), channel_id=1, source_target_pairs={{0,8},{4,12},{8,0},{12,4},{16,24},{20,28},{24,16},{28,20},{32,40},... | collective-permute-start | bytes 1572872 | tf_op jit(solution)/shard_map/ppermute | solution.py:291
  66.1 6.6 %collective-permute-start.20 = (bf16[256,256]{1,0:T(8,128)(2,1)S(1)}, bf16[256,256]{1,0:T(8,128)(2,1)S(1)}, u32[]{:S(2)}, u32[]{:S(2)}) collective-permute-start(bf16[256,256]{1,0:T(8,128)(2,1)S(1)} %get-tuple-element.73.refs_3_), channel_id=1, source_target_pairs={{0,1},{1,2},{2,3},{3,0},{4,5},{5,6},{6,7},{7,4},{8,9},{9,10},{10,1... | collective-permute-start | bytes 393224 | tf_op jit(solution)/shard_map/ppermute | solution.py:314
  66.6 6.8 %collective-permute-start.21 = (bf16[256,256]{1,0:T(8,128)(2,1)S(1)}, bf16[256,256]{1,0:T(8,128)(2,1)S(1)}, u32[]{:S(2)}, u32[]{:S(2)}) collective-permute-start(bf16[256,256]{1,0:T(8,128)(2,1)S(1)} %get-tuple-element.74.refs_4_), channel_id=1, source_target_pairs={{0,3},{1,0},{2,1},{3,2},{4,7},{5,4},{6,5},{7,6},{8,11},{9,8},{10,9... | collective-permute-start | bytes 393224 | tf_op jit(solution)/shard_map/ppermute | solution.py:314
  69.3 12.2 %collective-permute-start.24 = (bf16[256,256]{1,0:T(8,128)(2,1)S(1)}, bf16[256,256]{1,0:T(8,128)(2,1)S(1)}, u32[]{:S(2)}, u32[]{:S(2)}) collective-permute-start(bf16[256,256]{1,0:T(8,128)(2,1)S(1)} %get-tuple-element.81), channel_id=1, source_target_pairs={{0,3},{1,0},{2,1},{3,2},{4,7},{5,4},{6,5},{7,6},{8,11},{9,8},{10,9... | collective-permute-start | bytes 393224 | tf_op jit(solution)/shard_map/ppermute | solution.py:314
  70.2 11.3 %collective-permute-start.25 = (bf16[256,256]{1,0:T(8,128)(2,1)S(1)}, bf16[256,256]{1,0:T(8,128)(2,1)S(1)}, u32[]{:S(2)}, u32[]{:S(2)}) collective-permute-start(bf16[256,256]{1,0:T(8,128)(2,1)S(1)} %get-tuple-element.82), channel_id=1, source_target_pairs={{0,1},{1,2},{2,3},{3,0},{4,5},{5,6},{6,7},{7,4},{8,9},{9,10},{10,1... | collective-permute-start | bytes 393224 | tf_op jit(solution)/shard_map/ppermute | solution.py:314
  79.4 6.6 %collective-permute-start.27 = (bf16[256,256]{1,0:T(8,128)(2,1)S(1)}, bf16[256,256]{1,0:T(8,128)(2,1)S(1)}, u32[]{:S(2)}, u32[]{:S(2)}) collective-permute-start(bf16[256,256]{1,0:T(8,128)(2,1)S(1)} %get-tuple-element.85), channel_id=1, source_target_pairs={{0,1},{1,2},{2,3},{3,0},{4,5},{5,6},{6,7},{7,4},{8,9},{9,10},{10,1... | collective-permute-start | bytes 393224 | tf_op jit(solution)/shard_map/ppermute | solution.py:314
  79.9 6.6 %collective-permute-start.28 = (bf16[256,256]{1,0:T(8,128)(2,1)S(1)}, bf16[256,256]{1,0:T(8,128)(2,1)S(1)}, u32[]{:S(2)}, u32[]{:S(2)}) collective-permute-start(bf16[256,256]{1,0:T(8,128)(2,1)S(1)} %get-tuple-element.87), channel_id=1, source_target_pairs={{0,3},{1,0},{2,1},{3,2},{4,7},{5,4},{6,5},{7,6},{8,11},{9,8},{10,9... | collective-permute-start | bytes 393224 | tf_op jit(solution)/shard_map/ppermute | solution.py:314
  82.7 6.4 %collective-permute-start.31 = (bf16[256,256]{1,0:T(8,128)(2,1)S(1)}, bf16[256,256]{1,0:T(8,128)(2,1)S(1)}, u32[]{:S(2)}, u32[]{:S(2)}) collective-permute-start(bf16[256,256]{1,0:T(8,128)(2,1)S(1)} %get-tuple-element.91), channel_id=1, source_target_pairs={{0,3},{1,0},{2,1},{3,2},{4,7},{5,4},{6,5},{7,6},{8,11},{9,8},{10,9... | collective-permute-start | bytes 393224 | tf_op jit(solution)/shard_map/ppermute | solution.py:314
  83.6 6.2 %collective-permute-start.32 = (bf16[256,256]{1,0:T(8,128)(2,1)S(1)}, bf16[256,256]{1,0:T(8,128)(2,1)S(1)}, u32[]{:S(2)}, u32[]{:S(2)}) collective-permute-start(bf16[256,256]{1,0:T(8,128)(2,1)S(1)} %get-tuple-element.92), channel_id=1, source_target_pairs={{0,1},{1,2},{2,3},{3,0},{4,5},{5,6},{6,7},{7,4},{8,9},{9,10},{10,1... | collective-permute-start | bytes 393224 | tf_op jit(solution)/shard_map/ppermute | solution.py:314
  86.6 5.0 %collective-permute-start.29 = (bf16[256,256]{1,0:T(8,128)(2,1)S(1)}, bf16[256,256]{1,0:T(8,128)(2,1)S(1)}, u32[]{:S(2)}, u32[]{:S(2)}) collective-permute-start(bf16[256,256]{1,0:T(8,128)(2,1)S(1)} %get-tuple-element.89), channel_id=1, source_target_pairs={{0,1},{1,2},{2,3},{3,0},{4,5},{5,6},{6,7},{7,4},{8,9},{9,10},{10,1... | collective-permute-start | bytes 393224 | tf_op jit(solution)/shard_map/ppermute | solution.py:314
  86.8 6.2 %collective-permute-start.30 = (bf16[256,256]{1,0:T(8,128)(2,1)S(1)}, bf16[256,256]{1,0:T(8,128)(2,1)S(1)}, u32[]{:S(2)}, u32[]{:S(2)}) collective-permute-start(bf16[256,256]{1,0:T(8,128)(2,1)S(1)} %get-tuple-element.90), channel_id=1, source_target_pairs={{0,3},{1,0},{2,1},{3,2},{4,7},{5,4},{6,5},{7,6},{8,11},{9,8},{10,9... | collective-permute-start | bytes 393224 | tf_op jit(solution)/shard_map/ppermute | solution.py:314
  93.1 8.6 %collective-permute-start.33 = (bf16[256,512]{1,0:T(8,128)(2,1)S(1)}, bf16[256,512]{1,0:T(8,128)(2,1)S(1)}, u32[]{:S(2)}, u32[]{:S(2)}) collective-permute-start(bf16[256,512]{1,0:T(8,128)(2,1)S(1)} %shard_map.112), channel_id=1, source_target_pairs={{0,8},{4,12},{8,0},{12,4},{16,24},{20,28},{24,16},{28,20},{32,40},... | collective-permute-start | bytes 786440 | tf_op jit(solution)/shard_map/ppermute | solution.py:291
  94.1 5.0 %collective-permute-start.22 = (bf16[256,256]{1,0:T(8,128)(2,1)S(1)}, bf16[256,256]{1,0:T(8,128)(2,1)S(1)}, u32[]{:S(2)}, u32[]{:S(2)}) collective-permute-start(bf16[256,256]{1,0:T(8,128)(2,1)S(1)} %get-tuple-element.79.refs_3_), channel_id=1, source_target_pairs={{0,1},{1,2},{2,3},{3,0},{4,5},{5,6},{6,7},{7,4},{8,9},{9,10},{10,1... | collective-permute-start | bytes 393224 | tf_op jit(solution)/shard_map/ppermute | solution.py:314
  95.5 6.2 %collective-permute-start.23 = (bf16[256,256]{1,0:T(8,128)(2,1)S(1)}, bf16[256,256]{1,0:T(8,128)(2,1)S(1)}, u32[]{:S(2)}, u32[]{:S(2)}) collective-permute-start(bf16[256,256]{1,0:T(8,128)(2,1)S(1)} %get-tuple-element.80), channel_id=1, source_target_pairs={{0,3},{1,0},{2,1},{3,2},{4,7},{5,4},{6,5},{7,6},{8,11},{9,8},{10,9... | collective-permute-start | bytes 393224 | tf_op jit(solution)/shard_map/ppermute | solution.py:314
  (12 other events, 155.8 us)
